TPU v7x, 32 devices: a whole 2x2x4 slice. The times are simulated.
32 devices in a mesh: grp: 2 (over x), seq: 16 (over z, y, core).
Axes of the slice: x: 2, y: 2, z: 4, core: 2. Of those that a mesh axis runs over, the one named last changes fastest.
Arguments:
- hidden: bfloat16 [4, 5120, 1280], P('grp', 'seq'), parts along dimension 0, may hold values from -160 to 160
- mod_shift: float32 [5120], replicated, may hold values from -3 to 3
- mod_scale: float32 [5120], replicated, may hold values from -0.5 to 0.5
- head_weight: float32 [64, 5120], replicated, may hold values from -0.078125 to 0.078125
- head_bias: float32 [64], replicated, may hold values from -3 to 3
- conv_in_weight: bfloat16 [3, 3, 3, 16, 384], replicated, may hold values from -0.3125 to 0.3125
- conv_in_bias: float32 [384], replicated, may hold values from -3 to 3
- gain_in: float32 [384], replicated, may hold values from 0.1 to 1.9
- up_weight: bfloat16 [3, 3, 384, 192], replicated, may hold values from -0.109375 to 0.109375
- up_bias: float32 [192], replicated, may hold values from -3 to 3
- gain_up: float32 [192], replicated, may hold values from 0.1 to 1.9
- out_weight: bfloat16 [3, 3, 3, 192, 96], replicated, may hold values from -0.078125 to 0.078125
- out_bias: float32 [96], replicated, may hold values from -2 to 2
Outputs:
- decoded: bfloat16 [4, 64, 320, 96], P('grp', 'seq'), parts along dimension 0
There are 2 independent parts, one for each index of `grp`. A program takes and returns all parts, laid end to end along the dimension named above; an argument that names none is the same for every part. Nothing has to cross between parts.
All inputs are finite; a program needn't handle non-finite values.
Results may differ from a plain program's by a relative error of at most 0.0056.
Values may be sent and summed in bfloat16 or wider, within the bound.
No kernel may reach another device: no remote copies, remote signals or barrier semaphores. Data moves between devices by JAX's collectives and lax.ppermute only.
A program may use at most 64 MiB of HBM per device.

v0:
```python
import jax
import jax.numpy as jnp
from jax import lax
from jax.sharding import PartitionSpec as P

TOK_W = 80


def padded_2(block, sides, width):
    for axis, dim in sides:
        count = lax.axis_size(axis)
        forward = [(i, i + 1) for i in range(count - 1)]
        backward = [(target, source) for source, target in forward]
        low = lax.ppermute(
            lax.slice_in_dim(block, block.shape[dim] - width, None, axis=dim), axis, forward
        )
        high = lax.ppermute(lax.slice_in_dim(block, 0, width, axis=dim), axis, backward)
        block = jnp.concatenate([low, block, high], axis=dim)
    return block


def rms_silu(values, gain_vec):
    squares = jnp.mean(values * values, axis=-1, keepdims=True)
    normed = values * lax.rsqrt(squares + 1e-06) * gain_vec
    return normed * jax.nn.sigmoid(normed)


def conv_time(values, weight):
    padded = jnp.pad(values, ((2, 0), (0, 0), (1, 1), (0, 0)))
    result = lax.conv_general_dilated(
        padded[None],
        weight,
        (1, 1, 1),
        "VALID",
        dimension_numbers=("NDHWC", "DHWIO", "NDHWC"),
        preferred_element_type=jnp.float32,
    )
    return result[0]


def conv_plane(values, weight):
    padded = jnp.pad(values, ((0, 0), (0, 0), (1, 1), (0, 0)))
    return lax.conv_general_dilated(
        padded,
        weight,
        (1, 1),
        "VALID",
        dimension_numbers=("NHWC", "HWIO", "NHWC"),
        preferred_element_type=jnp.float32,
    )


def double_grid(values):
    return jnp.repeat(jnp.repeat(values, 2, axis=1), 2, axis=2)


def keep_rows(values, first_row, total_rows):
    grid_row = first_row + jnp.arange(values.shape[1], dtype=jnp.int32)
    inside = (grid_row >= 0) & (grid_row < total_rows)
    return jnp.where(inside[None, :, None, None], values, 0.0)


def local(
    hidden,
    mod_shift,
    mod_scale,
    head_weight,
    head_bias,
    conv_in_weight,
    conv_in_bias,
    gain_in,
    up_weight,
    up_bias,
    gain_up,
    out_weight,
    out_bias,
):
    num_dev = lax.axis_size("seq")
    dev_index = lax.axis_index("seq")
    frames, feat_local, tok_total = hidden.shape
    tok_cols = TOK_W
    rows_dev = tok_total // tok_cols // num_dev
    patch_len = head_weight.shape[0]
    lat_ch = patch_len // 4
    tokens_tile = lax.all_to_all(hidden, "seq", split_axis=2, concat_axis=1, tiled=True)
    values = tokens_tile.astype(jnp.float32)
    token_mean = jnp.mean(values, axis=1, keepdims=True)
    centred = values - token_mean
    variance = jnp.mean(centred * centred, axis=1, keepdims=True)
    modded = centred * lax.rsqrt(variance + 1e-06) * (1.0 + mod_scale)[:, None] + mod_shift[:, None]
    projected = (
        jnp.einsum("fdt,kd->ftk", modded, head_weight, precision=lax.Precision.HIGHEST) + head_bias
    )
    grid = projected.astype(jnp.bfloat16).reshape(frames, rows_dev, tok_cols, 2, 2, lat_ch)
    lat_rows = 2 * rows_dev
    lat_cols = 2 * tok_cols
    latent = grid.transpose(0, 1, 3, 2, 4, 5).reshape(frames, lat_rows, lat_cols, lat_ch)
    latent_ext = padded_2(latent.reshape(frames, lat_rows, lat_cols * lat_ch), (("seq", 1),), 2)
    latent_ext = latent_ext.reshape(frames, lat_rows + 4, lat_cols, lat_ch)
    first_pre = rms_silu(conv_time(latent_ext, conv_in_weight) + conv_in_bias, gain_in)
    first_act = keep_rows(first_pre, dev_index * lat_rows - 1, lat_rows * num_dev).astype(
        jnp.bfloat16
    )
    upsampled = double_grid(first_act)
    second_pre = rms_silu(conv_plane(upsampled, up_weight) + up_bias, gain_up)
    second_ext = keep_rows(second_pre, 2 * dev_index * lat_rows - 1, 2 * lat_rows * num_dev).astype(
        jnp.bfloat16
    )
    return (conv_time(second_ext, out_weight) + out_bias).astype(jnp.bfloat16)


def solution(mesh):
    placed = (P("grp", "seq", None), P(), P(), P(), P(), P(), P(), P(), P(), P(), P(), P(), P())
    return jax.shard_map(
        local, mesh=mesh, in_specs=placed, out_specs=P("grp", "seq", None, None), check_vma=False
    )
```

profile of v0, /device:TPU:16, one launch (start us, length us, event | category | flops | bytes accessed | tf_op | source)
XLA Modules:
  0.0 137.6 jit_solution(6802326855571328485)
XLA Ops:
  0.0 6.7 %copy.79 = bf16[2,320,1280]{1,0,2:T(2,128)(2,1)} copy(bf16[2,320,1280]{2,1,0:T(8,128)(2,1)} %param.13) | data formatting | bytes 3276800 | tf_op args[0]
  6.8 6.2 %all-to-all-start = ((bf16[2,320,1280]{1,0,2:T(2,128)(2,1)}), bf16[2,320,1280]{1,0,2:T(2,128)(2,1)S(1)}, u32[]{:S(2)}, u32[]{:S(2)}) async-start(bf16[2,320,1280]{1,0,2:T(2,128)(2,1)} %copy.79), calls=%async_computation | async-start | bytes 3932160 | tf_op jit(solution)/shard_map/all_to_all | solution.py:85
  13.0 44.8 %all-to-all-done = bf16[2,320,1280]{1,0,2:T(2,128)(2,1)S(1)} async-done(((bf16[2,320,1280]{1,0,2:T(2,128)(2,1)}), bf16[2,320,1280]{1,0,2:T(2,128)(2,1)S(1)}, u32[]{:S(2)}, u32[]{:S(2)}) %all-to-all-start) | async-done | bytes 1638432 | tf_op jit(solution)/shard_map/all_to_all | solution.py:85
  57.8 0.3 copy.80
  58.0 0.4 fusion.22
  58.4 0.3 convert_bitcast_fusion
  58.7 0.7 multiply_reduce_fusion.1
  59.5 3.0 %copy.81 = f32[2,16,320,80]{2,1,3,0:T(8,128)} copy(f32[2,16,320,80]{2,3,1,0:T(8,128)S(1)} %convert_bitcast_fusion) | data formatting | bytes 6553600 | tf_op jit(solution)/shard_map/convert_element_type | solution.py:86
  62.5 5.2 %reshape.96 = f32[2,5120,80]{1,2,0:T(8,128)} reshape(f32[2,16,320,80]{2,1,3,0:T(8,128)} %copy.81) | data formatting | bytes 6553600 | tf_op jit(solution)/shard_map/convert_element_type | solution.py:86
  67.7 6.1 %fusion.47 = bf16[2,80,64]{1,2,0:T(8,128)(2,1)S(1)} fusion(f32[64,5120]{1,0:T(8,128)S(1)} %copy-done.2, f32[2,5120,80]{1,2,0:T(8,128)} %reshape.96, f32[5120]{0:T(1024)S(1)} %copy-done.3, f32[5120]{0:T(1024)S(1)} %broadcast_add_fusion, f32[2,80]{1,0:T(2,128)S(1)} %add_rsqrt_fusion.2, f32[2,80]{1,0:T(2,128)S(1)} %broadcast_multiply_fusion, f32[64]{0:T(128)S(1)} %copy-done.8), kind=kOutput, calls=%fused_computation.53 | convolution fusion | flops 632442880 | bytes 4650496 | tf_op jit(solution)/shard_map/fdt,kd->ftk/dot_general | solution.py:92
  73.8 0.1 copy.82
  74.0 0.2 reshape_reshape.3
  74.2 2.9 %collective-permute-start.1 = (bf16[2,2,2560]{2,1,0:T(2,128)(2,1)S(1)}, bf16[2,2,2560]{2,1,0:T(2,128)(2,1)S(1)}, u32[]{:S(2)}, u32[]{:S(2)}) collective-permute-start(bf16[2,2,2560]{2,1,0:T(2,128)(2,1)S(1)} %reshape_reshape.3), channel_id=1, source_target_pairs={{1,0},{2,1},{3,2},{4,3},{5,4},{6,5},{7,6},{8,7},{9,8},{10,9},{11,1... | collective-permute-start | bytes 61448 | tf_op jit(solution)/shard_map/ppermute | solution.py:17
  77.1 2.1 %collective-permute-start = (bf16[2,2,2560]{2,1,0:T(2,128)(2,1)S(1)}, bf16[2,2,2560]{2,1,0:T(2,128)(2,1)S(1)}, u32[]{:S(2)}, u32[]{:S(2)}) collective-permute-start(bf16[2,2,2560]{2,1,0:T(2,128)(2,1)S(1)} %reshape_reshape.3), channel_id=1, source_target_pairs={{0,1},{1,2},{2,3},{3,4},{4,5},{5,6},{6,7},{7,8},{8,9},{9,10},{10,1... | collective-permute-start | bytes 61448 | tf_op jit(solution)/shard_map/ppermute | solution.py:14
  79.2 0.1 copy.84
  79.3 3.8 %collective-permute-done = bf16[2,2,2560]{2,1,0:T(2,128)(2,1)S(1)} collective-permute-done((bf16[2,2,2560]{2,1,0:T(2,128)(2,1)S(1)}, bf16[2,2,2560]{2,1,0:T(2,128)(2,1)S(1)}, u32[]{:S(2)}, u32[]{:S(2)}) %collective-permute-start) | collective-permute-done | bytes 20512 | tf_op jit(solution)/shard_map/ppermute | solution.py:14
  83.1 0.2 concatenate.10
  83.2 0.1 copy.83
  83.4 0.2 concatenate.12
  83.5 0.1 copy.85
  83.6 0.1 fusion.61
  83.8 0.6 reshape.75
  84.4 1.6 %copy.87 = bf16[4,6,1,8,21,16]{5,3,4,1,0,2:T(8,128)(2,1)S(1)} copy(bf16[4,6,1,8,21,16]{4,3,5,1,0,2:T(8,128)(2,1)S(1)} %reshape.75) | data formatting | bytes 258048 | tf_op jit(solution)/shard_map/conv_general_dilated | solution.py:30
  86.0 2.6 %convolution_select_fusion = f32[2,4,8,21,384]{4,2,3,1,0:T(8,128)S(1)} fusion(bf16[3,3,3,16,384]{4,3,2,1,0:T(8,128)(2,1)} %param.18, bf16[4,6,1,7,2,16]{5,3,4,1,0,2:T(8,128)(2,1)S(1)} %slice.7, bf16[4,6,1,8,21,16]{5,3,4,1,0,2:T(8,128)(2,1)S(1)} %copy.87, pred[8,21]{0,1:T(8,128)(4,1)S(1)} %copy-done.14), kind=kOutput, calls=%fused_computation.41 | convolution fusion | flops 446846976 | bytes 2536104 | tf_op jit(solution)/shard_map/conv_general_dilated | solution.py:30
  88.6 0.5 copy.88
  89.2 0.1 copy-done.5
  89.3 0.6 multiply_reduce_fusion.2
  89.9 1.5 %select_convert_fusion.1 = bf16[2,4,160,384]{3,1,2,0:T(4,128)(2,1)S(1)} fusion(f32[2,4,1,168,384]{4,1,3,0,2:T(4,128)S(1)} %bitcast.88, f32[384]{0:T(512)S(1)} %copy-done.6, f32[2,4,160]{1,2,0:T(8,128)S(1)} %add_rsqrt_fusion, f32[384]{0:T(512)S(1)} %copy-done.5, pred[4]{0:T(512)(128)(4,1)S(1)} %compare_and_fusion), kind=kLoop, calls=%fused_computation.35 | loop fusion | flops 4423680 | bytes 2957316 | tf_op jit(solution)/shard_map/convert_element_type | solution.py:101
  91.4 1.4 broadcast_in_dim.52
  92.7 1.8 %reshape.71 = bf16[2,8,160,384]{3,1,2,0:T(8,128)(2,1)} reshape(bf16[2,4,2,160,384]{4,2,1,3,0:T(2,128)(2,1)S(1)} %broadcast_in_dim.52) | data formatting | bytes 3932160 | tf_op jit(solution)/shard_map/reshape | solution.py:54
  94.5 1.9 %broadcast_in_dim.53 = bf16[2,8,160,2,384]{4,1,3,2,0:T(8,128)(2,1)S(1)} broadcast(bf16[2,8,160,384]{3,1,2,0:T(8,128)(2,1)} %reshape.71), dimensions={0,1,2,4} | broadcast | bytes 5898240 | tf_op jit(solution)/shard_map/broadcast_in_dim | solution.py:54
  96.4 0.4 pad.14
  96.9 0.5 fusion.6
  97.3 0.2 copy-done.11
  97.5 9.7 %multiply_reduce_fusion = (f32[6,16,41]{1,2,0:T(8,128)S(1)}, f32[6,16,41,192]{3,1,2,0:T(8,128)}) fusion(f32[192]{0:T(256)S(1)} %copy-done.11, bf16[3,3,384,192]{2,3,1,0:T(8,128)(2,1)S(1)} %copy-done, bf16[8,2,8,43,384]{4,0,3,2,1:T(8,128)(2,1)S(1)} %fusion.6, pred[16,41]{0,1:T(8,128)(4,1)S(1)} %copy-done.13), kind=kOutput, calls=%fused_computation.14 | convolution fusion | flops 5226500096 | bytes 8594192 | tf_op jit(solution)/shard_map/conv_general_dilated | solution.py:43
  107.2 0.1 copy.93
  107.5 6.6 %copy.92 = f32[6,16,41,192]{3,2,1,0:T(8,128)} copy(f32[6,16,41,192]{3,1,2,0:T(8,128)} %get-tuple-element.6) | data formatting | bytes 6045696 | tf_op jit(solution)/shard_map/add | solution.py:105
  114.1 5.0 %reshape.86 = f32[6,2,328,192]{3,2,1,0:T(8,128)} reshape(f32[6,16,41,192]{3,2,1,0:T(8,128)} %copy.92) | data formatting | bytes 6045696 | tf_op jit(solution)/shard_map/add | solution.py:105
  119.1 3.1 %select_convert_fusion = bf16[2,6,320,192]{3,2,0,1:T(8,128)(2,1)S(1)} fusion(f32[6,2,328,192]{3,2,1,0:T(8,128)} %reshape.86, f32[192]{0:T(256)S(1)} %copy-done.7, f32[2,6,320]{2,0,1:T(2,128)S(1)} %slice_bitcast_fusion.3, pred[6]{0:T(512)(128)(4,1)S(1)} %compare_and_fusion.1), kind=kLoop, calls=%fused_computation.21 | loop fusion | flops 5898240 | bytes 4439814 | tf_op jit(solution)/shard_map/convert_element_type | solution.py:106
  122.2 0.7 pad_bitcast_fusion
  123.0 1.5 %copy.99 = bf16[4,6,1,322,192]{4,0,3,1,2:T(4,128)(2,1)S(1)} copy(bf16[4,6,1,322,192]{4,3,0,1,2:T(8,128)(2,1)S(1)} %pad_bitcast_fusion) | data formatting | bytes 5935104
  124.5 1.8 %pad.16.clone = bf16[4,6,1,328,192]{4,0,3,1,2:T(4,128)(2,1)S(1)} pad(bf16[4,6,1,322,192]{4,0,3,1,2:T(4,128)(2,1)S(1)} %copy.99, bf16[]{:T(256)} %constant.39.clone.1), padding=0_0x0_0x0_0x0_6x0_0 | pad | bytes 5990402 | tf_op jit(solution)/shard_map/broadcast_in_dim | solution.py:31
  126.3 0.5 copy.96
  126.9 0.7 copy-done.10
  127.6 8.1 %fusion.30 = f32[2,4,8,41,96]{4,2,3,1,0:T(8,128)S(1)} fusion(bf16[3,3,3,192,96]{4,3,2,1,0:T(8,128)(2,1)S(1)} %copy-done.10, bf16[4,6,1,7,2,192]{5,3,4,1,0,2:T(8,128)(2,1)S(1)} %slice.12, bf16[4,6,1,8,41,192]{5,3,4,1,0,2:T(8,128)(2,1)S(1)} %copy.96, pred[8,41]{0,1:T(8,128)(4,1)S(1)} %copy-done.12), kind=kOutput, calls=%fused_computation.42 | convolution fusion | flops 2621503488 | bytes 5155144 | tf_op jit(solution)/shard_map/conv_general_dilated | solution.py:30
  135.8 0.3 copy.97
  136.1 0.2 fusion.34
  136.4 1.2 copy.98
  (41 shorter events, 0.4 us)
Async XLA Ops:
  0.0 97.3 %copy-start = (bf16[3,3,384,192]{2,3,1,0:T(8,128)(2,1)S(1)}, bf16[3,3,384,192]{2,3,1,0:T(8,128)(2,1)}, u32[]{:S(2)}) copy-start(bf16[3,3,384,192]{2,3,1,0:T(8,128)(2,1)} %param.21) | copy-start | bytes 3981316
  0.0 12.9 %copy-start.4 = (f32[5120]{0:T(1024)S(1)}, f32[5120]{0:T(1024)}, u32[]{:S(2)}) copy-start(f32[5120]{0:T(1024)} %param.15) | copy-start | bytes 61444
  6.8 51.0 %all-to-all-start = ((bf16[2,320,1280]{1,0,2:T(2,128)(2,1)}), bf16[2,320,1280]{1,0,2:T(2,128)(2,1)S(1)}, u32[]{:S(2)}, u32[]{:S(2)}) async-start(bf16[2,320,1280]{1,0,2:T(2,128)(2,1)} %copy.79), calls=%async_computation | async-start | bytes 3932160 | tf_op jit(solution)/shard_map/all_to_all | solution.py:85
  62.5 5.2 %copy-start.2 = (f32[64,5120]{1,0:T(8,128)S(1)}, f32[64,5120]{1,0:T(8,128)}, u32[]{:S(2)}) copy-start(f32[64,5120]{1,0:T(8,128)} %param.16) | copy-start | bytes 3932164
  62.5 5.2 %copy-start.3 = (f32[5120]{0:T(1024)S(1)}, f32[5120]{0:T(1024)}, u32[]{:S(2)}) copy-start(f32[5120]{0:T(1024)} %param.14) | copy-start | bytes 61444
  62.5 5.2 %copy-start.8 = (f32[64]{0:T(128)S(1)}, f32[64]{0:T(128)}, u32[]{:S(2)}) copy-start(f32[64]{0:T(128)} %param.17) | copy-start | bytes 772
  73.8 12.2 %copy-start.14 = (pred[8,21]{0,1:T(8,128)(4,1)S(1)}, pred[8,21]{0,1:T(8,128)(4,1)}, u32[]{:S(2)}) copy-start(pred[8,21]{0,1:T(8,128)(4,1)} %constant.60) | copy-start | bytes 508
  74.2 9.2 %collective-permute-start.1 = (bf16[2,2,2560]{2,1,0:T(2,128)(2,1)S(1)}, bf16[2,2,2560]{2,1,0:T(2,128)(2,1)S(1)}, u32[]{:S(2)}, u32[]{:S(2)}) collective-permute-start(bf16[2,2,2560]{2,1,0:T(2,128)(2,1)S(1)} %reshape_reshape.3), channel_id=1, source_target_pairs={{1,0},{2,1},{3,2},{4,3},{5,4},{6,5},{7,6},{8,7},{9,8},{10,9},{11,1... | collective-permute-start | bytes 61448 | tf_op jit(solution)/shard_map/ppermute | solution.py:17
  77.1 6.0 %collective-permute-start = (bf16[2,2,2560]{2,1,0:T(2,128)(2,1)S(1)}, bf16[2,2,2560]{2,1,0:T(2,128)(2,1)S(1)}, u32[]{:S(2)}, u32[]{:S(2)}) collective-permute-start(bf16[2,2,2560]{2,1,0:T(2,128)(2,1)S(1)} %reshape_reshape.3), channel_id=1, source_target_pairs={{0,1},{1,2},{2,3},{3,4},{4,5},{5,6},{6,7},{7,8},{8,9},{9,10},{10,1... | collective-permute-start | bytes 61448 | tf_op jit(solution)/shard_map/ppermute | solution.py:14
  88.6 0.7 copy-start.5
  88.6 1.3 copy-start.6
  96.8 0.7 copy-start.11
  96.8 0.7 copy-start.13
  114.1 5.0 %copy-start.7 = (f32[192]{0:T(256)S(1)}, f32[192]{0:T(256)}, u32[]{:S(2)}) copy-start(f32[192]{0:T(256)} %param.23) | copy-start | bytes 2308
  126.3 1.3 copy-start.10
  126.3 1.3 copy-start.12
  127.6 8.5 %copy-start.9 = (f32[96]{0:T(128)S(1)}, f32[96]{0:T(128)}, u32[]{:S(2)}) copy-start(f32[96]{0:T(128)} %param.25) | copy-start | bytes 1156
  127.6 9.9 %copy-start.1 = (bf16[3,3,384,192]{2,3,1,0:T(8,128)(2,1)S(1)}, bf16[3,3,384,192]{2,3,1,0:T(8,128)(2,1)}, u32[]{:S(2)}) copy-start(bf16[3,3,384,192]{2,3,1,0:T(8,128)(2,1)} %param.21) | copy-start | bytes 3981316
where the time goes:
time: 138 us
  waiting for transfers between devices  48.6 us (35%)
  local copies, waits for them, and re-layouts  43.5 us (32%)
  matrix products  26.5 us (19%)
  starting transfers between devices  11.2 us (8%)
  other arithmetic  7.41 us (5%)
    all_to_all x1, waiting for transfers between devices, local(): lax.all_to_all(hidden, 'seq', split_axis=2, concat_axis=1, tiled=True)  44.8 us
    add x2, local copies, waits for them, and re-layouts, local(): second_pre = rms_silu(conv_plane(upsampled, up_weight) + up_bias, gain_up)  11.6 us
    conv_general_dilated x2, matrix products, conv_time(): lax.conv_general_dilated(padded[None], weight, (1, 1, 1), 'VALID', dimens...  10.7 us
    conv_general_dilated x1, matrix products, conv_plane(): lax.conv_general_dilated(padded, weight, (1, 1), 'VALID', dimension_numbe...  9.71 us
    unnamed x33, local copies, waits for them, and re-layouts  9.48 us
    convert_element_type x2, local copies, waits for them, and re-layouts, local(): values = tokens_tile.astype(jnp.float32)  8.24 us
    all_to_all x1, starting transfers between devices, local(): lax.all_to_all(hidden, 'seq', split_axis=2, concat_axis=1, tiled=True)  6.18 us
    dot_general x1, matrix products, local(): jnp.einsum('fdt,kd->ftk', modded, head_weight, precision=lax.Precision.HI...  6.1 us
  transfers between devices with their start and end apart: 3, of which 2 were waited for; matrix products, arithmetic and copies ran while one was open for 0% of the time, Pallas kernels for 0%

commit v1 on v0

v1 whole, which is shorter than its diff:
```python
import functools
import jax
import jax.numpy as jnp
import numpy as np
from jax import lax
from jax.experimental import pallas as pl
from jax.experimental.pallas import tpu as pltpu
from jax.sharding import PartitionSpec as P

TOK_W = 80
HALF = TOK_W // 2
STAT = 4
EPS = 1e-06
HIGH = lax.Precision.HIGHEST
BF = jnp.bfloat16
F32 = jnp.float32


def split(values):
    high = values.astype(BF).astype(F32)
    return high, values - high


def lanes(rows):
    return lax.broadcasted_iota(jnp.int32, (rows, 128), 1)


def project_kernel(hid_ref, w_ref, scale_ref, out_ref):
    feats = hid_ref.shape[1]
    width = hid_ref.shape[2]
    gain = w_ref[...] * (1.0 + scale_ref[...])
    gain = jnp.concatenate([gain[0:16], gain[32:48], gain[16:32], gain[48:64]], axis=0)
    high, low = split(gain)
    gain_sum = jnp.sum(gain, axis=1, keepdims=True)
    stack = jnp.concatenate([high, low, jnp.ones((16, feats), F32)], axis=0).astype(BF)
    parts, stats = [], []
    for f in range(2):
        x = hid_ref[f]
        prod = jnp.dot(stack, x, preferred_element_type=F32)
        mean = prod[128:129] * (1.0 / feats)
        parts.append(prod[0:64] + prod[64:128] - gain_sum * mean)
        off = x.astype(F32) - mean
        second = jnp.sum(off * off, axis=0, keepdims=True)
        m_hi, m_lo = split(mean)
        s_hi, s_lo = split(second)
        stats.append(
            jnp.concatenate([m_hi, m_lo, s_hi, s_lo, jnp.zeros((4, width), F32)], axis=0)
        )
    flat = jnp.concatenate(parts, axis=0).T
    lane = lanes(8)
    for row in range(width // TOK_W):
        for h in range(2):
            at = row * TOK_W + h * HALF
            base = (at // 128) * 128
            wide = min(256, width - base)
            picks = []
            for f in range(2):
                window = stats[f][:, base : base + wide]
                shift = (64 * f - (at - base)) % wide
                if shift:
                    window = pltpu.roll(window, shift, 1)
                picks.append(window[:, :128])
            tail = jnp.where(
                lane < HALF, picks[0], jnp.where((lane >= 64) & (lane < 64 + HALF), picks[1], 0.0)
            )
            out_ref[h, row] = jnp.concatenate([flat[at : at + HALF], tail], axis=0).astype(BF)


def project(hidden, w_slice, scale_slice):
    frames, feats, tokens = hidden.shape
    block = 640
    rows = tokens // TOK_W
    rows_block = block // TOK_W
    return pl.pallas_call(
        project_kernel,
        grid=(tokens // block,),
        in_specs=[
            pl.BlockSpec((frames, feats, block), lambda i: (0, 0, i)),
            pl.BlockSpec((64, feats), lambda i: (0, 0)),
            pl.BlockSpec((1, feats), lambda i: (0, 0)),
        ],
        out_specs=pl.BlockSpec((2, rows_block, 48, 128), lambda i: (0, i, 0, 0)),
        out_shape=jax.ShapeDtypeStruct((2, rows, 48, 128), BF),
        compiler_params=pltpu.CompilerParams(vmem_limit_bytes=32 << 20),
        name="project",
    )(hidden, w_slice, scale_slice)


def prepare_kernel(
    w_ref, scale_ref, shift_ref, hb_ref, dev_ref, cin_ref, up_ref, upv_ref, cout_ref,
    table_ref, const_ref, cin_out, up_out, upv_out, cout_out,
):
    feats = w_ref.shape[1] * 2 // dev_ref.shape[0]
    head = w_ref[...]
    head = jnp.concatenate([head[0:16], head[32:48], head[16:32], head[48:64]], axis=0)
    gain = head * (1.0 + scale_ref[...])
    count = dev_ref.shape[0]
    place = lax.broadcasted_iota(jnp.int32, (count, w_ref.shape[1]), 1) - dev_ref[...] * feats
    inside = ((place >= 0) & (place < feats)).astype(F32)
    dims = (((1,), (1,)), ((), ()))
    sums = lax.dot_general(inside, gain, dims, precision=HIGH, preferred_element_type=F32)
    table_ref[...] = jnp.concatenate([sums, sums], axis=1)
    const = lax.dot_general(
        shift_ref[...], head, dims, precision=HIGH, preferred_element_type=F32
    )
    hb = hb_ref[...]
    hb = jnp.concatenate([hb[:, 0:16], hb[:, 32:48], hb[:, 16:32], hb[:, 48:64]], axis=1)
    const = const + hb
    const_ref[...] = jnp.concatenate([const, const], axis=1)

    zero16 = jnp.zeros((16, 384), BF)
    for tap in range(2):
        for ly in range(4):
            for lx in range(4):
                row = (ly // 2) * 128 + lx * 32 + (ly % 2) * 16
                for qy in range(2):
                    for qx in range(2):
                        dy, dx = ly - qy, lx - qx
                        good = 0 <= dy < 3 and 0 <= dx < 3
                        piece = cin_ref[tap + 1, dy, dx] if good else zero16
                        col = (qy * 2 + qx) * 384
                        cin_out[tap, row : row + 16, col : col + 384] = piece

    taps = {(0, 0): (0, 1), (0, 1): (2,), (1, 0): (0,), (1, 1): (1, 2)}
    lane = lanes(384)
    for dx in range(2):
        for dy in range(2):
            for py in range(2):
                blocks = []
                for px in range(2):
                    total = None
                    for b in taps[py, dy]:
                        for e in taps[px, dx]:
                            term = up_ref[b, e].astype(F32)
                            total = term if total is None else total + term
                    blocks.append(total)
                left, right = blocks
                ends = jnp.concatenate([left[:, 128:192], right[:, 128:192]], axis=1)
                row = (dy * 2 + dx) * 384
                col = py * 384
                up_out[row : row + 384, col : col + 128] = left[:, 0:128].astype(BF)
                up_out[row : row + 384, col + 128 : col + 256] = right[:, 0:128].astype(BF)
                up_out[row : row + 384, col + 256 : col + 384] = ends.astype(BF)
    vec = upv_ref[...]
    piece = jnp.concatenate(
        [vec[:, 0:128], vec[:, 0:128], vec[:, 128:192], vec[:, 128:192]], axis=1
    )
    upv_out[...] = piece

    cout_out[...] = jnp.zeros(cout_out.shape, BF)
    for tap in range(2):
        for b in range(3):
            for v in range(2):
                for s in range(2):
                    for o in range(2):
                        e = 2 * v + s - o
                        if not 0 <= e < 3:
                            continue
                        row = b * 768 + v * 384
                        weight = cout_ref[tap + 1, b, e]
                        lo = row + s * 128
                        hi = row + 256 + s * 64
                        cout_out[tap, lo : lo + 128, o * 128 : o * 128 + 96] = weight[0:128]
                        cout_out[tap, hi : hi + 64, o * 128 : o * 128 + 96] = weight[128:192]


def prepare(head_weight, mod_scale, mod_shift, head_bias, devs, cin, up, upv, cout):
    count = devs.shape[0]
    return pl.pallas_call(
        prepare_kernel,
        out_shape=[
            jax.ShapeDtypeStruct((count, 128), F32),
            jax.ShapeDtypeStruct((1, 128), F32),
            jax.ShapeDtypeStruct((2, 256, 1536), BF),
            jax.ShapeDtypeStruct((1536, 768), BF),
            jax.ShapeDtypeStruct((2, 384), F32),
            jax.ShapeDtypeStruct((2, 2304, 256), BF),
        ],
        compiler_params=pltpu.CompilerParams(vmem_limit_bytes=40 << 20),
        cost_estimate=pl.CostEstimate(
            flops=20_000_000, bytes_accessed=10_000_000, transcendentals=0
        ),
        name="prepare",
    )(head_weight, mod_scale, mod_shift, head_bias, devs, cin, up, upv, cout)


def silu_half(half):
    return half + half * jnp.tanh(half)


def decode_kernel(
    flags_ref, sums_ref, table_ref, const_ref, cin_ref, cinv_ref, up_ref, upv_ref, cout_ref,
    coutv_ref, out_ref, fa, fb, fx, ua, ub, xe, xo, lines,
):
    count = table_ref.shape[0] // 2
    feats = count * 0 + flags_ref.shape[0] * 0
    del feats
    has_low = flags_ref[0]
    has_high = flags_ref[1]
    group = flags_ref[2].astype(F32)
    n_stat = sums_ref.shape[2] - HALF

    pick_row = lax.broadcasted_iota(jnp.int32, (count + 8, n_stat), 0)
    pick_col = lax.broadcasted_iota(jnp.int32, (count + 8, n_stat), 1)
    of_dev, of_kind = pick_col // STAT, pick_col % STAT
    pick = ((of_kind < 2) & (pick_row == of_dev)) | ((of_kind >= 2) & (pick_row == count))
    pick = pick.astype(F32).astype(BF)
    lane40, sub40 = lanes(HALF), lax.broadcasted_iota(jnp.int32, (HALF, 128), 0)
    lane80, sub80 = lanes(TOK_W), lax.broadcasted_iota(jnp.int32, (TOK_W, 128), 0)
    spread_mask = (lane40 % 64) == sub40
    ones_block = (
        (lax.broadcasted_iota(jnp.int32, (128, 128), 0) // 64) == (lanes(128) // 64)
    ).astype(F32)
    edge = [[None] * 3 for _ in range(2)]
    for j in range(3):
        halves = []
        for h in range(2):
            block = sums_ref[h, j]
            stats = jnp.dot(pick, block[HALF:], preferred_element_type=F32)
            means = stats[0:count]
            mean = jnp.sum(means, axis=0, keepdims=True) * (1.0 / count)
            off = means - mean
            total = count * group
            var = (
                stats[count : count + 1] + group * jnp.sum(off * off, axis=0, keepdims=True)
            ) / total
            inv = lax.rsqrt(var + EPS)
            shift = lax.dot_general(
                off, table_ref[h * count : (h + 1) * count], (((0,), (0,)), ((), ())),
                precision=HIGH, preferred_element_type=F32,
            )
            shift = jnp.where(lane40 < 64, shift[0:HALF], shift[64 : 64 + HALF])
            inv_all = jnp.dot(
                jnp.where(spread_mask, inv, 0.0), ones_block,
                precision=HIGH, preferred_element_type=F32,
            )
            halves.append((block[0:HALF].astype(F32) + shift) * inv_all + const_ref[...])
        row = jnp.concatenate(halves, axis=0)
        if j == 0:
            row = jnp.where(has_low > 0, row, 0.0)
        if j == 2:
            row = jnp.where(has_high > 0, row, 0.0)
        swapped = pltpu.roll(row, 64, 1)
        for f in range(2):
            first = lane80 < 64 if f == 0 else lane80 >= 64
            both = pltpu.roll(jnp.where(first, row, swapped), 32, 1)
            before = jnp.where(sub80 == 0, 0.0, pltpu.roll(both, 1, 0))
            after = jnp.where(sub80 == TOK_W - 1, 0.0, pltpu.roll(both, TOK_W - 1, 0))
            edge[f][j] = jnp.where(
                lane80 < 32, before, jnp.where(lane80 >= 96, after, both)
            ).astype(BF)

    def patch(f):
        return jnp.concatenate(
            [jnp.concatenate([edge[f][b], edge[f][b + 1]], axis=1) for b in range(2)], axis=0
        )

    patches = [patch(0), patch(1)]
    bias_in, gain_in = cinv_ref[0:1], cinv_ref[1:2] * 0.5
    sub_one = lax.broadcasted_iota(jnp.int32, (TOK_W, 384), 0)
    zeros_ext = jnp.zeros((TOK_W, 384), F32)
    for f in range(2):
        pre = jnp.dot(patches[f], cin_ref[1], preferred_element_type=F32)
        if f == 1:
            pre = pre + jnp.dot(patches[0], cin_ref[0], preferred_element_type=F32)
        for b in range(2):
            for qy in range(2):
                y = 2 * b + qy
                act = []
                for qx in range(2):
                    col = (qy * 2 + qx) * 384
                    v = pre[b * TOK_W : (b + 1) * TOK_W, col : col + 384] + bias_in
                    mean_sq = jnp.sum(v * v, axis=1, keepdims=True) * (1.0 / 384)
                    a = silu_half(v * lax.rsqrt(mean_sq + EPS) * gain_in)
                    if y == 0:
                        a = jnp.where(has_low > 0, a, 0.0)
                    if y == 3:
                        a = jnp.where(has_high > 0, a, 0.0)
                    act.append(a)
                even, odd = act
                back = jnp.where(sub_one == 0, 0.0, pltpu.roll(odd, 1, 0))
                even, odd, back = even.astype(BF), odd.astype(BF), back.astype(BF)
                for pair, part in ((y - 1, 1), (y, 0)):
                    if not 0 <= pair < 3:
                        continue
                    at = slice((f * 3 + pair) * TOK_W, (f * 3 + pair + 1) * TOK_W)
                    fa[at, part * 768 : part * 768 + 384] = even
                    fa[at, part * 768 + 384 : part * 768 + 768] = odd
                    fb[at, part * 768 : part * 768 + 384] = back
                    fb[at, part * 768 + 384 : part * 768 + 768] = even
                    fx[f * 3 + pair : f * 3 + pair + 1, part * 768 : part * 768 + 384] = act[1][
                        TOK_W - 1 : TOK_W
                    ]
                    fx[f * 3 + pair : f * 3 + pair + 1, part * 768 + 384 : part * 768 + 768] = (
                        zeros_ext[0:1]
                    )
    del sub_one

    ua[...] = jnp.dot(fa[...], up_ref[...], preferred_element_type=F32)
    ub[0 : 6 * TOK_W] = jnp.dot(fb[...], up_ref[...], preferred_element_type=F32)
    extra_in = jnp.where(
        lax.broadcasted_iota(jnp.int32, (8, 1536), 0) < 6, fx[...], 0.0
    )
    extra_in = jnp.concatenate([extra_in, jnp.zeros((8, 1536), F32)], axis=0).astype(BF)
    extra = jnp.dot(extra_in, up_ref[...], preferred_element_type=F32)[0:8]
    bias_up, gain_up = upv_ref[0:1], upv_ref[1:2] * 0.5

    def second(u):
        v = u + bias_up
        t0, t1, t2 = v[:, 0:128], v[:, 128:256], v[:, 256:384]
        lane = lanes(u.shape[0])
        q = t2 * t2
        left = jnp.sum(t0 * t0 + jnp.where(lane < 64, q, 0.0), axis=1, keepdims=True)
        right = jnp.sum(t1 * t1 + jnp.where(lane < 64, 0.0, q), axis=1, keepdims=True)
        left = lax.rsqrt(left * (1.0 / 192) + EPS)
        right = lax.rsqrt(right * (1.0 / 192) + EPS)
        g = gain_up
        return (
            silu_half(t0 * left * g[:, 0:128]),
            silu_half(t1 * right * g[:, 128:256]),
            silu_half(t2 * jnp.where(lane < 64, left, right) * g[:, 256:384]),
        )

    for f in range(2):
        for pair in range(3):
            at = (f * 3 + pair) * TOK_W
            for py in range(2):
                y = pair * 2 + py
                cols = slice(py * 384, py * 384 + 384)

                def keep(value, y=y):
                    if y == 0:
                        return jnp.where(has_low > 0, value, 0.0)
                    if y == 5:
                        return jnp.where(has_high > 0, value, 0.0)
                    return value

                mid = [keep(t) for t in second(ua[at : at + TOK_W, cols])]
                low = [keep(t) for t in second(ub[at : at + TOK_W, cols])]
                end = [keep(t) for t in second(extra[:, cols])]
                to = slice(y * TOK_W, (y + 1) * TOK_W)
                first = sub80 == 0
                low[0] = jnp.where(first, 0.0, low[0])
                low[2] = jnp.where(first & (lane80 < 64), 0.0, low[2])
                end[1] = jnp.zeros_like(end[1])
                end[2] = jnp.where(lanes(8) < 64, end[2], 0.0)
                for k in range(3):
                    m = mid[k].astype(BF)
                    xe[f, to, k * 128 : k * 128 + 128] = low[k].astype(BF)
                    xe[f, to, 384 + k * 128 : 512 + k * 128] = m
                    xo[f, to, k * 128 : k * 128 + 128] = m
                    last = end[k][f * 3 + pair : f * 3 + pair + 1]
                    ahead = jnp.where(
                        sub80 == TOK_W - 1, last, pltpu.roll(low[k], TOK_W - 1, 0)
                    )
                    xo[f, to, 384 + k * 128 : 512 + k * 128] = ahead.astype(BF)

    bias_out = coutv_ref[...]
    for f in range(2):
        for side, x in enumerate((xe, xo)):
            acc = None
            for b in range(3):
                rows = slice(b * TOK_W, (b + 4) * TOK_W)
                ks = slice(b * 768, b * 768 + 768)
                term = jnp.dot(x[f, rows], cout_ref[1, ks], preferred_element_type=F32)
                acc = term if acc is None else acc + term
                if f == 1:
                    acc = acc + jnp.dot(x[0, rows], cout_ref[0, ks], preferred_element_type=F32)
            for j in range(4):
                for o in range(2):
                    lines[j, pl.ds(2 * side + o, TOK_W, stride=4), :] = (
                        acc[j * TOK_W : (j + 1) * TOK_W, o * 128 : o * 128 + 128] + bias_out
                    )
        for j in range(4):
            out_ref[f, j] = lines[j][:, 0:96].astype(BF)


def decode(flags, sums, table, const, cin, cinv, up, upv, cout, coutv):
    vmem = pl.BlockSpec(memory_space=pltpu.VMEM)
    return pl.pallas_call(
        decode_kernel,
        in_specs=[pl.BlockSpec(memory_space=pltpu.SMEM)] + [vmem] * 9,
        out_specs=vmem,
        out_shape=jax.ShapeDtypeStruct((2, 4, 4 * TOK_W, 96), BF),
        scratch_shapes=[
            pltpu.VMEM((6 * TOK_W, 1536), BF),
            pltpu.VMEM((6 * TOK_W, 1536), BF),
            pltpu.VMEM((8, 1536), F32),
            pltpu.VMEM((6 * TOK_W, 768), F32),
            pltpu.VMEM((6 * TOK_W, 768), F32),
            pltpu.VMEM((2, 6 * TOK_W, 768), BF),
            pltpu.VMEM((2, 6 * TOK_W, 768), BF),
            pltpu.VMEM((4, 4 * TOK_W, 128), F32),
        ],
        compiler_params=pltpu.CompilerParams(vmem_limit_bytes=48 << 20),
        cost_estimate=pl.CostEstimate(
            flops=5_000_000_000, bytes_accessed=8_000_000, transcendentals=1_300_000
        ),
        name="decode",
    )(flags, sums, table, const, cin, cinv, up, upv, cout, coutv)


def exchange(block, mask, count):
    return lax.ppermute(block, "seq", [(i, i ^ mask) for i in range(count)])


def merged(own, received):
    total = own[:, :HALF].astype(F32)
    for item in received:
        total = total + item[:, :HALF].astype(F32)
    return jnp.concatenate(
        [total.astype(BF), own[:, HALF:]] + [item[:, HALF:] for item in received], axis=1
    )


def cut(block, start, size):
    return lax.dynamic_slice_in_dim(block, start, size, 0)


def gather_rows(parts, me, count):
    parts = parts[:, :, : HALF + STAT]
    core = me & 1
    own = lax.dynamic_index_in_dim(parts, core, 0, False)
    give = lax.dynamic_index_in_dim(parts, 1 - core, 0, False)
    block = merged(own, [exchange(give, 1, count)])
    order = [0, 1]

    def window(base, size):
        return jnp.clip(base - 1, 0, count - size)

    start = jnp.int32(0)
    bits = count.bit_length() - 1
    bit = bits - 2
    steps = [[2 << bit, 1 << bit, 3 << bit]]
    while bit > 1:
        bit -= 1
        steps.append([1 << bit])
    for masks in steps:
        unit = min(masks)
        size = unit + 2
        base = (me // unit) * unit
        new = window(base, size)
        received = [
            exchange(cut(block, window(base ^ mask, size) - start, size), mask, count)
            for mask in masks
        ]
        block = merged(cut(block, new - start, size), received)
        order = order + [o ^ mask for mask in masks for o in order]
        start = new
    padded = jnp.pad(block, ((1, 1), (0, 0), (0, 0)))
    mine = cut(padded, me - start, 3)
    other = exchange(cut(padded, (me ^ 1) - start, 3), 1, count)
    low = jnp.where(core == 0, mine, other)
    high = jnp.where(core == 0, other, mine)
    return jnp.stack([low, high]), order


def local(
    hidden,
    mod_shift,
    mod_scale,
    head_weight,
    head_bias,
    conv_in_weight,
    conv_in_bias,
    gain_in,
    up_weight,
    up_bias,
    gain_up,
    out_weight,
    out_bias,
):
    count = lax.axis_size("seq")
    me = lax.axis_index("seq")
    feats = hidden.shape[1]
    w_slice = lax.dynamic_slice_in_dim(head_weight, me * feats, feats, 1)
    scale_slice = lax.dynamic_slice_in_dim(mod_scale, me * feats, feats, 0)[None]
    parts = project(hidden, w_slice, scale_slice)
    sums, order = gather_rows(parts, me, count)
    masks = np.asarray(order, np.int32)
    devs = jnp.concatenate([((me // 2) * 2) ^ masks, ((me // 2) * 2 + 1) ^ masks])[:, None]
    table, const, cin, up, upv, cout = prepare(
        head_weight, mod_scale[None], mod_shift[None], head_bias[None], devs,
        conv_in_weight, up_weight, jnp.stack([up_bias, gain_up]), out_weight,
    )
    flags = jnp.stack([(me > 0).astype(jnp.int32), (me < count - 1).astype(jnp.int32), jnp.int32(feats)])
    cinv = jnp.stack([conv_in_bias, gain_in])
    coutv = jnp.pad(out_bias, (0, 32))[None]
    return decode(flags, sums, table, const, cin, cinv, up, upv, cout, coutv)


def solution(mesh):
    placed = (P("grp", "seq", None), P(), P(), P(), P(), P(), P(), P(), P(), P(), P(), P(), P())
    return jax.shard_map(
        local, mesh=mesh, in_specs=placed, out_specs=P("grp", "seq", None, None), check_vma=False
    )
```

time: 138 us -> 45.9 us (0.33)
  the two profiles are of different devices: /device:TPU:16 before, /device:TPU:0 now
where the time goes in v1:
time: 45.9 us; the launch traced here: 45.4 us
  Pallas kernels  15.2 us (33%)
  local copies, waits for them, and re-layouts  10.9 us (24%)
  waiting for transfers between devices  10.1 us (22%)
  starting transfers between devices  7.34 us (16%)
  other arithmetic  1.51 us (3%)
    pallas_call x1, Pallas kernels, decode(): pl.pallas_call(decode_kernel, in_specs=[pl.BlockSpec(memory_space=pltpu.S...  10.3 us
    ppermute x6, waiting for transfers between devices, exchange(): return lax.ppermute(block, 'seq', [(i, i ^ mask) for i in range(count)])  10.1 us
    ppermute x6, starting transfers between devices, exchange(): return lax.ppermute(block, 'seq', [(i, i ^ mask) for i in range(count)])  7.34 us
    unnamed x34, local copies, waits for them, and re-layouts  5.5 us
    pallas_call x1, Pallas kernels, prepare(): pl.pallas_call(prepare_kernel, out_shape=[jax.ShapeDtypeStruct((count, 12...  3.32 us
    pallas_call x1, Pallas kernels, project(): pl.pallas_call(project_kernel, grid=(tokens // block,), in_specs=[pl.Bloc...  1.59 us
    convert_element_type x2, other arithmetic, merged(): total.astype(BF)  1.19 us
    pallas_call x1, local copies, waits for them, and re-layouts, decode(): pl.pallas_call(decode_kernel, in_specs=[pl.BlockSpec(memory_space=pltpu.S...  1.09 us
  transfers between devices with their start and end apart: 6, of which 5 were waited for; matrix products, arithmetic and copies ran while one was open for 8% of the time, Pallas kernels for 7%

profile of v1, /device:TPU:0, one launch (start us, length us, event | category | flops | bytes accessed | tf_op | source)
XLA Modules:
  0.0 45.4 jit_solution(12526289380629927986)
XLA Ops:
  0.0 1.0 %constant_dynamic-slice_fusion.6.w_ref = f32[64,320]{1,0:T(8,128)S(1)} fusion(f32[64,5120]{1,0:T(8,128)} %w_ref.1, s32[]{:T(128)S(6)} %select_n.50), kind=kLoop, calls=%fused_computation.28 | loop fusion | bytes 163844 | tf_op jit(solution)/shard_map/dynamic_slice | solution.py:476
  1.0 0.0 copy-start.13
  1.0 0.8 %dynamic_slice.38 = f32[320]{0:T(512)S(1)} dynamic-slice(f32[5120]{0:T(1024)} %param.16, s32[]{:T(128)S(6)} %select_n.50), dynamic_slice_sizes={320} | dynamic-slice | bytes 2564 | tf_op jit(solution)/shard_map/dynamic_slice | solution.py:477
  1.8 1.4 %copy-done = bf16[2,320,1280]{2,1,0:T(8,128)(2,1)S(1)} copy-done((bf16[2,320,1280]{2,1,0:T(8,128)(2,1)S(1)}, bf16[2,320,1280]{2,1,0:T(8,128)(2,1)}, u32[]{:S(2)}) %copy-start) | copy-done | bytes 1638424
  3.2 1.6 %project.1 = bf16[2,16,48,128]{3,2,1,0:T(8,128)(2,1)S(1)} custom-call(bf16[2,320,1280]{2,1,0:T(8,128)(2,1)S(1)} %copy-done, f32[64,320]{1,0:T(8,128)S(1)} %constant_dynamic-slice_fusion.6.w_ref, f32[1,320]{1,0:T(1,128)S(1)} %broadcast_in_dim.18.scale_ref), custom_call_target="tpu_custom_call" | custom-call | tf_op jit(solution)/shard_map/project/pallas_call | solution.py:74
  4.8 0.8 %dynamic-slice_bitcast_fusion.1 = (bf16[16,44,128]{2,1,0:T(8,128)(2,1)}, bf16[16,44,128]{2,1,0:T(8,128)(2,1)}) fusion(bf16[2,16,44,128]{3,2,1,0:T(8,128)(2,1)S(1)} %bitcast.20, s32[]{:T(128)S(6)} %select_n.51, s32[]{:T(128)S(6)} %select_n.52), kind=kLoop, calls=%fused_computation.6 | loop fusion | bytes 720904 | tf_op jit(solution)/shard_map/jit(dynamic_index_in_dim)/squeeze | solution.py:423
  5.6 0.5 collective-permute-start
  6.1 0.0 copy-done.13
  6.1 0.1 add_bitcast_fusion
  6.1 0.1 copy.15.dev_ref
  6.2 0.0 copy-start.12
  6.2 0.0 copy-start.1
  6.3 0.0 copy-start.3
  6.3 0.0 copy-start.4
  6.3 0.0 copy-start.5
  6.3 0.0 copy-start.6
  6.3 2.6 %copy.16.up_ref = bf16[3,3,384,192]{3,2,1,0:T(8,128)(2,1)S(1)} copy(bf16[3,3,384,192]{2,3,1,0:T(8,128)(2,1)} %param.22) | data formatting | bytes 2654208 | tf_op args[8]
  9.0 0.8 %slice.71 = bf16[16,4,128]{2,1,0:T(4,128)(2,1)S(1)} slice(bf16[16,44,128]{2,1,0:T(8,128)(2,1)} %get-tuple-element.17), slice={[0:16], [40:44], [0:128]} | slice | bytes 32768 | tf_op jit(solution)/shard_map/slice | solution.py:412
  9.7 0.0 copy-done.9
  9.7 0.0 copy-done.10
  9.8 0.0 copy-done.11
  9.8 0.0 copy-done.12
  9.8 0.0 copy-done.1
  9.8 0.0 copy-done.3
  9.8 0.0 copy-done.4
  9.9 0.0 copy-done.5
  9.9 0.0 copy-done.6
  9.9 0.0 copy-start.2
  9.9 1.3 %copy-done.2 = bf16[3,3,3,192,96]{4,3,2,1,0:T(8,128)(2,1)S(1)} copy-done((bf16[3,3,3,192,96]{4,3,2,1,0:T(8,128)(2,1)S(1)}, bf16[3,3,3,192,96]{4,3,2,1,0:T(8,128)(2,1)}, u32[]{:S(2)}) %copy-start.2) | copy-done | bytes 995352
  11.2 3.3 %prepare.1 = (f32[32,128]{1,0:T(8,128)S(1)}, f32[1,128]{1,0:T(1,128)S(1)}, bf16[2,256,1536]{2,1,0:T(8,128)(2,1)S(1)}, bf16[1536,768]{1,0:T(8,128)(2,1)S(1)}, f32...) custom-call(f32[64,5120]{1,0:T(8,128)S(1)} %copy-done.1, f32[1,5120]{1,0:T(1,128)S(1)} %bitcast.21, ...), custom_call_target="tpu_custom_call" | custom-call | flops 20000000 | bytes 10000000 | tf_op jit(solution)/shard_map/prepare/pallas_call | solution.py:169
  14.5 0.0 copy-start.7
  14.6 0.0 collective-permute-done
  14.6 1.2 %add_convert_fusion = bf16[16,40,128]{2,1,0:T(8,128)(2,1)S(1)} fusion(bf16[16,44,128]{2,1,0:T(8,128)(2,1)} %collective-permute-done, bf16[16,44,128]{2,1,0:T(8,128)(2,1)S(1)} %copy-done.8), kind=kLoop, calls=%fused_computation.2 | loop fusion | flops 327680 | bytes 491520 | tf_op jit(solution)/shard_map/convert_element_type | solution.py:412
  15.8 0.8 %slice.72 = bf16[16,4,128]{2,1,0:T(4,128)(2,1)S(1)} slice(bf16[16,44,128]{2,1,0:T(8,128)(2,1)} %collective-permute-done), slice={[0:16], [40:44], [0:128]} | slice | bytes 32768 | tf_op jit(solution)/shard_map/slice | solution.py:412
  16.6 3.7 %collective-permute-start.1 = (bf16[6,48,128]{2,1,0:T(8,128)(2,1)S(1)}, bf16[6,48,128]{2,1,0:T(8,128)(2,1)S(1)}, u32[]{:S(2)}, u32[]{:S(2)}) collective-permute-start(bf16[6,48,128]{2,1,0:T(8,128)(2,1)S(1)} %get-tuple-element.21), channel_id=1, source_target_pairs={{0,8},{1,9},{2,10},{3,11},{4,12},{5,13},{6,14},{7,15},{8,0},{9,1},... | collective-permute-start | bytes 221192 | tf_op jit(solution)/shard_map/ppermute | solution.py:404
  20.3 1.6 %collective-permute-start.2 = (bf16[6,48,128]{2,1,0:T(8,128)(2,1)S(1)}, bf16[6,48,128]{2,1,0:T(8,128)(2,1)S(1)}, u32[]{:S(2)}, u32[]{:S(2)}) collective-permute-start(bf16[6,48,128]{2,1,0:T(8,128)(2,1)S(1)} %get-tuple-element.23), channel_id=1, source_target_pairs={{0,4},{1,5},{2,6},{3,7},{4,0},{5,1},{6,2},{7,3},{8,12},{9,13},{10,... | collective-permute-start | bytes 221192 | tf_op jit(solution)/shard_map/ppermute | solution.py:404
  21.8 0.0 collective-permute-start.3
  21.8 0.0 copy-done.14
  21.8 3.1 %collective-permute-done.1 = bf16[6,48,128]{2,1,0:T(8,128)(2,1)S(1)} collective-permute-done((bf16[6,48,128]{2,1,0:T(8,128)(2,1)S(1)}, bf16[6,48,128]{2,1,0:T(8,128)(2,1)S(1)}, u32[]{:S(2)}, u32[]{:S(2)}) %collective-permute-start.1) | collective-permute-done | bytes 73760 | tf_op jit(solution)/shard_map/ppermute | solution.py:404
  25.0 0.1 collective-permute-done.2
  25.1 2.9 %collective-permute-done.3 = bf16[6,48,128]{2,1,0:T(8,128)(2,1)S(1)} collective-permute-done((bf16[6,48,128]{2,1,0:T(8,128)(2,1)S(1)}, bf16[6,48,128]{2,1,0:T(8,128)(2,1)S(1)}, u32[]{:S(2)}, u32[]{:S(2)}) %collective-permute-start.3) | collective-permute-done | bytes 73760 | tf_op jit(solution)/shard_map/ppermute | solution.py:404
  28.1 1.6 %collective-permute-start.4 = (bf16[4,72,128]{2,1,0:T(8,128)(2,1)S(1)}, bf16[4,72,128]{2,1,0:T(8,128)(2,1)S(1)}, u32[]{:S(2)}, u32[]{:S(2)}) collective-permute-start(bf16[4,72,128]{2,1,0:T(8,128)(2,1)S(1)} %constant_dynamic-slice_fusion.1), channel_id=1, source_target_pairs={{0,2},{1,3},{2,0},{3,1},{4,6},{5,7},{6,4},{7,5},{8,10},{9,11},{10,... | collective-permute-start | bytes 221192 | tf_op jit(solution)/shard_map/ppermute | solution.py:404
  29.7 2.8 %collective-permute-done.4 = bf16[4,72,128]{2,1,0:T(8,128)(2,1)S(1)} collective-permute-done((bf16[4,72,128]{2,1,0:T(8,128)(2,1)S(1)}, bf16[4,72,128]{2,1,0:T(8,128)(2,1)S(1)}, u32[]{:S(2)}, u32[]{:S(2)}) %collective-permute-start.4) | collective-permute-done | bytes 73760 | tf_op jit(solution)/shard_map/ppermute | solution.py:404
  32.6 0.1 collective-permute-start.5
  32.7 0.1 pad_add_fusion.flags_ref
  32.8 1.2 %collective-permute-done.5 = bf16[3,104,128]{2,1,0:T(8,128)(2,1)S(1)} collective-permute-done((bf16[3,104,128]{2,1,0:T(8,128)(2,1)S(1)}, bf16[3,104,128]{2,1,0:T(8,128)(2,1)S(1)}, u32[]{:S(2)}, u32[]{:S(2)}) %collective-permute-start.5) | collective-permute-done | bytes 79904 | tf_op jit(solution)/shard_map/ppermute | solution.py:404
  34.0 10.3 %decode.1 = bf16[2,4,320,96]{3,2,1,0:T(8,128)(2,1)S(1)} custom-call(s32[3]{0:T(128)S(1)} %pad_add_fusion.flags_ref, bf16[2,3,104,128]{3,2,1,0:T(8,128)(2,1)S(1)} %pad_maximum_fusion.1.sums_ref, f32[32,128]{1,0:T(8,128)S(1)} %get-tuple-element.11.table_ref, f32[1,128]{1,0:T(1,128)S(1)} %get-tuple-element.12.const_ref, ...), custom_call_target="tpu_custom_call" | custom-call | flops 5000000000 | bytes 8000000 | tf_op jit(solution)/shard_map/decode/pallas_call | solution.py:380
  44.3 1.1 %copy.17 = bf16[2,4,320,96]{2,3,1,0:T(8,128)(2,1)} copy(bf16[2,4,320,96]{3,2,1,0:T(8,128)(2,1)S(1)} %decode.1) | data formatting | bytes 983040 | tf_op jit(solution)/shard_map/decode/pallas_call | solution.py:380
  (30 shorter events, 0.3 us)
Async XLA Ops:
  1.0 5.1 %copy-start.13 = (s32[16]{0:T(128)S(1)}, s32[16]{0:T(128)}, u32[]{:S(2)}) copy-start(s32[16]{0:T(128)} %constant.76.clone) | copy-start | bytes 196
  1.8 1.4 %copy-start = (bf16[2,320,1280]{2,1,0:T(8,128)(2,1)S(1)}, bf16[2,320,1280]{2,1,0:T(8,128)(2,1)}, u32[]{:S(2)}) copy-start(bf16[2,320,1280]{2,1,0:T(8,128)(2,1)} %hid_ref.1) | copy-start | bytes 4915204
  5.6 9.0 %collective-permute-start = (bf16[16,44,128]{2,1,0:T(8,128)(2,1)}, bf16[16,44,128]{2,1,0:T(8,128)(2,1)}, u32[]{:S(2)}, u32[]{:S(2)}) collective-permute-start(bf16[16,44,128]{2,1,0:T(8,128)(2,1)} %get-tuple-element.18), channel_id=1, source_target_pairs={{0,1},{1,0},{2,3},{3,2},{4,5},{5,4},{6,7},{7,6},{8,9},{9,8},{10,11... | collective-permute-start | bytes 540680 | tf_op jit(solution)/shard_map/ppermute | solution.py:404
  6.2 3.5 %copy-start.9 = (f32[384]{0:T(512)S(1)}, f32[384]{0:T(512)}, u32[]{:S(2)}) copy-start(f32[384]{0:T(512)} %param.20) | copy-start | bytes 4612
  6.2 3.5 %copy-start.10 = (f32[384]{0:T(512)S(1)}, f32[384]{0:T(512)}, u32[]{:S(2)}) copy-start(f32[384]{0:T(512)} %param.21) | copy-start | bytes 4612
  6.2 3.6 %copy-start.11 = (f32[192]{0:T(256)S(1)}, f32[192]{0:T(256)}, u32[]{:S(2)}) copy-start(f32[192]{0:T(256)} %param.24) | copy-start | bytes 2308
  6.2 3.6 %copy-start.12 = (f32[192]{0:T(256)S(1)}, f32[192]{0:T(256)}, u32[]{:S(2)}) copy-start(f32[192]{0:T(256)} %param.23) | copy-start | bytes 2308
  6.2 3.6 %copy-start.1 = (f32[64,5120]{1,0:T(8,128)S(1)}, f32[64,5120]{1,0:T(8,128)}, u32[]{:S(2)}) copy-start(f32[64,5120]{1,0:T(8,128)} %w_ref.1) | copy-start | bytes 3932164
  6.3 3.6 %copy-start.3 = (bf16[3,3,3,16,384]{4,3,2,1,0:T(8,128)(2,1)S(1)}, bf16[3,3,3,16,384]{4,3,2,1,0:T(8,128)(2,1)}, u32[]{:S(2)}) copy-start(bf16[3,3,3,16,384]{4,3,2,1,0:T(8,128)(2,1)} %cin_ref.1) | copy-start | bytes 995332
  6.3 3.6 %copy-start.4 = (f32[5120]{0:T(1024)S(1)}, f32[5120]{0:T(1024)}, u32[]{:S(2)}) copy-start(f32[5120]{0:T(1024)} %param.16) | copy-start | bytes 61444
  6.3 3.6 %copy-start.5 = (f32[5120]{0:T(1024)S(1)}, f32[5120]{0:T(1024)}, u32[]{:S(2)}) copy-start(f32[5120]{0:T(1024)} %param.15) | copy-start | bytes 61444
  6.3 3.6 %copy-start.6 = (f32[64]{0:T(128)S(1)}, f32[64]{0:T(128)}, u32[]{:S(2)}) copy-start(f32[64]{0:T(128)} %param.18) | copy-start | bytes 772
  9.9 1.3 %copy-start.2 = (bf16[3,3,3,192,96]{4,3,2,1,0:T(8,128)(2,1)S(1)}, bf16[3,3,3,192,96]{4,3,2,1,0:T(8,128)(2,1)}, u32[]{:S(2)}) copy-start(bf16[3,3,3,192,96]{4,3,2,1,0:T(8,128)(2,1)} %cout_ref.1) | copy-start | bytes 2985988
  11.2 3.4 %copy-start.8 = (bf16[16,44,128]{2,1,0:T(8,128)(2,1)S(1)}, bf16[16,44,128]{2,1,0:T(8,128)(2,1)}, u32[]{:S(2)}) copy-start(bf16[16,44,128]{2,1,0:T(8,128)(2,1)} %get-tuple-element.17) | copy-start | bytes 540676
  11.2 10.6 %copy-start.14 = (f32[96]{0:T(128)S(1)}, f32[96]{0:T(128)}, u32[]{:S(2)}) copy-start(f32[96]{0:T(128)} %param.26) | copy-start | bytes 1156
  14.5 19.5 %copy-start.7 = (bf16[2,2304,256]{2,1,0:T(8,128)(2,1)}, bf16[2,2304,256]{2,1,0:T(8,128)(2,1)S(1)}, u32[]{:S(2)}) copy-start(bf16[2,2304,256]{2,1,0:T(8,128)(2,1)S(1)} %get-tuple-element.16.cout_ref) | copy-start | bytes 7077892
  16.6 8.4 %collective-permute-start.1 = (bf16[6,48,128]{2,1,0:T(8,128)(2,1)S(1)}, bf16[6,48,128]{2,1,0:T(8,128)(2,1)S(1)}, u32[]{:S(2)}, u32[]{:S(2)}) collective-permute-start(bf16[6,48,128]{2,1,0:T(8,128)(2,1)S(1)} %get-tuple-element.21), channel_id=1, source_target_pairs={{0,8},{1,9},{2,10},{3,11},{4,12},{5,13},{6,14},{7,15},{8,0},{9,1},... | collective-permute-start | bytes 221192 | tf_op jit(solution)/shard_map/ppermute | solution.py:404
  20.3 4.8 %collective-permute-start.2 = (bf16[6,48,128]{2,1,0:T(8,128)(2,1)S(1)}, bf16[6,48,128]{2,1,0:T(8,128)(2,1)S(1)}, u32[]{:S(2)}, u32[]{:S(2)}) collective-permute-start(bf16[6,48,128]{2,1,0:T(8,128)(2,1)S(1)} %get-tuple-element.23), channel_id=1, source_target_pairs={{0,4},{1,5},{2,6},{3,7},{4,0},{5,1},{6,2},{7,3},{8,12},{9,13},{10,... | collective-permute-start | bytes 221192 | tf_op jit(solution)/shard_map/ppermute | solution.py:404
  21.8 6.2 %collective-permute-start.3 = (bf16[6,48,128]{2,1,0:T(8,128)(2,1)S(1)}, bf16[6,48,128]{2,1,0:T(8,128)(2,1)S(1)}, u32[]{:S(2)}, u32[]{:S(2)}) collective-permute-start(bf16[6,48,128]{2,1,0:T(8,128)(2,1)S(1)} %get-tuple-element.22), channel_id=1, source_target_pairs={{0,12},{1,13},{2,14},{3,15},{4,8},{5,9},{6,10},{7,11},{8,4},{9,5},... | collective-permute-start | bytes 221192 | tf_op jit(solution)/shard_map/ppermute | solution.py:404
  28.1 4.4 %collective-permute-start.4 = (bf16[4,72,128]{2,1,0:T(8,128)(2,1)S(1)}, bf16[4,72,128]{2,1,0:T(8,128)(2,1)S(1)}, u32[]{:S(2)}, u32[]{:S(2)}) collective-permute-start(bf16[4,72,128]{2,1,0:T(8,128)(2,1)S(1)} %constant_dynamic-slice_fusion.1), channel_id=1, source_target_pairs={{0,2},{1,3},{2,0},{3,1},{4,6},{5,7},{6,4},{7,5},{8,10},{9,11},{10,... | collective-permute-start | bytes 221192 | tf_op jit(solution)/shard_map/ppermute | solution.py:404
  32.6 1.3 %collective-permute-start.5 = (bf16[3,104,128]{2,1,0:T(8,128)(2,1)S(1)}, bf16[3,104,128]{2,1,0:T(8,128)(2,1)S(1)}, u32[]{:S(2)}, u32[]{:S(2)}) collective-permute-start(bf16[3,104,128]{2,1,0:T(8,128)(2,1)S(1)} %constant_dynamic-slice_fusion), channel_id=1, source_target_pairs={{0,1},{1,0},{2,3},{3,2},{4,5},{5,4},{6,7},{7,6},{8,9},{9,8},{10,11... | collective-permute-start | bytes 239624 | tf_op jit(solution)/shard_map/ppermute | solution.py:404

commit v2 on v1

--- a/solution.py
+++ b/solution.py
@@ -16,6 +16,10 @@
 F32 = jnp.float32
 
 
+def in_hbm(value):
+    return pltpu.with_memory_space_constraint(value, pltpu.HBM)
+
+
 def split(values):
     high = values.astype(BF).astype(F32)
     return high, values - high
@@ -25,73 +29,176 @@
     return lax.broadcasted_iota(jnp.int32, (rows, 128), 1)
 
 
-def project_kernel(hid_ref, w_ref, scale_ref, out_ref):
-    feats = hid_ref.shape[1]
-    width = hid_ref.shape[2]
-    gain = w_ref[...] * (1.0 + scale_ref[...])
+def project_kernel(flags_ref, hid_ref, w_ref, scale_ref, own_ref, give_ref, hid, w, scale, sems):
+    frames, feats, tokens = hid_ref.shape
+    width = hid.shape[3]
+    me = flags_ref[0]
+    core = me & 1
+    wide = w.shape[1]
+    at = jnp.minimum(lax.div(me * feats, 128) * 128, w_ref.shape[1] - wide)
+    at = pl.multiple_of(at, 128)
+    copies = [
+        pltpu.make_async_copy(w_ref.at[:, pl.ds(at, wide)], w, sems.at[0]),
+        pltpu.make_async_copy(scale_ref.at[:, pl.ds(at, wide)], scale, sems.at[1]),
+    ]
+    blocks = tokens // width
+    for i in range(blocks):
+        copies.append(
+            pltpu.make_async_copy(
+                hid_ref.at[:, :, pl.ds(i * width, width)], hid.at[i], sems.at[2 + i]
+            )
+        )
+    for copy in copies:
+        copy.start()
+    copies[0].wait()
+    copies[1].wait()
+    gain = w[...] * (1.0 + scale[...])
+    gain = pltpu.roll(gain, wide - (me * feats - at), 1)[:, :feats]
     gain = jnp.concatenate([gain[0:16], gain[32:48], gain[16:32], gain[48:64]], axis=0)
     high, low = split(gain)
     gain_sum = jnp.sum(gain, axis=1, keepdims=True)
     stack = jnp.concatenate([high, low, jnp.ones((16, feats), F32)], axis=0).astype(BF)
-    parts, stats = [], []
-    for f in range(2):
-        x = hid_ref[f]
-        prod = jnp.dot(stack, x, preferred_element_type=F32)
-        mean = prod[128:129] * (1.0 / feats)
-        parts.append(prod[0:64] + prod[64:128] - gain_sum * mean)
-        off = x.astype(F32) - mean
-        second = jnp.sum(off * off, axis=0, keepdims=True)
-        m_hi, m_lo = split(mean)
-        s_hi, s_lo = split(second)
-        stats.append(
-            jnp.concatenate([m_hi, m_lo, s_hi, s_lo, jnp.zeros((4, width), F32)], axis=0)
-        )
-    flat = jnp.concatenate(parts, axis=0).T
     lane = lanes(8)
-    for row in range(width // TOK_W):
-        for h in range(2):
-            at = row * TOK_W + h * HALF
-            base = (at // 128) * 128
-            wide = min(256, width - base)
-            picks = []
-            for f in range(2):
-                window = stats[f][:, base : base + wide]
-                shift = (64 * f - (at - base)) % wide
-                if shift:
-                    window = pltpu.roll(window, shift, 1)
-                picks.append(window[:, :128])
-            tail = jnp.where(
-                lane < HALF, picks[0], jnp.where((lane >= 64) & (lane < 64 + HALF), picks[1], 0.0)
-            )
-            out_ref[h, row] = jnp.concatenate([flat[at : at + HALF], tail], axis=0).astype(BF)
-
-
-def project(hidden, w_slice, scale_slice):
+    sub = lax.broadcasted_iota(jnp.int32, (8, 128), 0)
+    for i in range(blocks):
+        copies[2 + i].wait()
+        parts, stats = [], []
+        for f in range(frames):
+            x = hid[i, f]
+            prod = jnp.dot(stack, x, preferred_element_type=F32)
+            mean = prod[128:129] * (1.0 / feats)
+            parts.append(prod[0:64] + prod[64:128] - gain_sum * mean)
+            off = x.astype(F32) - mean
+            second = jnp.sum(off * off, axis=0, keepdims=True)
+            m_hi, m_lo = split(mean)
+            s_hi, s_lo = split(second)
+            four = jnp.concatenate([m_hi, m_lo, s_hi, s_lo] * 2, axis=0)
+            stats.append(four)
+        flat = jnp.concatenate(parts, axis=0).T
+        for row in range(width // TOK_W):
+            pair = []
+            for h in range(2):
+                first = row * TOK_W + h * HALF
+                base = (first // 128) * 128
+                span = min(256, width - base)
+                picks = []
+                for f in range(2):
+                    window = stats[f][:, base : base + span]
+                    shift = (64 * f - (first - base)) % span
+                    if shift:
+                        window = pltpu.roll(window, shift, 1)
+                    picks.append(window[:, :128])
+                tail = jnp.where(
+                    lane < HALF,
+                    picks[0],
+                    jnp.where((lane >= 64) & (lane < 64 + HALF), picks[1], 0.0),
+                )
+                tail = jnp.where(lax.div(sub, STAT) == core, tail, 0.0)
+                pair.append(jnp.concatenate([flat[first : first + HALF], tail], axis=0))
+            to = i * (width // TOK_W) + row
+            own_ref[to] = jnp.where(core == 0, pair[0], pair[1]).astype(BF)
+            give_ref[to] = jnp.where(core == 0, pair[1], pair[0]).astype(BF)
+
+
+def project(flags, hidden, head_weight, scale):
     frames, feats, tokens = hidden.shape
-    block = 640
+    width = 640
     rows = tokens // TOK_W
-    rows_block = block // TOK_W
+    wide = min(head_weight.shape[1], (feats + 127) // 128 * 128 + 128)
+    hbm = pl.BlockSpec(memory_space=pltpu.HBM)
+    vmem = pl.BlockSpec(memory_space=pltpu.VMEM)
     return pl.pallas_call(
         project_kernel,
-        grid=(tokens // block,),
-        in_specs=[
-            pl.BlockSpec((frames, feats, block), lambda i: (0, 0, i)),
-            pl.BlockSpec((64, feats), lambda i: (0, 0)),
-            pl.BlockSpec((1, feats), lambda i: (0, 0)),
+        in_specs=[pl.BlockSpec(memory_space=pltpu.SMEM), hbm, hbm, hbm],
+        out_specs=[vmem, vmem],
+        out_shape=[jax.ShapeDtypeStruct((rows, HALF + 2 * STAT, 128), BF)] * 2,
+        scratch_shapes=[
+            pltpu.VMEM((tokens // width, frames, feats, width), BF),
+            pltpu.VMEM((64, wide), F32),
+            pltpu.VMEM((1, wide), F32),
+            pltpu.SemaphoreType.DMA((2 + tokens // width,)),
         ],
-        out_specs=pl.BlockSpec((2, rows_block, 48, 128), lambda i: (0, i, 0, 0)),
-        out_shape=jax.ShapeDtypeStruct((2, rows, 48, 128), BF),
-        compiler_params=pltpu.CompilerParams(vmem_limit_bytes=32 << 20),
+        compiler_params=pltpu.CompilerParams(vmem_limit_bytes=16 << 20),
         name="project",
-    )(hidden, w_slice, scale_slice)
+    )(flags, in_hbm(hidden), in_hbm(head_weight), in_hbm(scale))
+
+
+def prepare_first(cin_ref, cin_out):
+    zero16 = jnp.zeros((16, 384), BF)
+    for tap in range(2):
+        for ly in range(4):
+            for lx in range(4):
+                row = (ly // 2) * 128 + lx * 32 + (ly % 2) * 16
+                for qy in range(2):
+                    for qx in range(2):
+                        dy, dx = ly - qy, lx - qx
+                        good = 0 <= dy < 3 and 0 <= dx < 3
+                        piece = cin_ref[tap + 1, dy, dx] if good else zero16
+                        col = (qy * 2 + qx) * 384
+                        cin_out[tap, row : row + 16, col : col + 384] = piece
+
+
+def prepare_up(up_ref, up_out):
+    taps = {(0, 0): (0, 1), (0, 1): (2,), (1, 0): (0,), (1, 1): (1, 2)}
+    for dx in range(2):
+        for dy in range(2):
+            for py in range(2):
+                for px in range(2):
+                    total = None
+                    for b in taps[py, dy]:
+                        for e in taps[px, dx]:
+                            term = up_ref[b, e].astype(F32)
+                            total = term if total is None else total + term
+                    total = total.astype(BF)
+                    k = slice((dy * 2 + dx) * 384, (dy * 2 + dx + 1) * 384)
+                    n = py * 384
+                    up_out[n + px * 128 : n + px * 128 + 128, k] = total[0:128]
+                    up_out[n + 256 + px * 64 : n + 320 + px * 64, k] = total[128:192]
+
+
+def prepare_last(cout_ref, cout_out):
+    cout_out[...] = jnp.zeros(cout_out.shape, BF)
+    for tap in range(2):
+        for b in range(3):
+            for v in range(2):
+                for s in range(2):
+                    for o in range(2):
+                        e = 2 * v + s - o
+                        if not 0 <= e < 3:
+                            continue
+                        row = b * 768 + v * 384
+                        weight = cout_ref[tap + 1, b, e]
+                        lo = row + s * 128
+                        hi = row + 256 + s * 64
+                        cout_out[tap, lo : lo + 128, o * 128 : o * 128 + 96] = weight[0:128]
+                        cout_out[tap, hi : hi + 64, o * 128 : o * 128 + 96] = weight[128:192]
 
 
 def prepare_kernel(
     w_ref, scale_ref, shift_ref, hb_ref, dev_ref, cin_ref, up_ref, upv_ref, cout_ref,
-    table_ref, const_ref, cin_out, up_out, upv_out, cout_out,
+    table_ref, const_ref, cin_out, up_out, upv_out, cout_out, w, cin, up, cout, sems,
 ):
-    feats = w_ref.shape[1] * 2 // dev_ref.shape[0]
-    head = w_ref[...]
+    copies = [
+        pltpu.make_async_copy(source, target, sems.at[i])
+        for i, (source, target) in enumerate(
+            ((cin_ref, cin), (up_ref, up), (cout_ref, cout), (w_ref, w))
+        )
+    ]
+    for copy in copies:
+        copy.start()
+    copies[0].wait()
+    prepare_first(cin, cin_out)
+    copies[1].wait()
+    prepare_up(up, up_out)
+    vec = upv_ref[...]
+    upv_out[...] = jnp.concatenate(
+        [vec[:, 0:128], vec[:, 0:128], vec[:, 128:192], vec[:, 128:192]], axis=1
+    )
+    copies[2].wait()
+    prepare_last(cout, cout_out)
+    copies[3].wait()
+    feats = w_ref.shape[1] // dev_ref.shape[0]
+    head = w[...]
     head = jnp.concatenate([head[0:16], head[32:48], head[16:32], head[48:64]], axis=0)
     gain = head * (1.0 + scale_ref[...])
     count = dev_ref.shape[0]
@@ -108,80 +215,38 @@
     const = const + hb
     const_ref[...] = jnp.concatenate([const, const], axis=1)
 
-    zero16 = jnp.zeros((16, 384), BF)
-    for tap in range(2):
-        for ly in range(4):
-            for lx in range(4):
-                row = (ly // 2) * 128 + lx * 32 + (ly % 2) * 16
-                for qy in range(2):
-                    for qx in range(2):
-                        dy, dx = ly - qy, lx - qx
-                        good = 0 <= dy < 3 and 0 <= dx < 3
-                        piece = cin_ref[tap + 1, dy, dx] if good else zero16
-                        col = (qy * 2 + qx) * 384
-                        cin_out[tap, row : row + 16, col : col + 384] = piece
-
-    taps = {(0, 0): (0, 1), (0, 1): (2,), (1, 0): (0,), (1, 1): (1, 2)}
-    lane = lanes(384)
-    for dx in range(2):
-        for dy in range(2):
-            for py in range(2):
-                blocks = []
-                for px in range(2):
-                    total = None
-                    for b in taps[py, dy]:
-                        for e in taps[px, dx]:
-                            term = up_ref[b, e].astype(F32)
-                            total = term if total is None else total + term
-                    blocks.append(total)
-                left, right = blocks
-                ends = jnp.concatenate([left[:, 128:192], right[:, 128:192]], axis=1)
-                row = (dy * 2 + dx) * 384
-                col = py * 384
-                up_out[row : row + 384, col : col + 128] = left[:, 0:128].astype(BF)
-                up_out[row : row + 384, col + 128 : col + 256] = right[:, 0:128].astype(BF)
-                up_out[row : row + 384, col + 256 : col + 384] = ends.astype(BF)
-    vec = upv_ref[...]
-    piece = jnp.concatenate(
-        [vec[:, 0:128], vec[:, 0:128], vec[:, 128:192], vec[:, 128:192]], axis=1
-    )
-    upv_out[...] = piece
-
-    cout_out[...] = jnp.zeros(cout_out.shape, BF)
-    for tap in range(2):
-        for b in range(3):
-            for v in range(2):
-                for s in range(2):
-                    for o in range(2):
-                        e = 2 * v + s - o
-                        if not 0 <= e < 3:
-                            continue
-                        row = b * 768 + v * 384
-                        weight = cout_ref[tap + 1, b, e]
-                        lo = row + s * 128
-                        hi = row + 256 + s * 64
-                        cout_out[tap, lo : lo + 128, o * 128 : o * 128 + 96] = weight[0:128]
-                        cout_out[tap, hi : hi + 64, o * 128 : o * 128 + 96] = weight[128:192]
-
 
 def prepare(head_weight, mod_scale, mod_shift, head_bias, devs, cin, up, upv, cout):
     count = devs.shape[0]
+    hbm = pl.BlockSpec(memory_space=pltpu.HBM)
+    vmem = pl.BlockSpec(memory_space=pltpu.VMEM)
     return pl.pallas_call(
         prepare_kernel,
+        in_specs=[hbm, vmem, vmem, vmem, vmem, hbm, hbm, vmem, hbm],
+        scratch_shapes=[
+            pltpu.VMEM(head_weight.shape, F32),
+            pltpu.VMEM(cin.shape, BF),
+            pltpu.VMEM(up.shape, BF),
+            pltpu.VMEM(cout.shape, BF),
+            pltpu.SemaphoreType.DMA((4,)),
+        ],
         out_shape=[
             jax.ShapeDtypeStruct((count, 128), F32),
             jax.ShapeDtypeStruct((1, 128), F32),
             jax.ShapeDtypeStruct((2, 256, 1536), BF),
-            jax.ShapeDtypeStruct((1536, 768), BF),
+            jax.ShapeDtypeStruct((768, 1536), BF),
             jax.ShapeDtypeStruct((2, 384), F32),
             jax.ShapeDtypeStruct((2, 2304, 256), BF),
         ],
-        compiler_params=pltpu.CompilerParams(vmem_limit_bytes=40 << 20),
+        compiler_params=pltpu.CompilerParams(vmem_limit_bytes=20 << 20),
         cost_estimate=pl.CostEstimate(
             flops=20_000_000, bytes_accessed=10_000_000, transcendentals=0
         ),
         name="prepare",
-    )(head_weight, mod_scale, mod_shift, head_bias, devs, cin, up, upv, cout)
+    )(
+        in_hbm(head_weight), mod_scale, mod_shift, head_bias, devs, in_hbm(cin), in_hbm(up), upv,
+        in_hbm(cout),
+    )
 
 
 def silu_half(half):
@@ -189,15 +254,12 @@
 
 
 def decode_kernel(
-    flags_ref, sums_ref, table_ref, const_ref, cin_ref, cinv_ref, up_ref, upv_ref, cout_ref,
+    group, flags_ref, sums_ref, table_ref, const_ref, cin_ref, cinv_ref, up_ref, upv_ref, cout_ref,
     coutv_ref, out_ref, fa, fb, fx, ua, ub, xe, xo, lines,
 ):
-    count = table_ref.shape[0] // 2
-    feats = count * 0 + flags_ref.shape[0] * 0
-    del feats
-    has_low = flags_ref[0]
-    has_high = flags_ref[1]
-    group = flags_ref[2].astype(F32)
+    count = table_ref.shape[0]
+    has_low = flags_ref[1]
+    has_high = flags_ref[2]
     n_stat = sums_ref.shape[2] - HALF
 
     pick_row = lax.broadcasted_iota(jnp.int32, (count + 8, n_stat), 0)
@@ -220,13 +282,13 @@
             means = stats[0:count]
             mean = jnp.sum(means, axis=0, keepdims=True) * (1.0 / count)
             off = means - mean
-            total = count * group
+            feats_all = count * group
             var = (
                 stats[count : count + 1] + group * jnp.sum(off * off, axis=0, keepdims=True)
-            ) / total
+            ) / feats_all
             inv = lax.rsqrt(var + EPS)
             shift = lax.dot_general(
-                off, table_ref[h * count : (h + 1) * count], (((0,), (0,)), ((), ())),
+                off, table_ref[...], (((0,), (0,)), ((), ())),
                 precision=HIGH, preferred_element_type=F32,
             )
             shift = jnp.where(lane40 < 64, shift[0:HALF], shift[64 : 64 + HALF])
@@ -296,13 +358,17 @@
                     )
     del sub_one
 
-    ua[...] = jnp.dot(fa[...], up_ref[...], preferred_element_type=F32)
-    ub[0 : 6 * TOK_W] = jnp.dot(fb[...], up_ref[...], preferred_element_type=F32)
+    def times_up(x):
+        dims = (((1,), (1,)), ((), ()))
+        return lax.dot_general(x, up_ref[...], dims, preferred_element_type=F32)
+
+    ua[...] = times_up(fa[...])
+    ub[0 : 6 * TOK_W] = times_up(fb[...])
     extra_in = jnp.where(
         lax.broadcasted_iota(jnp.int32, (8, 1536), 0) < 6, fx[...], 0.0
     )
     extra_in = jnp.concatenate([extra_in, jnp.zeros((8, 1536), F32)], axis=0).astype(BF)
-    extra = jnp.dot(extra_in, up_ref[...], preferred_element_type=F32)[0:8]
+    extra = times_up(extra_in)[0:8]
     bias_up, gain_up = upv_ref[0:1], upv_ref[1:2] * 0.5
 
     def second(u):
@@ -372,16 +438,16 @@
                         acc[j * TOK_W : (j + 1) * TOK_W, o * 128 : o * 128 + 128] + bias_out
                     )
         for j in range(4):
-            out_ref[f, j] = lines[j][:, 0:96].astype(BF)
-
-
-def decode(flags, sums, table, const, cin, cinv, up, upv, cout, coutv):
+            out_ref[f, j] = lines[j].T[0:96].astype(BF)
+
+
+def decode(group, flags, sums, table, const, cin, cinv, up, upv, cout, coutv):
     vmem = pl.BlockSpec(memory_space=pltpu.VMEM)
     return pl.pallas_call(
-        decode_kernel,
+        functools.partial(decode_kernel, float(group)),
         in_specs=[pl.BlockSpec(memory_space=pltpu.SMEM)] + [vmem] * 9,
         out_specs=vmem,
-        out_shape=jax.ShapeDtypeStruct((2, 4, 4 * TOK_W, 96), BF),
+        out_shape=jax.ShapeDtypeStruct((2, 4, 96, 4 * TOK_W), BF),
         scratch_shapes=[
             pltpu.VMEM((6 * TOK_W, 1536), BF),
             pltpu.VMEM((6 * TOK_W, 1536), BF),
@@ -392,7 +458,7 @@
             pltpu.VMEM((2, 6 * TOK_W, 768), BF),
             pltpu.VMEM((4, 4 * TOK_W, 128), F32),
         ],
-        compiler_params=pltpu.CompilerParams(vmem_limit_bytes=48 << 20),
+        compiler_params=pltpu.CompilerParams(vmem_limit_bytes=24 << 20),
         cost_estimate=pl.CostEstimate(
             flops=5_000_000_000, bytes_accessed=8_000_000, transcendentals=1_300_000
         ),
@@ -417,25 +483,32 @@
     return lax.dynamic_slice_in_dim(block, start, size, 0)
 
 
-def gather_rows(parts, me, count):
-    parts = parts[:, :, : HALF + STAT]
-    core = me & 1
-    own = lax.dynamic_index_in_dim(parts, core, 0, False)
-    give = lax.dynamic_index_in_dim(parts, 1 - core, 0, False)
-    block = merged(own, [exchange(give, 1, count)])
-    order = [0, 1]
-
-    def window(base, size):
-        return jnp.clip(base - 1, 0, count - size)
-
-    start = jnp.int32(0)
-    bits = count.bit_length() - 1
-    bit = bits - 2
+def steps_of(count):
+    bit = count.bit_length() - 3
     steps = [[2 << bit, 1 << bit, 3 << bit]]
     while bit > 1:
         bit -= 1
         steps.append([1 << bit])
-    for masks in steps:
+    return steps
+
+
+def device_order(count):
+    order = [0]
+    for masks in steps_of(count):
+        order = order + [o ^ mask for mask in masks for o in order]
+    return np.asarray([o + c for o in order for c in range(2)], np.int32)
+
+
+def gather_rows(own, give, weights, ready, me, count):
+    core = me & 1
+    block = (own.astype(F32) + exchange(give, 1, count).astype(F32)).astype(BF)
+    block, weights = lax.optimization_barrier((block, weights))
+
+    def window(base, size):
+        return jnp.clip(base - 1, 0, count - size)
+
+    start = jnp.int32(0)
+    for masks in steps_of(count):
         unit = min(masks)
         size = unit + 2
         base = (me // unit) * unit
@@ -445,14 +518,15 @@
             for mask in masks
         ]
         block = merged(cut(block, new - start, size), received)
-        order = order + [o ^ mask for mask in masks for o in order]
+        if len(masks) > 1:
+            block, weights = lax.optimization_barrier((block, ready(weights)))
         start = new
     padded = jnp.pad(block, ((1, 1), (0, 0), (0, 0)))
     mine = cut(padded, me - start, 3)
     other = exchange(cut(padded, (me ^ 1) - start, 3), 1, count)
     low = jnp.where(core == 0, mine, other)
     high = jnp.where(core == 0, other, mine)
-    return jnp.stack([low, high]), order
+    return jnp.stack([low, high]), weights
 
 
 def local(
@@ -473,20 +547,24 @@
     count = lax.axis_size("seq")
     me = lax.axis_index("seq")
     feats = hidden.shape[1]
-    w_slice = lax.dynamic_slice_in_dim(head_weight, me * feats, feats, 1)
-    scale_slice = lax.dynamic_slice_in_dim(mod_scale, me * feats, feats, 0)[None]
-    parts = project(hidden, w_slice, scale_slice)
-    sums, order = gather_rows(parts, me, count)
-    masks = np.asarray(order, np.int32)
-    devs = jnp.concatenate([((me // 2) * 2) ^ masks, ((me // 2) * 2 + 1) ^ masks])[:, None]
-    table, const, cin, up, upv, cout = prepare(
-        head_weight, mod_scale[None], mod_shift[None], head_bias[None], devs,
-        conv_in_weight, up_weight, jnp.stack([up_bias, gain_up]), out_weight,
-    )
-    flags = jnp.stack([(me > 0).astype(jnp.int32), (me < count - 1).astype(jnp.int32), jnp.int32(feats)])
+    flags = jnp.stack([me, (me > 0).astype(jnp.int32), (me < count - 1).astype(jnp.int32)])
+    own, give = project(flags, hidden, head_weight, mod_scale[None])
+    weights = (head_weight, conv_in_weight, jnp.swapaxes(up_weight, 2, 3), out_weight)
+
+    def ready(parts):
+        head_again, cin, up, cout = parts
+        return prepare(
+            head_again, mod_scale[None], mod_shift[None], head_bias[None],
+            (((me // 2) * 2) ^ device_order(count))[:, None],
+            cin, up, jnp.stack([up_bias, gain_up]), cout,
+        )
+
+    sums, weights = gather_rows(own, give, weights, ready, me, count)
+    table, const, cin, up, upv, cout = weights
     cinv = jnp.stack([conv_in_bias, gain_in])
     coutv = jnp.pad(out_bias, (0, 32))[None]
-    return decode(flags, sums, table, const, cin, cinv, up, upv, cout, coutv)
+    out = decode(feats, flags, sums, table, const, cin, cinv, up, upv, cout, coutv)
+    return jnp.swapaxes(out, 2, 3)
 
 
 def solution(mesh):

time: 45.9 us -> 32.6 us (0.71)
  local copies, waits for them, and re-layouts: 10.9 us -> 0.25 us
  waiting for transfers between devices: 10.1 us -> 5.21 us
  Pallas kernels: 15.2 us -> 18.6 us
  other arithmetic: 1.51 us -> 0.28 us
  starting transfers between devices: 7.34 us -> 7.89 us
    unnamed x34 -> x21, local copies, waits for them, and re-layouts: 5.5 us -> 0.08 us
    ppermute x6, waiting for transfers between devices: 10.1 us -> 5.21 us  [exchange(): return lax.ppermute(block, 'seq', [(i, i ^ mask) for i in range(count)])]
    pallas_call x3, Pallas kernels: 15.2 us -> 18.6 us  [the longest x1 10.2 us: decode(): pl.pallas_call(functools.partial(decode_kernel, float(group)), in_specs=[...]
    dynamic_slice x2 -> x0, local copies, waits for them, and re-layouts: 1.77 us -> none  [the longest x1 0.99 us: local(): w_slice = lax.dynamic_slice_in_dim(head_weight, me * feats, feats, 1)]
    convert_element_type x2 -> x1, other arithmetic: 1.19 us -> 0.01 us  [merged(): total.astype(BF)]
    pallas_call x1 -> x0, local copies, waits for them, and re-layouts: 1.09 us -> none  [decode(): pl.pallas_call(decode_kernel, in_specs=[pl.BlockSpec(memory_space=pltpu.S...]
    squeeze x1 -> x0, local copies, waits for them, and re-layouts: 0.78 us -> none  [gather_rows(): own = lax.dynamic_index_in_dim(parts, core, 0, False)]
    slice x2 -> x1, local copies, waits for them, and re-layouts: 0.77 us -> 0.01 us  [merged(): own[:, HALF:]]
  transfers between devices with their start and end apart: 6 -> 6, of which waited for: 5 -> 4; matrix products, arithmetic and copies ran while one was open for 8% -> 0% of each run, Pallas kernels for 7% -> 16%
where the time goes in v2:
time: 32.6 us; the launch traced here: 32.4 us
  Pallas kernels  18.6 us (57%)
  starting transfers between devices  7.89 us (24%)
  waiting for transfers between devices  5.21 us (16%)
    pallas_call x1, Pallas kernels, decode(): pl.pallas_call(functools.partial(decode_kernel, float(group)), in_specs=[...  10.2 us
    ppermute x6, starting transfers between devices, exchange(): return lax.ppermute(block, 'seq', [(i, i ^ mask) for i in range(count)])  7.89 us
    ppermute x6, waiting for transfers between devices, exchange(): return lax.ppermute(block, 'seq', [(i, i ^ mask) for i in range(count)])  5.21 us
    pallas_call x1, Pallas kernels, prepare(): pl.pallas_call(prepare_kernel, in_specs=[hbm, vmem, vmem, vmem, vmem, hbm...  5.15 us
    pallas_call x1, Pallas kernels, project(): pl.pallas_call(project_kernel, in_specs=[pl.BlockSpec(memory_space=pltpu....  3.22 us
  transfers between devices with their start and end apart: 6, of which 4 were waited for; matrix products, arithmetic and copies ran while one was open for 0% of the time, Pallas kernels for 16%

profile of v2, /device:TPU:0, one launch (start us, length us, event | category | flops | bytes accessed | tf_op | source)
XLA Modules:
  0.0 32.4 jit_solution(15718772160515259257)
XLA Ops:
  0.0 0.0 copy-start.8
  0.0 0.0 copy-start.3
  0.0 0.0 copy-start.4
  0.0 0.1 pad_add_fusion.flags_ref
  0.1 0.0 copy-start.5
  0.1 0.0 copy-start.6
  0.1 0.0 copy-start
  0.1 0.0 copy-start.1
  0.1 0.0 copy-start.2
  0.1 3.2 %project.1 = (bf16[16,48,128]{2,1,0:T(8,128)(2,1)S(1)}, bf16[16,48,128]{2,1,0:T(8,128)(2,1)S(1)}) custom-call(s32[3]{0:T(128)S(1)} %pad_add_fusion.flags_ref, bf16[2,320,1280]{2,1,0:T(8,128)(2,1)} %hid_ref.1, f32[64,5120]{1,0:T(8,128)} %w_ref.2, f32[1,5120]{1,0:T(1,128)} %bitcast.18), custom_call_target="tpu_custom_call" | custom-call | tf_op jit(solution)/shard_map/project/pallas_call | solution.py:110
  3.3 0.5 %collective-permute-start = (bf16[16,48,128]{2,1,0:T(8,128)(2,1)S(1)}, bf16[16,48,128]{2,1,0:T(8,128)(2,1)S(1)}, u32[]{:S(2)}, u32[]{:S(2)}) collective-permute-start(bf16[16,48,128]{2,1,0:T(8,128)(2,1)S(1)} %get-tuple-element.26), channel_id=1, source_target_pairs={{0,1},{1,0},{2,3},{3,2},{4,5},{5,4},{6,7},{7,6},{8,9},{9,8},{10,11... | collective-permute-start | bytes 589832 | tf_op jit(solution)/shard_map/ppermute | solution.py:470
  3.9 0.0 copy-done.8
  3.9 0.0 copy-done.3
  3.9 0.0 copy-done.4
  3.9 0.1 copy.15.dev_ref
  4.0 0.9 %collective-permute-done = bf16[16,48,128]{2,1,0:T(8,128)(2,1)S(1)} collective-permute-done((bf16[16,48,128]{2,1,0:T(8,128)(2,1)S(1)}, bf16[16,48,128]{2,1,0:T(8,128)(2,1)S(1)}, u32[]{:S(2)}, u32[]{:S(2)}) %collective-permute-start) | collective-permute-done | bytes 196640 | tf_op jit(solution)/shard_map/ppermute | solution.py:470
  4.9 0.1 add_convert_fusion
  5.0 4.0 %collective-permute-start.1 = (bf16[6,48,128]{2,1,0:T(8,128)(2,1)S(1)}, bf16[6,48,128]{2,1,0:T(8,128)(2,1)S(1)}, u32[]{:S(2)}, u32[]{:S(2)}) collective-permute-start(bf16[6,48,128]{2,1,0:T(8,128)(2,1)S(1)} %get-tuple-element.47), channel_id=1, source_target_pairs={{0,8},{1,9},{2,10},{3,11},{4,12},{5,13},{6,14},{7,15},{8,0},{9,1},... | collective-permute-start | bytes 221192 | tf_op jit(solution)/shard_map/ppermute | solution.py:470
  9.1 1.3 %collective-permute-start.3 = (bf16[6,48,128]{2,1,0:T(8,128)(2,1)S(1)}, bf16[6,48,128]{2,1,0:T(8,128)(2,1)S(1)}, u32[]{:S(2)}, u32[]{:S(2)}) collective-permute-start(bf16[6,48,128]{2,1,0:T(8,128)(2,1)S(1)} %get-tuple-element.48), channel_id=1, source_target_pairs={{0,12},{1,13},{2,14},{3,15},{4,8},{5,9},{6,10},{7,11},{8,4},{9,5},... | collective-permute-start | bytes 221192 | tf_op jit(solution)/shard_map/ppermute | solution.py:470
  10.4 0.2 collective-permute-start.2
  10.6 0.0 copy-done.5
  10.6 0.0 copy-done.6
  10.6 0.0 copy-done
  10.7 0.0 copy-done.1
  10.7 0.0 copy-done.2
  10.7 0.0 copy-start.7
  10.7 5.2 %prepare.1 = (f32[16,128]{1,0:T(8,128)S(1)}, f32[1,128]{1,0:T(1,128)S(1)}, bf16[2,256,1536]{2,1,0:T(8,128)(2,1)S(1)}, bf16[768,1536]{1,0:T(8,128)(2,1)S(1)}, f32...) custom-call(f32[64,5120]{1,0:T(8,128)} %w_ref.2, f32[1,5120]{1,0:T(1,128)S(1)} %bitcast.19, f32[1,5120]{1,0:T(1,128)S(1)} %bitcast.20, ...), custom_call_target="tpu_custom_call" | custom-call | flops 20000000 | bytes 10000000 | tf_op jit(solution)/shard_map/prepare/pallas_call | solution.py:223
  15.9 0.0 collective-permute-done.1
  15.9 0.0 collective-permute-done.3
  15.9 0.3 collective-permute-done.2
  16.3 1.7 %collective-permute-start.4 = (bf16[4,72,128]{2,1,0:T(8,128)(2,1)S(1)}, bf16[4,72,128]{2,1,0:T(8,128)(2,1)S(1)}, u32[]{:S(2)}, u32[]{:S(2)}) collective-permute-start(bf16[4,72,128]{2,1,0:T(8,128)(2,1)S(1)} %constant_dynamic-slice_fusion.1), channel_id=1, source_target_pairs={{0,2},{1,3},{2,0},{3,1},{4,6},{5,7},{6,4},{7,5},{8,10},{9,11},{10,... | collective-permute-start | bytes 221192 | tf_op jit(solution)/shard_map/ppermute | solution.py:470
  18.0 2.7 %collective-permute-done.4 = bf16[4,72,128]{2,1,0:T(8,128)(2,1)S(1)} collective-permute-done((bf16[4,72,128]{2,1,0:T(8,128)(2,1)S(1)}, bf16[4,72,128]{2,1,0:T(8,128)(2,1)S(1)}, u32[]{:S(2)}, u32[]{:S(2)}) %collective-permute-start.4) | collective-permute-done | bytes 73760 | tf_op jit(solution)/shard_map/ppermute | solution.py:470
  20.8 0.1 collective-permute-start.5
  20.9 0.0 copy-done.7
  20.9 1.2 %collective-permute-done.5 = bf16[3,104,128]{2,1,0:T(8,128)(2,1)S(1)} collective-permute-done((bf16[3,104,128]{2,1,0:T(8,128)(2,1)S(1)}, bf16[3,104,128]{2,1,0:T(8,128)(2,1)S(1)}, u32[]{:S(2)}, u32[]{:S(2)}) %collective-permute-start.5) | collective-permute-done | bytes 79904 | tf_op jit(solution)/shard_map/ppermute | solution.py:470
  22.2 10.2 %decode.1 = bf16[2,4,96,320]{3,2,1,0:T(8,128)(2,1)} custom-call(s32[3]{0:T(128)S(1)} %pad_add_fusion.flags_ref, bf16[2,3,104,128]{3,2,1,0:T(8,128)(2,1)S(1)} %pad_maximum_fusion.sums_ref, f32[16,128]{1,0:T(8,128)S(1)} %get-tuple-element.39.table_ref, f32[1,128]{1,0:T(1,128)S(1)} %get-tuple-element.40.const_ref, ...), custom_call_target="tpu_custom_call" | custom-call | flops 5000000000 | bytes 8000000 | tf_op jit(solution)/shard_map/decode/pallas_call | solution.py:446
  (20 shorter events, 0.3 us)
Async XLA Ops:
  0.0 3.9 %copy-start.8 = (s32[16]{0:T(128)S(1)}, s32[16]{0:T(128)}, u32[]{:S(2)}) copy-start(s32[16]{0:T(128)} %constant.61.clone) | copy-start | bytes 196
  0.0 3.9 %copy-start.3 = (f32[384]{0:T(512)S(1)}, f32[384]{0:T(512)}, u32[]{:S(2)}) copy-start(f32[384]{0:T(512)} %param.20) | copy-start | bytes 4612
  0.0 3.9 %copy-start.4 = (f32[384]{0:T(512)S(1)}, f32[384]{0:T(512)}, u32[]{:S(2)}) copy-start(f32[384]{0:T(512)} %param.21) | copy-start | bytes 4612
  0.1 10.6 %copy-start.5 = (f32[192]{0:T(256)S(1)}, f32[192]{0:T(256)}, u32[]{:S(2)}) copy-start(f32[192]{0:T(256)} %param.24) | copy-start | bytes 2308
  0.1 10.6 %copy-start.6 = (f32[192]{0:T(256)S(1)}, f32[192]{0:T(256)}, u32[]{:S(2)}) copy-start(f32[192]{0:T(256)} %param.23) | copy-start | bytes 2308
  0.1 10.6 %copy-start = (f32[5120]{0:T(1024)S(1)}, f32[5120]{0:T(1024)}, u32[]{:S(2)}) copy-start(f32[5120]{0:T(1024)} %param.16) | copy-start | bytes 61444
  0.1 10.6 %copy-start.1 = (f32[5120]{0:T(1024)S(1)}, f32[5120]{0:T(1024)}, u32[]{:S(2)}) copy-start(f32[5120]{0:T(1024)} %param.15) | copy-start | bytes 61444
  0.1 10.6 %copy-start.2 = (f32[64]{0:T(128)S(1)}, f32[64]{0:T(128)}, u32[]{:S(2)}) copy-start(f32[64]{0:T(128)} %param.18) | copy-start | bytes 772
  3.3 1.6 %collective-permute-start = (bf16[16,48,128]{2,1,0:T(8,128)(2,1)S(1)}, bf16[16,48,128]{2,1,0:T(8,128)(2,1)S(1)}, u32[]{:S(2)}, u32[]{:S(2)}) collective-permute-start(bf16[16,48,128]{2,1,0:T(8,128)(2,1)S(1)} %get-tuple-element.26), channel_id=1, source_target_pairs={{0,1},{1,0},{2,3},{3,2},{4,5},{5,4},{6,7},{7,6},{8,9},{9,8},{10,11... | collective-permute-start | bytes 589832 | tf_op jit(solution)/shard_map/ppermute | solution.py:470
  5.0 10.8 %collective-permute-start.1 = (bf16[6,48,128]{2,1,0:T(8,128)(2,1)S(1)}, bf16[6,48,128]{2,1,0:T(8,128)(2,1)S(1)}, u32[]{:S(2)}, u32[]{:S(2)}) collective-permute-start(bf16[6,48,128]{2,1,0:T(8,128)(2,1)S(1)} %get-tuple-element.47), channel_id=1, source_target_pairs={{0,8},{1,9},{2,10},{3,11},{4,12},{5,13},{6,14},{7,15},{8,0},{9,1},... | collective-permute-start | bytes 221192 | tf_op jit(solution)/shard_map/ppermute | solution.py:470
  9.1 6.8 %collective-permute-start.3 = (bf16[6,48,128]{2,1,0:T(8,128)(2,1)S(1)}, bf16[6,48,128]{2,1,0:T(8,128)(2,1)S(1)}, u32[]{:S(2)}, u32[]{:S(2)}) collective-permute-start(bf16[6,48,128]{2,1,0:T(8,128)(2,1)S(1)} %get-tuple-element.48), channel_id=1, source_target_pairs={{0,12},{1,13},{2,14},{3,15},{4,8},{5,9},{6,10},{7,11},{8,4},{9,5},... | collective-permute-start | bytes 221192 | tf_op jit(solution)/shard_map/ppermute | solution.py:470
  10.4 5.8 %collective-permute-start.2 = (bf16[6,48,128]{2,1,0:T(8,128)(2,1)S(1)}, bf16[6,48,128]{2,1,0:T(8,128)(2,1)S(1)}, u32[]{:S(2)}, u32[]{:S(2)}) collective-permute-start(bf16[6,48,128]{2,1,0:T(8,128)(2,1)S(1)} %get-tuple-element.49), channel_id=1, source_target_pairs={{0,4},{1,5},{2,6},{3,7},{4,0},{5,1},{6,2},{7,3},{8,12},{9,13},{10,... | collective-permute-start | bytes 221192 | tf_op jit(solution)/shard_map/ppermute | solution.py:470
  10.7 10.2 %copy-start.7 = (f32[96]{0:T(128)S(1)}, f32[96]{0:T(128)}, u32[]{:S(2)}) copy-start(f32[96]{0:T(128)} %param.26) | copy-start | bytes 1156
  16.3 4.4 %collective-permute-start.4 = (bf16[4,72,128]{2,1,0:T(8,128)(2,1)S(1)}, bf16[4,72,128]{2,1,0:T(8,128)(2,1)S(1)}, u32[]{:S(2)}, u32[]{:S(2)}) collective-permute-start(bf16[4,72,128]{2,1,0:T(8,128)(2,1)S(1)} %constant_dynamic-slice_fusion.1), channel_id=1, source_target_pairs={{0,2},{1,3},{2,0},{3,1},{4,6},{5,7},{6,4},{7,5},{8,10},{9,11},{10,... | collective-permute-start | bytes 221192 | tf_op jit(solution)/shard_map/ppermute | solution.py:470
  20.8 1.3 %collective-permute-start.5 = (bf16[3,104,128]{2,1,0:T(8,128)(2,1)S(1)}, bf16[3,104,128]{2,1,0:T(8,128)(2,1)S(1)}, u32[]{:S(2)}, u32[]{:S(2)}) collective-permute-start(bf16[3,104,128]{2,1,0:T(8,128)(2,1)S(1)} %constant_dynamic-slice_fusion), channel_id=1, source_target_pairs={{0,1},{1,0},{2,3},{3,2},{4,5},{5,4},{6,7},{7,6},{8,9},{9,8},{10,11... | collective-permute-start | bytes 239624 | tf_op jit(solution)/shard_map/ppermute | solution.py:470

commit v3 on v2

--- a/solution.py
+++ b/solution.py
@@ -254,49 +254,72 @@
 
 
 def decode_kernel(
-    group, flags_ref, sums_ref, table_ref, const_ref, cin_ref, cinv_ref, up_ref, upv_ref, cout_ref,
-    coutv_ref, out_ref, fa, fb, fx, ua, ub, xe, xo, lines,
+    group, flags_ref, own_ref, near_ref, core_ref, far_ref, table_ref, const_ref, cin_ref, cinv_ref, up_ref, upv_ref, cout_ref,
+    coutv_ref, out_ref, fa, fb, fx, ua, ub, xe, xo, lines, outs, sems,
 ):
     count = table_ref.shape[0]
     has_low = flags_ref[1]
     has_high = flags_ref[2]
-    n_stat = sums_ref.shape[2] - HALF
+    n_stat = 2 * (own_ref.shape[1] - HALF)
+    first_half = (flags_ref[0] & 1) == 0
 
     pick_row = lax.broadcasted_iota(jnp.int32, (count + 8, n_stat), 0)
     pick_col = lax.broadcasted_iota(jnp.int32, (count + 8, n_stat), 1)
     of_dev, of_kind = pick_col // STAT, pick_col % STAT
     pick = ((of_kind < 2) & (pick_row == of_dev)) | ((of_kind >= 2) & (pick_row == count))
     pick = pick.astype(F32).astype(BF)
-    lane40, sub40 = lanes(HALF), lax.broadcasted_iota(jnp.int32, (HALF, 128), 0)
+    lane40 = lanes(HALF)
     lane80, sub80 = lanes(TOK_W), lax.broadcasted_iota(jnp.int32, (TOK_W, 128), 0)
-    spread_mask = (lane40 % 64) == sub40
-    ones_block = (
-        (lax.broadcasted_iota(jnp.int32, (128, 128), 0) // 64) == (lanes(128) // 64)
-    ).astype(F32)
+    wide = []
+    for j in range(3):
+        mine, other = [
+            jnp.concatenate([a[j, HALF:], b[j, HALF:]], axis=0)
+            for a, b in ((own_ref, near_ref), (core_ref, far_ref))
+        ]
+        wide += [jnp.where(first_half, mine, other), jnp.where(first_half, other, mine)]
+    wide = jnp.concatenate(wide, axis=1)
+    stats = jnp.dot(pick, wide, preferred_element_type=F32)
+    means = stats[0:count]
+    off = means - jnp.sum(means, axis=0, keepdims=True) * (1.0 / count)
+    var = stats[count : count + 1] + group * jnp.sum(off * off, axis=0, keepdims=True)
+    inv = lax.rsqrt(var * (1.0 / (count * group)) + EPS)
+    off_hi, off_lo = split(off)
+    inv_hi, inv_lo = split(inv)
+    left = jnp.concatenate(
+        [off_hi, off_lo, off_hi, inv_hi, inv_lo, jnp.zeros((14, off.shape[1]), F32)], axis=0
+    )
+    tab_hi, tab_lo = split(table_ref[...])
+    right = jnp.concatenate(
+        [
+            jnp.concatenate([tab_hi, tab_hi, tab_lo, jnp.zeros((16, 128), F32)], axis=0),
+            jnp.concatenate(
+                [
+                    jnp.zeros((3 * count, 128), F32),
+                    jnp.ones((2, 128), F32),
+                    jnp.zeros((14, 128), F32),
+                ],
+                axis=0,
+            ),
+        ],
+        axis=1,
+    )
+    per_token = jnp.dot(left.T.astype(BF), right.astype(BF), preferred_element_type=F32)
     edge = [[None] * 3 for _ in range(2)]
     for j in range(3):
         halves = []
+        mine, other = [
+            a[j, 0:HALF].astype(F32) + b[j, 0:HALF].astype(F32)
+            for a, b in ((own_ref, near_ref), (core_ref, far_ref))
+        ]
+        sums = [jnp.where(first_half, mine, other), jnp.where(first_half, other, mine)]
         for h in range(2):
-            block = sums_ref[h, j]
-            stats = jnp.dot(pick, block[HALF:], preferred_element_type=F32)
-            means = stats[0:count]
-            mean = jnp.sum(means, axis=0, keepdims=True) * (1.0 / count)
-            off = means - mean
-            feats_all = count * group
-            var = (
-                stats[count : count + 1] + group * jnp.sum(off * off, axis=0, keepdims=True)
-            ) / feats_all
-            inv = lax.rsqrt(var + EPS)
-            shift = lax.dot_general(
-                off, table_ref[...], (((0,), (0,)), ((), ())),
-                precision=HIGH, preferred_element_type=F32,
+            at = (j * 2 + h) * 128
+            both = jnp.concatenate([lane40, lane40], axis=1) % 128 < 64
+            token = jnp.where(both, per_token[at : at + HALF], per_token[at + 64 : at + 64 + HALF])
+            halves.append(
+                (sums[h] + token[:, 0:128]) * token[:, 128:256]
+                + const_ref[...]
             )
-            shift = jnp.where(lane40 < 64, shift[0:HALF], shift[64 : 64 + HALF])
-            inv_all = jnp.dot(
-                jnp.where(spread_mask, inv, 0.0), ones_block,
-                precision=HIGH, preferred_element_type=F32,
-            )
-            halves.append((block[0:HALF].astype(F32) + shift) * inv_all + const_ref[...])
         row = jnp.concatenate(halves, axis=0)
         if j == 0:
             row = jnp.where(has_low > 0, row, 0.0)
@@ -363,12 +386,13 @@
         return lax.dot_general(x, up_ref[...], dims, preferred_element_type=F32)
 
     ua[...] = times_up(fa[...])
-    ub[0 : 6 * TOK_W] = times_up(fb[...])
     extra_in = jnp.where(
         lax.broadcasted_iota(jnp.int32, (8, 1536), 0) < 6, fx[...], 0.0
     )
     extra_in = jnp.concatenate([extra_in, jnp.zeros((8, 1536), F32)], axis=0).astype(BF)
-    extra = times_up(extra_in)[0:8]
+    fb[6 * TOK_W :] = extra_in
+    ub[...] = times_up(fb[...])
+    extra = ub[6 * TOK_W : 6 * TOK_W + 8]
     bias_up, gain_up = upv_ref[0:1], upv_ref[1:2] * 0.5
 
     def second(u):
@@ -422,6 +446,7 @@
                     xo[f, to, 384 + k * 128 : 512 + k * 128] = ahead.astype(BF)
 
     bias_out = coutv_ref[...]
+    copies = []
     for f in range(2):
         for side, x in enumerate((xe, xo)):
             acc = None
@@ -434,36 +459,43 @@
                     acc = acc + jnp.dot(x[0, rows], cout_ref[0, ks], preferred_element_type=F32)
             for j in range(4):
                 for o in range(2):
-                    lines[j, pl.ds(2 * side + o, TOK_W, stride=4), :] = (
+                    lines[f, j, pl.ds(2 * side + o, TOK_W, stride=4), :] = (
                         acc[j * TOK_W : (j + 1) * TOK_W, o * 128 : o * 128 + 128] + bias_out
                     )
         for j in range(4):
-            out_ref[f, j] = lines[j].T[0:96].astype(BF)
-
-
-def decode(group, flags, sums, table, const, cin, cinv, up, upv, cout, coutv):
+            outs[f, j] = lines[f, j].T[0:96].astype(BF)
+        copy = pltpu.make_async_copy(outs.at[f], out_ref.at[f], sems.at[f])
+        copy.start()
+        copies.append(copy)
+    for copy in copies:
+        copy.wait()
+
+
+def decode(group, flags, pieces, table, const, cin, cinv, up, upv, cout, coutv):
     vmem = pl.BlockSpec(memory_space=pltpu.VMEM)
     return pl.pallas_call(
         functools.partial(decode_kernel, float(group)),
-        in_specs=[pl.BlockSpec(memory_space=pltpu.SMEM)] + [vmem] * 9,
-        out_specs=vmem,
+        in_specs=[pl.BlockSpec(memory_space=pltpu.SMEM)] + [vmem] * 12,
+        out_specs=pl.BlockSpec(memory_space=pltpu.HBM),
         out_shape=jax.ShapeDtypeStruct((2, 4, 96, 4 * TOK_W), BF),
         scratch_shapes=[
             pltpu.VMEM((6 * TOK_W, 1536), BF),
-            pltpu.VMEM((6 * TOK_W, 1536), BF),
+            pltpu.VMEM((6 * TOK_W + 16, 1536), BF),
             pltpu.VMEM((8, 1536), F32),
             pltpu.VMEM((6 * TOK_W, 768), F32),
-            pltpu.VMEM((6 * TOK_W, 768), F32),
+            pltpu.VMEM((6 * TOK_W + 16, 768), F32),
             pltpu.VMEM((2, 6 * TOK_W, 768), BF),
             pltpu.VMEM((2, 6 * TOK_W, 768), BF),
-            pltpu.VMEM((4, 4 * TOK_W, 128), F32),
+            pltpu.VMEM((2, 4, 4 * TOK_W, 128), F32),
+            pltpu.VMEM((2, 4, 96, 4 * TOK_W), BF),
+            pltpu.SemaphoreType.DMA((2,)),
         ],
         compiler_params=pltpu.CompilerParams(vmem_limit_bytes=24 << 20),
         cost_estimate=pl.CostEstimate(
             flops=5_000_000_000, bytes_accessed=8_000_000, transcendentals=1_300_000
         ),
         name="decode",
-    )(flags, sums, table, const, cin, cinv, up, upv, cout, coutv)
+    )(flags, *pieces, table, const, cin, cinv, up, upv, cout, coutv)
 
 
 def exchange(block, mask, count):
@@ -486,7 +518,7 @@
 def steps_of(count):
     bit = count.bit_length() - 3
     steps = [[2 << bit, 1 << bit, 3 << bit]]
-    while bit > 1:
+    while bit > 2:
         bit -= 1
         steps.append([1 << bit])
     return steps
@@ -496,11 +528,11 @@
     order = [0]
     for masks in steps_of(count):
         order = order + [o ^ mask for mask in masks for o in order]
+    order = order + [o ^ 2 for o in order]
     return np.asarray([o + c for o in order for c in range(2)], np.int32)
 
 
 def gather_rows(own, give, weights, ready, me, count):
-    core = me & 1
     block = (own.astype(F32) + exchange(give, 1, count).astype(F32)).astype(BF)
     block, weights = lax.optimization_barrier((block, weights))
 
@@ -522,11 +554,10 @@
             block, weights = lax.optimization_barrier((block, ready(weights)))
         start = new
     padded = jnp.pad(block, ((1, 1), (0, 0), (0, 0)))
-    mine = cut(padded, me - start, 3)
-    other = exchange(cut(padded, (me ^ 1) - start, 3), 1, count)
-    low = jnp.where(core == 0, mine, other)
-    high = jnp.where(core == 0, other, mine)
-    return jnp.stack([low, high]), weights
+    pieces = [cut(padded, me - start, 3)]
+    for mask in (2, 1, 3):
+        pieces.append(exchange(cut(padded, (me ^ mask) - start, 3), mask, count))
+    return pieces, weights
 
 
 def local(
@@ -559,11 +590,11 @@
             cin, up, jnp.stack([up_bias, gain_up]), cout,
         )
 
-    sums, weights = gather_rows(own, give, weights, ready, me, count)
+    pieces, weights = gather_rows(own, give, weights, ready, me, count)
     table, const, cin, up, upv, cout = weights
     cinv = jnp.stack([conv_in_bias, gain_in])
     coutv = jnp.pad(out_bias, (0, 32))[None]
-    out = decode(feats, flags, sums, table, const, cin, cinv, up, upv, cout, coutv)
+    out = decode(feats, flags, pieces, table, const, cin, cinv, up, upv, cout, coutv)
     return jnp.swapaxes(out, 2, 3)
 
 

time: 32.6 us -> 30.4 us (0.933)
  Pallas kernels: 18.6 us -> 17 us
  waiting for transfers between devices: 5.21 us -> 4.56 us
    pallas_call x1, Pallas kernels: 10.2 us -> 8.65 us  [decode(): pl.pallas_call(functools.partial(decode_kernel, float(group)), in_specs=[...]
    ppermute x6 -> x7, waiting for transfers between devices: 5.21 us -> 4.56 us  [exchange(): return lax.ppermute(block, 'seq', [(i, i ^ mask) for i in range(count)])]
    ppermute x6 -> x7, starting transfers between devices: 7.89 us -> 8.06 us  [exchange(): return lax.ppermute(block, 'seq', [(i, i ^ mask) for i in range(count)])]
  transfers between devices with their start and end apart: 6 -> 7, of which waited for: 4 -> 4; matrix products, arithmetic and copies ran while one was open for 0% -> 0% of each run, Pallas kernels for 16% -> 17%
where the time goes in v3:
time: 30.4 us; the launch traced here: 30.2 us
  Pallas kernels  17 us (56%)
  starting transfers between devices  8.06 us (27%)
  waiting for transfers between devices  4.56 us (15%)
    pallas_call x1, Pallas kernels, decode(): pl.pallas_call(functools.partial(decode_kernel, float(group)), in_specs=[...  8.65 us
    ppermute x7, starting transfers between devices, exchange(): return lax.ppermute(block, 'seq', [(i, i ^ mask) for i in range(count)])  8.06 us
    pallas_call x1, Pallas kernels, prepare(): pl.pallas_call(prepare_kernel, in_specs=[hbm, vmem, vmem, vmem, vmem, hbm...  5.15 us
    ppermute x7, waiting for transfers between devices, exchange(): return lax.ppermute(block, 'seq', [(i, i ^ mask) for i in range(count)])  4.56 us
    pallas_call x1, Pallas kernels, project(): pl.pallas_call(project_kernel, in_specs=[pl.BlockSpec(memory_space=pltpu....  3.22 us
  transfers between devices with their start and end apart: 7, of which 4 were waited for; matrix products, arithmetic and copies ran while one was open for 0% of the time, Pallas kernels for 17%

profile of v3, /device:TPU:0, one launch (start us, length us, event | category | flops | bytes accessed | tf_op | source)
XLA Modules:
  0.0 30.2 jit_solution(5770293038817228417)
XLA Ops:
  0.0 0.0 copy-start.8
  0.0 0.0 copy-start.3
  0.0 0.0 copy-start.4
  0.0 0.1 pad_add_fusion.flags_ref
  0.1 0.0 copy-start.5
  0.1 0.0 copy-start.6
  0.1 0.0 copy-start
  0.1 0.0 copy-start.1
  0.1 0.0 copy-start.2
  0.1 3.2 %project.1 = (bf16[16,48,128]{2,1,0:T(8,128)(2,1)S(1)}, bf16[16,48,128]{2,1,0:T(8,128)(2,1)S(1)}) custom-call(s32[3]{0:T(128)S(1)} %pad_add_fusion.flags_ref, bf16[2,320,1280]{2,1,0:T(8,128)(2,1)} %hid_ref.1, f32[64,5120]{1,0:T(8,128)} %w_ref.2, f32[1,5120]{1,0:T(1,128)} %bitcast.14), custom_call_target="tpu_custom_call" | custom-call | tf_op jit(solution)/shard_map/project/pallas_call | solution.py:110
  3.3 0.5 %collective-permute-start = (bf16[16,48,128]{2,1,0:T(8,128)(2,1)S(1)}, bf16[16,48,128]{2,1,0:T(8,128)(2,1)S(1)}, u32[]{:S(2)}, u32[]{:S(2)}) collective-permute-start(bf16[16,48,128]{2,1,0:T(8,128)(2,1)S(1)} %get-tuple-element.26), channel_id=1, source_target_pairs={{0,1},{1,0},{2,3},{3,2},{4,5},{5,4},{6,7},{7,6},{8,9},{9,8},{10,11... | collective-permute-start | bytes 589832 | tf_op jit(solution)/shard_map/ppermute | solution.py:502
  3.9 0.0 copy-done.8
  3.9 0.0 copy-done.3
  3.9 0.0 copy-done.4
  3.9 0.1 copy.15.dev_ref
  4.0 0.9 %collective-permute-done = bf16[16,48,128]{2,1,0:T(8,128)(2,1)S(1)} collective-permute-done((bf16[16,48,128]{2,1,0:T(8,128)(2,1)S(1)}, bf16[16,48,128]{2,1,0:T(8,128)(2,1)S(1)}, u32[]{:S(2)}, u32[]{:S(2)}) %collective-permute-start) | collective-permute-done | bytes 196640 | tf_op jit(solution)/shard_map/ppermute | solution.py:502
  4.9 0.1 add_convert_fusion
  5.0 4.0 %collective-permute-start.1 = (bf16[6,48,128]{2,1,0:T(8,128)(2,1)S(1)}, bf16[6,48,128]{2,1,0:T(8,128)(2,1)S(1)}, u32[]{:S(2)}, u32[]{:S(2)}) collective-permute-start(bf16[6,48,128]{2,1,0:T(8,128)(2,1)S(1)} %get-tuple-element.45), channel_id=1, source_target_pairs={{0,8},{1,9},{2,10},{3,11},{4,12},{5,13},{6,14},{7,15},{8,0},{9,1},... | collective-permute-start | bytes 221192 | tf_op jit(solution)/shard_map/ppermute | solution.py:502
  9.1 1.3 %collective-permute-start.3 = (bf16[6,48,128]{2,1,0:T(8,128)(2,1)S(1)}, bf16[6,48,128]{2,1,0:T(8,128)(2,1)S(1)}, u32[]{:S(2)}, u32[]{:S(2)}) collective-permute-start(bf16[6,48,128]{2,1,0:T(8,128)(2,1)S(1)} %get-tuple-element.46), channel_id=1, source_target_pairs={{0,12},{1,13},{2,14},{3,15},{4,8},{5,9},{6,10},{7,11},{8,4},{9,5},... | collective-permute-start | bytes 221192 | tf_op jit(solution)/shard_map/ppermute | solution.py:502
  10.4 0.2 collective-permute-start.2
  10.6 0.0 copy-done.5
  10.6 0.0 copy-done.6
  10.6 0.0 copy-done
  10.7 0.0 copy-done.1
  10.7 0.0 copy-done.2
  10.7 0.0 copy-start.7
  10.7 5.1 %prepare.1 = (f32[16,128]{1,0:T(8,128)S(1)}, f32[1,128]{1,0:T(1,128)S(1)}, bf16[2,256,1536]{2,1,0:T(8,128)(2,1)S(1)}, bf16[768,1536]{1,0:T(8,128)(2,1)S(1)}, f32...) custom-call(f32[64,5120]{1,0:T(8,128)} %w_ref.2, f32[1,5120]{1,0:T(1,128)S(1)} %bitcast.15, f32[1,5120]{1,0:T(1,128)S(1)} %bitcast.16, ...), custom_call_target="tpu_custom_call" | custom-call | flops 20000000 | bytes 10000000 | tf_op jit(solution)/shard_map/prepare/pallas_call | solution.py:223
  15.8 0.0 collective-permute-done.1
  15.9 0.0 collective-permute-done.3
  15.9 0.3 %collective-permute-done.2 = bf16[6,48,128]{2,1,0:T(8,128)(2,1)S(1)} collective-permute-done((bf16[6,48,128]{2,1,0:T(8,128)(2,1)S(1)}, bf16[6,48,128]{2,1,0:T(8,128)(2,1)S(1)}, u32[]{:S(2)}, u32[]{:S(2)}) %collective-permute-start.2) | collective-permute-done | bytes 73760 | tf_op jit(solution)/shard_map/ppermute | solution.py:502
  16.3 0.1 pad_dynamic-slice_fusion
  16.4 0.5 %collective-permute-start.6 = (bf16[3,72,128]{2,1,0:T(8,128)(2,1)S(1)}, bf16[3,72,128]{2,1,0:T(8,128)(2,1)S(1)}, u32[]{:S(2)}, u32[]{:S(2)}) collective-permute-start(bf16[3,72,128]{2,1,0:T(8,128)(2,1)S(1)} %get-tuple-element.48), channel_id=1, source_target_pairs={{0,3},{1,2},{2,1},{3,0},{4,7},{5,6},{6,5},{7,4},{8,11},{9,10},{10,... | collective-permute-start | bytes 165896 | tf_op jit(solution)/shard_map/ppermute | solution.py:502
  16.8 1.3 %collective-permute-start.4 = (bf16[3,72,128]{2,1,0:T(8,128)(2,1)S(1)}, bf16[3,72,128]{2,1,0:T(8,128)(2,1)S(1)}, u32[]{:S(2)}, u32[]{:S(2)}) collective-permute-start(bf16[3,72,128]{2,1,0:T(8,128)(2,1)S(1)} %get-tuple-element.49), channel_id=1, source_target_pairs={{0,2},{1,3},{2,0},{3,1},{4,6},{5,7},{6,4},{7,5},{8,10},{9,11},{10,... | collective-permute-start | bytes 165896 | tf_op jit(solution)/shard_map/ppermute | solution.py:502
  18.1 0.2 collective-permute-start.5
  18.3 0.0 copy-done.7
  18.3 2.1 %collective-permute-done.6.far_ref = bf16[3,72,128]{2,1,0:T(8,128)(2,1)S(1)} collective-permute-done((bf16[3,72,128]{2,1,0:T(8,128)(2,1)S(1)}, bf16[3,72,128]{2,1,0:T(8,128)(2,1)S(1)}, u32[]{:S(2)}, u32[]{:S(2)}) %collective-permute-start.6) | collective-permute-done | bytes 55328 | tf_op jit(solution)/shard_map/ppermute | solution.py:502
  20.4 1.2 %collective-permute-done.4.near_ref = bf16[3,72,128]{2,1,0:T(8,128)(2,1)S(1)} collective-permute-done((bf16[3,72,128]{2,1,0:T(8,128)(2,1)S(1)}, bf16[3,72,128]{2,1,0:T(8,128)(2,1)S(1)}, u32[]{:S(2)}, u32[]{:S(2)}) %collective-permute-start.4) | collective-permute-done | bytes 55328 | tf_op jit(solution)/shard_map/ppermute | solution.py:502
  21.6 0.0 collective-permute-done.5.core_ref
  21.6 8.6 %decode.1 = bf16[2,4,96,320]{3,2,1,0:T(8,128)(2,1)} custom-call(s32[3]{0:T(128)S(1)} %pad_add_fusion.flags_ref, bf16[3,72,128]{2,1,0:T(8,128)(2,1)S(1)} %get-tuple-element.51.own_ref, bf16[3,72,128]{2,1,0:T(8,128)(2,1)S(1)} %collective-permute-done.4.near_ref, bf16[3,72,128]{2,1,0:T(8,128)(2,1)S(1)} %collective-permute-done.5.core_ref, ...), custom_call_target="tpu_custom_call" | custom-call | flops 5000000000 | bytes 8000000 | tf_op jit(solution)/shard_map/decode/pallas_call | solution.py:476
  (12 shorter events, 0.1 us)
Async XLA Ops:
  0.0 3.9 %copy-start.8 = (s32[16]{0:T(128)S(1)}, s32[16]{0:T(128)}, u32[]{:S(2)}) copy-start(s32[16]{0:T(128)} %constant.56.clone) | copy-start | bytes 196
  0.0 3.9 %copy-start.3 = (f32[384]{0:T(512)S(1)}, f32[384]{0:T(512)}, u32[]{:S(2)}) copy-start(f32[384]{0:T(512)} %param.20) | copy-start | bytes 4612
  0.0 3.9 %copy-start.4 = (f32[384]{0:T(512)S(1)}, f32[384]{0:T(512)}, u32[]{:S(2)}) copy-start(f32[384]{0:T(512)} %param.21) | copy-start | bytes 4612
  0.1 10.6 %copy-start.5 = (f32[192]{0:T(256)S(1)}, f32[192]{0:T(256)}, u32[]{:S(2)}) copy-start(f32[192]{0:T(256)} %param.24) | copy-start | bytes 2308
  0.1 10.6 %copy-start.6 = (f32[192]{0:T(256)S(1)}, f32[192]{0:T(256)}, u32[]{:S(2)}) copy-start(f32[192]{0:T(256)} %param.23) | copy-start | bytes 2308
  0.1 10.6 %copy-start = (f32[5120]{0:T(1024)S(1)}, f32[5120]{0:T(1024)}, u32[]{:S(2)}) copy-start(f32[5120]{0:T(1024)} %param.16) | copy-start | bytes 61444
  0.1 10.6 %copy-start.1 = (f32[5120]{0:T(1024)S(1)}, f32[5120]{0:T(1024)}, u32[]{:S(2)}) copy-start(f32[5120]{0:T(1024)} %param.15) | copy-start | bytes 61444
  0.1 10.6 %copy-start.2 = (f32[64]{0:T(128)S(1)}, f32[64]{0:T(128)}, u32[]{:S(2)}) copy-start(f32[64]{0:T(128)} %param.18) | copy-start | bytes 772
  3.3 1.6 %collective-permute-start = (bf16[16,48,128]{2,1,0:T(8,128)(2,1)S(1)}, bf16[16,48,128]{2,1,0:T(8,128)(2,1)S(1)}, u32[]{:S(2)}, u32[]{:S(2)}) collective-permute-start(bf16[16,48,128]{2,1,0:T(8,128)(2,1)S(1)} %get-tuple-element.26), channel_id=1, source_target_pairs={{0,1},{1,0},{2,3},{3,2},{4,5},{5,4},{6,7},{7,6},{8,9},{9,8},{10,11... | collective-permute-start | bytes 589832 | tf_op jit(solution)/shard_map/ppermute | solution.py:502
  5.0 10.8 %collective-permute-start.1 = (bf16[6,48,128]{2,1,0:T(8,128)(2,1)S(1)}, bf16[6,48,128]{2,1,0:T(8,128)(2,1)S(1)}, u32[]{:S(2)}, u32[]{:S(2)}) collective-permute-start(bf16[6,48,128]{2,1,0:T(8,128)(2,1)S(1)} %get-tuple-element.45), channel_id=1, source_target_pairs={{0,8},{1,9},{2,10},{3,11},{4,12},{5,13},{6,14},{7,15},{8,0},{9,1},... | collective-permute-start | bytes 221192 | tf_op jit(solution)/shard_map/ppermute | solution.py:502
  9.1 6.8 %collective-permute-start.3 = (bf16[6,48,128]{2,1,0:T(8,128)(2,1)S(1)}, bf16[6,48,128]{2,1,0:T(8,128)(2,1)S(1)}, u32[]{:S(2)}, u32[]{:S(2)}) collective-permute-start(bf16[6,48,128]{2,1,0:T(8,128)(2,1)S(1)} %get-tuple-element.46), channel_id=1, source_target_pairs={{0,12},{1,13},{2,14},{3,15},{4,8},{5,9},{6,10},{7,11},{8,4},{9,5},... | collective-permute-start | bytes 221192 | tf_op jit(solution)/shard_map/ppermute | solution.py:502
  10.4 5.8 %collective-permute-start.2 = (bf16[6,48,128]{2,1,0:T(8,128)(2,1)S(1)}, bf16[6,48,128]{2,1,0:T(8,128)(2,1)S(1)}, u32[]{:S(2)}, u32[]{:S(2)}) collective-permute-start(bf16[6,48,128]{2,1,0:T(8,128)(2,1)S(1)} %get-tuple-element.47), channel_id=1, source_target_pairs={{0,4},{1,5},{2,6},{3,7},{4,0},{5,1},{6,2},{7,3},{8,12},{9,13},{10,... | collective-permute-start | bytes 221192 | tf_op jit(solution)/shard_map/ppermute | solution.py:502
  10.7 7.6 %copy-start.7 = (f32[96]{0:T(128)S(1)}, f32[96]{0:T(128)}, u32[]{:S(2)}) copy-start(f32[96]{0:T(128)} %param.26) | copy-start | bytes 1156
  16.4 4.1 %collective-permute-start.6 = (bf16[3,72,128]{2,1,0:T(8,128)(2,1)S(1)}, bf16[3,72,128]{2,1,0:T(8,128)(2,1)S(1)}, u32[]{:S(2)}, u32[]{:S(2)}) collective-permute-start(bf16[3,72,128]{2,1,0:T(8,128)(2,1)S(1)} %get-tuple-element.48), channel_id=1, source_target_pairs={{0,3},{1,2},{2,1},{3,0},{4,7},{5,6},{6,5},{7,4},{8,11},{9,10},{10,... | collective-permute-start | bytes 165896 | tf_op jit(solution)/shard_map/ppermute | solution.py:502
  16.8 4.8 %collective-permute-start.4 = (bf16[3,72,128]{2,1,0:T(8,128)(2,1)S(1)}, bf16[3,72,128]{2,1,0:T(8,128)(2,1)S(1)}, u32[]{:S(2)}, u32[]{:S(2)}) collective-permute-start(bf16[3,72,128]{2,1,0:T(8,128)(2,1)S(1)} %get-tuple-element.49), channel_id=1, source_target_pairs={{0,2},{1,3},{2,0},{3,1},{4,6},{5,7},{6,4},{7,5},{8,10},{9,11},{10,... | collective-permute-start | bytes 165896 | tf_op jit(solution)/shard_map/ppermute | solution.py:502
  18.1 3.5 %collective-permute-start.5 = (bf16[3,72,128]{2,1,0:T(8,128)(2,1)S(1)}, bf16[3,72,128]{2,1,0:T(8,128)(2,1)S(1)}, u32[]{:S(2)}, u32[]{:S(2)}) collective-permute-start(bf16[3,72,128]{2,1,0:T(8,128)(2,1)S(1)} %get-tuple-element.50), channel_id=1, source_target_pairs={{0,1},{1,0},{2,3},{3,2},{4,5},{5,4},{6,7},{7,6},{8,9},{9,8},{10,11... | collective-permute-start | bytes 165896 | tf_op jit(solution)/shard_map/ppermute | solution.py:502

commit v4 on v3

--- a/solution.py
+++ b/solution.py
@@ -29,10 +29,53 @@
     return lax.broadcasted_iota(jnp.int32, (rows, 128), 1)
 
 
-def project_kernel(flags_ref, hid_ref, w_ref, scale_ref, own_ref, give_ref, hid, w, scale, sems):
-    frames, feats, tokens = hid_ref.shape
-    width = hid.shape[3]
-    me = flags_ref[0]
+def frame_sums(x, stack, gain_sum, core, out_ref):
+    feats, tokens = x.shape
+    width = 640
+    lane40 = lanes(HALF)
+    lane = lanes(8)
+    sub = lax.broadcasted_iota(jnp.int32, (8, 128), 0)
+    for i in range(tokens // width):
+        block = x[:, i * width : (i + 1) * width]
+        prod = jnp.dot(stack, block, preferred_element_type=F32)
+        mean = prod[128:129] * (1.0 / feats)
+        part = prod[0:64] + prod[64:128] - gain_sum * mean
+        off = block.astype(F32) - mean
+        second = jnp.sum(off * off, axis=0, keepdims=True)
+        m_hi, m_lo = split(mean)
+        s_hi, s_lo = split(second)
+        stats = jnp.concatenate([m_hi, m_lo, s_hi, s_lo] * 2, axis=0)
+        flat = jnp.concatenate([part, part], axis=0).T
+        for row in range(width // TOK_W):
+            first = row * TOK_W
+            sums = jnp.where(
+                lane40 < 64, flat[first : first + HALF], flat[first + HALF : first + TOK_W]
+            )
+            picks = []
+            for h in range(2):
+                at = first + h * HALF
+                base = (at // 128) * 128
+                span = min(256, width - base)
+                window = stats[:, base : base + span]
+                shift = (64 * h - (at - base)) % span
+                if shift:
+                    window = pltpu.roll(window, shift, 1)
+                picks.append(window[:, :128])
+            tail = jnp.where(
+                lane < HALF,
+                picks[0],
+                jnp.where((lane >= 64) & (lane < 64 + HALF), picks[1], 0.0),
+            )
+            tail = jnp.where(lax.div(sub, STAT) == core, tail, 0.0)
+            out_ref[i * (width // TOK_W) + row] = jnp.concatenate([sums, tail], axis=0).astype(BF)
+
+
+def project_give_kernel(
+    hid_ref, w_ref, scale_ref, give_ref, own_ref, stack_ref, gsum_ref,
+    hid, w, scale, sems,
+):
+    feats = hid_ref.shape[1]
+    me = lax.axis_index("seq")
     core = me & 1
     wide = w.shape[1]
     at = jnp.minimum(lax.div(me * feats, 128) * 128, w_ref.shape[1] - wide)
@@ -40,14 +83,9 @@
     copies = [
         pltpu.make_async_copy(w_ref.at[:, pl.ds(at, wide)], w, sems.at[0]),
         pltpu.make_async_copy(scale_ref.at[:, pl.ds(at, wide)], scale, sems.at[1]),
+        pltpu.make_async_copy(hid_ref.at[1 - core], hid, sems.at[2]),
+        pltpu.make_async_copy(hid_ref.at[core], own_ref, sems.at[3]),
     ]
-    blocks = tokens // width
-    for i in range(blocks):
-        copies.append(
-            pltpu.make_async_copy(
-                hid_ref.at[:, :, pl.ds(i * width, width)], hid.at[i], sems.at[2 + i]
-            )
-        )
     for copy in copies:
         copy.start()
     copies[0].wait()
@@ -58,69 +96,59 @@
     high, low = split(gain)
     gain_sum = jnp.sum(gain, axis=1, keepdims=True)
     stack = jnp.concatenate([high, low, jnp.ones((16, feats), F32)], axis=0).astype(BF)
-    lane = lanes(8)
-    sub = lax.broadcasted_iota(jnp.int32, (8, 128), 0)
-    for i in range(blocks):
-        copies[2 + i].wait()
-        parts, stats = [], []
-        for f in range(frames):
-            x = hid[i, f]
-            prod = jnp.dot(stack, x, preferred_element_type=F32)
-            mean = prod[128:129] * (1.0 / feats)
-            parts.append(prod[0:64] + prod[64:128] - gain_sum * mean)
-            off = x.astype(F32) - mean
-            second = jnp.sum(off * off, axis=0, keepdims=True)
-            m_hi, m_lo = split(mean)
-            s_hi, s_lo = split(second)
-            four = jnp.concatenate([m_hi, m_lo, s_hi, s_lo] * 2, axis=0)
-            stats.append(four)
-        flat = jnp.concatenate(parts, axis=0).T
-        for row in range(width // TOK_W):
-            pair = []
-            for h in range(2):
-                first = row * TOK_W + h * HALF
-                base = (first // 128) * 128
-                span = min(256, width - base)
-                picks = []
-                for f in range(2):
-                    window = stats[f][:, base : base + span]
-                    shift = (64 * f - (first - base)) % span
-                    if shift:
-                        window = pltpu.roll(window, shift, 1)
-                    picks.append(window[:, :128])
-                tail = jnp.where(
-                    lane < HALF,
-                    picks[0],
-                    jnp.where((lane >= 64) & (lane < 64 + HALF), picks[1], 0.0),
-                )
-                tail = jnp.where(lax.div(sub, STAT) == core, tail, 0.0)
-                pair.append(jnp.concatenate([flat[first : first + HALF], tail], axis=0))
-            to = i * (width // TOK_W) + row
-            own_ref[to] = jnp.where(core == 0, pair[0], pair[1]).astype(BF)
-            give_ref[to] = jnp.where(core == 0, pair[1], pair[0]).astype(BF)
-
-
-def project(flags, hidden, head_weight, scale):
-    frames, feats, tokens = hidden.shape
-    width = 640
+    stack_ref[...] = stack
+    gsum_ref[...] = jnp.broadcast_to(gain_sum, gsum_ref.shape)
+    copies[2].wait()
+    frame_sums(hid[...], stack, gain_sum, core, give_ref)
+    copies[3].wait()
+
+
+def project_own_kernel(hid_ref, stack_ref, gsum_ref, own_ref):
+    frame_sums(
+        hid_ref[...], stack_ref[...], gsum_ref[:, 0:1], lax.axis_index("seq") & 1, own_ref
+    )
+
+
+def project(hidden, head_weight, scale):
+    _, feats, tokens = hidden.shape
     rows = tokens // TOK_W
     wide = min(head_weight.shape[1], (feats + 127) // 128 * 128 + 128)
     hbm = pl.BlockSpec(memory_space=pltpu.HBM)
     vmem = pl.BlockSpec(memory_space=pltpu.VMEM)
-    return pl.pallas_call(
-        project_kernel,
-        in_specs=[pl.BlockSpec(memory_space=pltpu.SMEM), hbm, hbm, hbm],
-        out_specs=[vmem, vmem],
-        out_shape=[jax.ShapeDtypeStruct((rows, HALF + 2 * STAT, 128), BF)] * 2,
+    sums = jax.ShapeDtypeStruct((rows, HALF + 2 * STAT, 128), BF)
+    params = pltpu.CompilerParams(vmem_limit_bytes=16 << 20)
+    give, frame, stack, gsum = pl.pallas_call(
+        project_give_kernel,
+        in_specs=[hbm, hbm, hbm],
+        out_specs=[vmem] * 4,
+        out_shape=[
+            sums,
+            jax.ShapeDtypeStruct((feats, tokens), BF),
+            jax.ShapeDtypeStruct((144, feats), BF),
+            jax.ShapeDtypeStruct((64, 128), F32),
+        ],
         scratch_shapes=[
-            pltpu.VMEM((tokens // width, frames, feats, width), BF),
+            pltpu.VMEM((feats, tokens), BF),
             pltpu.VMEM((64, wide), F32),
             pltpu.VMEM((1, wide), F32),
-            pltpu.SemaphoreType.DMA((2 + tokens // width,)),
+            pltpu.SemaphoreType.DMA((4,)),
         ],
-        compiler_params=pltpu.CompilerParams(vmem_limit_bytes=16 << 20),
-        name="project",
-    )(flags, in_hbm(hidden), in_hbm(head_weight), in_hbm(scale))
+        compiler_params=params,
+        name="project_give",
+    )(in_hbm(hidden), in_hbm(head_weight), in_hbm(scale))
+
+    own = pl.pallas_call(
+        project_own_kernel,
+        in_specs=[vmem, vmem, vmem],
+        out_specs=vmem,
+        out_shape=sums,
+        compiler_params=params,
+        cost_estimate=pl.CostEstimate(
+            flops=2 * 144 * feats * tokens, bytes_accessed=1_300_000, transcendentals=0
+        ),
+        name="project_own",
+    )(frame, stack, gsum)
+    return own, give
 
 
 def prepare_first(cin_ref, cin_out):
@@ -258,10 +286,14 @@
     coutv_ref, out_ref, fa, fb, fx, ua, ub, xe, xo, lines, outs, sems,
 ):
     count = table_ref.shape[0]
-    has_low = flags_ref[1]
-    has_high = flags_ref[2]
+
+    def flagged(row, value):
+        return jnp.broadcast_to(flags_ref[row : row + 1, 0 : value.shape[1]], value.shape) > 0.5
+
+    def choose(row, yes, no):
+        return jnp.where(flagged(row, yes), yes, no)
+
     n_stat = 2 * (own_ref.shape[1] - HALF)
-    first_half = (flags_ref[0] & 1) == 0
 
     pick_row = lax.broadcasted_iota(jnp.int32, (count + 8, n_stat), 0)
     pick_col = lax.broadcasted_iota(jnp.int32, (count + 8, n_stat), 1)
@@ -276,7 +308,7 @@
             jnp.concatenate([a[j, HALF:], b[j, HALF:]], axis=0)
             for a, b in ((own_ref, near_ref), (core_ref, far_ref))
         ]
-        wide += [jnp.where(first_half, mine, other), jnp.where(first_half, other, mine)]
+        wide += [choose(0, mine, other), choose(0, other, mine)]
     wide = jnp.concatenate(wide, axis=1)
     stats = jnp.dot(pick, wide, preferred_element_type=F32)
     means = stats[0:count]
@@ -305,30 +337,29 @@
     )
     per_token = jnp.dot(left.T.astype(BF), right.astype(BF), preferred_element_type=F32)
     edge = [[None] * 3 for _ in range(2)]
+    first_lanes = jnp.concatenate([lane40, lane40], axis=1) % 128 < 64
     for j in range(3):
-        halves = []
         mine, other = [
             a[j, 0:HALF].astype(F32) + b[j, 0:HALF].astype(F32)
             for a, b in ((own_ref, near_ref), (core_ref, far_ref))
         ]
-        sums = [jnp.where(first_half, mine, other), jnp.where(first_half, other, mine)]
-        for h in range(2):
-            at = (j * 2 + h) * 128
-            both = jnp.concatenate([lane40, lane40], axis=1) % 128 < 64
-            token = jnp.where(both, per_token[at : at + HALF], per_token[at + 64 : at + 64 + HALF])
-            halves.append(
-                (sums[h] + token[:, 0:128]) * token[:, 128:256]
-                + const_ref[...]
+        sums = [choose(0, mine, other), choose(0, other, mine)]
+        for f in range(2):
+            at = (j * 2 + f) * 128
+            token = jnp.where(
+                first_lanes, per_token[at : at + HALF], per_token[at + 64 : at + 64 + HALF]
             )
-        row = jnp.concatenate(halves, axis=0)
-        if j == 0:
-            row = jnp.where(has_low > 0, row, 0.0)
-        if j == 2:
-            row = jnp.where(has_high > 0, row, 0.0)
-        swapped = pltpu.roll(row, 64, 1)
-        for f in range(2):
-            first = lane80 < 64 if f == 0 else lane80 >= 64
-            both = pltpu.roll(jnp.where(first, row, swapped), 32, 1)
+            row = (sums[f] + token[:, 0:128]) * token[:, 128:256] + const_ref[...]
+            if j == 0:
+                row = choose(1, row, 0.0)
+            if j == 2:
+                row = choose(2, row, 0.0)
+            swapped = pltpu.roll(row, 64, 1)
+            both = jnp.concatenate(
+                [jnp.where(lane40 < 64, row, swapped), jnp.where(lane40 < 64, swapped, row)],
+                axis=0,
+            )
+            both = pltpu.roll(both, 32, 1)
             before = jnp.where(sub80 == 0, 0.0, pltpu.roll(both, 1, 0))
             after = jnp.where(sub80 == TOK_W - 1, 0.0, pltpu.roll(both, TOK_W - 1, 0))
             edge[f][j] = jnp.where(
@@ -341,13 +372,18 @@
         )
 
     patches = [patch(0), patch(1)]
+    both, late = [], []
+    for n in range(2):
+        cols = slice(n * 768, n * 768 + 768)
+        both.append(jnp.dot(jnp.concatenate(patches, axis=0), cin_ref[1, :, cols], preferred_element_type=F32))
+        late.append(jnp.dot(patches[0], cin_ref[0, :, cols], preferred_element_type=F32))
+    both = jnp.concatenate(both, axis=1)
+    pres = [both[0 : 2 * TOK_W], both[2 * TOK_W :] + jnp.concatenate(late, axis=1)]
     bias_in, gain_in = cinv_ref[0:1], cinv_ref[1:2] * 0.5
     sub_one = lax.broadcasted_iota(jnp.int32, (TOK_W, 384), 0)
     zeros_ext = jnp.zeros((TOK_W, 384), F32)
     for f in range(2):
-        pre = jnp.dot(patches[f], cin_ref[1], preferred_element_type=F32)
-        if f == 1:
-            pre = pre + jnp.dot(patches[0], cin_ref[0], preferred_element_type=F32)
+        pre = pres[f]
         for b in range(2):
             for qy in range(2):
                 y = 2 * b + qy
@@ -358,9 +394,9 @@
                     mean_sq = jnp.sum(v * v, axis=1, keepdims=True) * (1.0 / 384)
                     a = silu_half(v * lax.rsqrt(mean_sq + EPS) * gain_in)
                     if y == 0:
-                        a = jnp.where(has_low > 0, a, 0.0)
+                        a = choose(1, a, 0.0)
                     if y == 3:
-                        a = jnp.where(has_high > 0, a, 0.0)
+                        a = choose(2, a, 0.0)
                     act.append(a)
                 even, odd = act
                 back = jnp.where(sub_one == 0, 0.0, pltpu.roll(odd, 1, 0))
@@ -411,6 +447,7 @@
             silu_half(t2 * jnp.where(lane < 64, left, right) * g[:, 256:384]),
         )
 
+    ends = [second(extra[:, py * 384 : py * 384 + 384]) for py in range(2)]
     for f in range(2):
         for pair in range(3):
             at = (f * 3 + pair) * TOK_W
@@ -420,14 +457,14 @@
 
                 def keep(value, y=y):
                     if y == 0:
-                        return jnp.where(has_low > 0, value, 0.0)
+                        return choose(1, value, 0.0)
                     if y == 5:
-                        return jnp.where(has_high > 0, value, 0.0)
+                        return choose(2, value, 0.0)
                     return value
 
                 mid = [keep(t) for t in second(ua[at : at + TOK_W, cols])]
                 low = [keep(t) for t in second(ub[at : at + TOK_W, cols])]
-                end = [keep(t) for t in second(extra[:, cols])]
+                end = [keep(t) for t in ends[py]]
                 to = slice(y * TOK_W, (y + 1) * TOK_W)
                 first = sub80 == 0
                 low[0] = jnp.where(first, 0.0, low[0])
@@ -475,7 +512,7 @@
     vmem = pl.BlockSpec(memory_space=pltpu.VMEM)
     return pl.pallas_call(
         functools.partial(decode_kernel, float(group)),
-        in_specs=[pl.BlockSpec(memory_space=pltpu.SMEM)] + [vmem] * 12,
+        in_specs=[vmem] * 13,
         out_specs=pl.BlockSpec(memory_space=pltpu.HBM),
         out_shape=jax.ShapeDtypeStruct((2, 4, 96, 4 * TOK_W), BF),
         scratch_shapes=[
@@ -578,8 +615,9 @@
     count = lax.axis_size("seq")
     me = lax.axis_index("seq")
     feats = hidden.shape[1]
-    flags = jnp.stack([me, (me > 0).astype(jnp.int32), (me < count - 1).astype(jnp.int32)])
-    own, give = project(flags, hidden, head_weight, mod_scale[None])
+    flags = jnp.stack([me % 2 == 0, me > 0, me < count - 1]).astype(F32)
+    flags = jnp.broadcast_to(flags[:, None], (3, 384))
+    own, give = project(hidden, head_weight, mod_scale[None])
     weights = (head_weight, conv_in_weight, jnp.swapaxes(up_weight, 2, 3), out_weight)
 
     def ready(parts):

time: 30.4 us -> 28.5 us (0.938)
  Pallas kernels: 17 us -> 15.8 us
  waiting for transfers between devices: 4.56 us -> 3.79 us
    ppermute x7, waiting for transfers between devices: 4.56 us -> 3.79 us  [exchange(): return lax.ppermute(block, 'seq', [(i, i ^ mask) for i in range(count)])]
    pallas_call x1, Pallas kernels: 8.65 us -> 7.95 us  [decode(): pl.pallas_call(functools.partial(decode_kernel, float(group)), in_specs=[...]
    pallas_call x1 -> x2, Pallas kernels: 3.22 us -> 2.75 us  [the longest x1 2.05 us: project(): pl.pallas_call(project_give_kernel, in_specs=[hbm, hbm, hbm], out_specs=[...]
  transfers between devices with their start and end apart: 7 -> 7, of which waited for: 4 -> 4; matrix products, arithmetic and copies ran while one was open for 0% -> 1% of each run, Pallas kernels for 17% -> 21%
where the time goes in v4:
time: 28.5 us; the launch traced here: 28.4 us
  Pallas kernels  15.8 us (55%)
  starting transfers between devices  8.05 us (28%)
  waiting for transfers between devices  3.79 us (13%)
  local copies, waits for them, and re-layouts  0.35 us (1%)
    ppermute x7, starting transfers between devices, exchange(): return lax.ppermute(block, 'seq', [(i, i ^ mask) for i in range(count)])  8.05 us
    pallas_call x1, Pallas kernels, decode(): pl.pallas_call(functools.partial(decode_kernel, float(group)), in_specs=[...  7.95 us
    pallas_call x1, Pallas kernels, prepare(): pl.pallas_call(prepare_kernel, in_specs=[hbm, vmem, vmem, vmem, vmem, hbm...  5.14 us
    ppermute x7, waiting for transfers between devices, exchange(): return lax.ppermute(block, 'seq', [(i, i ^ mask) for i in range(count)])  3.79 us
    pallas_call x1, Pallas kernels, project(): pl.pallas_call(project_give_kernel, in_specs=[hbm, hbm, hbm], out_specs=[...  2.05 us
    pallas_call x1, Pallas kernels, project(): pl.pallas_call(project_own_kernel, in_specs=[vmem, vmem, vmem], out_specs...  0.7 us
  transfers between devices with their start and end apart: 7, of which 4 were waited for; matrix products, arithmetic and copies ran while one was open for 1% of the time, Pallas kernels for 21%

profile of v4, /device:TPU:0, one launch (start us, length us, event | category | flops | bytes accessed | tf_op | source)
XLA Modules:
  0.0 28.4 jit_solution(8966583886217398869)
XLA Ops:
  0.0 0.0 copy-start.8
  0.0 0.0 copy-start.3
  0.0 0.0 copy-start.4
  0.0 0.0 copy-start.5
  0.0 0.0 copy-start.6
  0.0 2.0 %project_give.1 = (bf16[16,48,128]{2,1,0:T(8,128)(2,1)S(1)}, bf16[320,1280]{1,0:T(8,128)(2,1)S(1)}, bf16[144,320]{1,0:T(8,128)(2,1)S(1)}, f32[64,128]{1,0:T(8,128)S(1)}) custom-call(bf16[2,320,1280]{2,1,0:T(8,128)(2,1)} %hid_ref.1, f32[64,5120]{1,0:T(8,128)} %w_ref.2, f32[1,5120]{1,0:T(1,128)} %bitcast.14), custom_call_target="tpu_custom_call" | custom-call | tf_op jit(solution)/shard_map/project_give/pallas_call | solution.py:120
  2.1 0.0 copy-start.7
  2.1 0.0 copy-start
  2.1 0.0 copy-start.1
  2.1 0.0 copy-start.2
  2.1 0.5 %collective-permute-start = (bf16[16,48,128]{2,1,0:T(8,128)(2,1)S(1)}, bf16[16,48,128]{2,1,0:T(8,128)(2,1)S(1)}, u32[]{:S(2)}, u32[]{:S(2)}) collective-permute-start(bf16[16,48,128]{2,1,0:T(8,128)(2,1)S(1)} %get-tuple-element.30), channel_id=1, source_target_pairs={{0,1},{1,0},{2,3},{3,2},{4,5},{5,4},{6,7},{7,6},{8,9},{9,8},{10,11... | collective-permute-start | bytes 589832 | tf_op jit(solution)/shard_map/ppermute | solution.py:539
  2.6 0.0 copy-done.3
  2.6 0.0 copy-done.4
  2.7 0.0 copy-done.8
  2.7 0.1 copy.15.dev_ref
  2.8 0.7 %project_own.1 = bf16[16,48,128]{2,1,0:T(8,128)(2,1)S(1)} custom-call(bf16[320,1280]{1,0:T(8,128)(2,1)S(1)} %get-tuple-element.27.hid_ref, bf16[144,320]{1,0:T(8,128)(2,1)S(1)} %get-tuple-element.28.stack_ref, f32[64,128]{1,0:T(8,128)S(1)} %get-tuple-element.29.gsum_ref), custom_call_target="tpu_custom_call" | custom-call | flops 117964800 | bytes 1300000 | tf_op jit(solution)/shard_map/project_own/pallas_call | solution.py:140
  3.5 0.0 copy-done.5
  3.5 0.0 copy-done.6
  3.5 0.2 collective-permute-done
  3.7 0.1 add_convert_fusion
  3.8 4.0 %collective-permute-start.1 = (bf16[6,48,128]{2,1,0:T(8,128)(2,1)S(1)}, bf16[6,48,128]{2,1,0:T(8,128)(2,1)S(1)}, u32[]{:S(2)}, u32[]{:S(2)}) collective-permute-start(bf16[6,48,128]{2,1,0:T(8,128)(2,1)S(1)} %get-tuple-element.49), channel_id=1, source_target_pairs={{0,8},{1,9},{2,10},{3,11},{4,12},{5,13},{6,14},{7,15},{8,0},{9,1},... | collective-permute-start | bytes 221192 | tf_op jit(solution)/shard_map/ppermute | solution.py:539
  7.8 1.3 %collective-permute-start.3 = (bf16[6,48,128]{2,1,0:T(8,128)(2,1)S(1)}, bf16[6,48,128]{2,1,0:T(8,128)(2,1)S(1)}, u32[]{:S(2)}, u32[]{:S(2)}) collective-permute-start(bf16[6,48,128]{2,1,0:T(8,128)(2,1)S(1)} %get-tuple-element.50), channel_id=1, source_target_pairs={{0,12},{1,13},{2,14},{3,15},{4,8},{5,9},{6,10},{7,11},{8,4},{9,5},... | collective-permute-start | bytes 221192 | tf_op jit(solution)/shard_map/ppermute | solution.py:539
  9.2 0.2 collective-permute-start.2
  9.4 0.0 copy-done.7
  9.4 0.0 copy-done
  9.4 0.0 copy-done.1
  9.4 0.0 copy-done.2
  9.4 5.1 %prepare.1 = (f32[16,128]{1,0:T(8,128)S(1)}, f32[1,128]{1,0:T(1,128)S(1)}, bf16[2,256,1536]{2,1,0:T(8,128)(2,1)S(1)}, bf16[768,1536]{1,0:T(8,128)(2,1)S(1)}, f32...) custom-call(f32[64,5120]{1,0:T(8,128)} %w_ref.2, f32[1,5120]{1,0:T(1,128)S(1)} %bitcast.15, f32[1,5120]{1,0:T(1,128)S(1)} %bitcast.16, ...), custom_call_target="tpu_custom_call" | custom-call | flops 20000000 | bytes 10000000 | tf_op jit(solution)/shard_map/prepare/pallas_call | solution.py:251
  14.6 0.0 collective-permute-done.1
  14.6 0.0 collective-permute-done.3
  14.6 0.3 %collective-permute-done.2 = bf16[6,48,128]{2,1,0:T(8,128)(2,1)S(1)} collective-permute-done((bf16[6,48,128]{2,1,0:T(8,128)(2,1)S(1)}, bf16[6,48,128]{2,1,0:T(8,128)(2,1)S(1)}, u32[]{:S(2)}, u32[]{:S(2)}) %collective-permute-start.2) | collective-permute-done | bytes 73760 | tf_op jit(solution)/shard_map/ppermute | solution.py:539
  15.1 0.1 pad_dynamic-slice_fusion
  15.1 0.5 %collective-permute-start.6 = (bf16[3,72,128]{2,1,0:T(8,128)(2,1)S(1)}, bf16[3,72,128]{2,1,0:T(8,128)(2,1)S(1)}, u32[]{:S(2)}, u32[]{:S(2)}) collective-permute-start(bf16[3,72,128]{2,1,0:T(8,128)(2,1)S(1)} %get-tuple-element.52), channel_id=1, source_target_pairs={{0,3},{1,2},{2,1},{3,0},{4,7},{5,6},{6,5},{7,4},{8,11},{9,10},{10,... | collective-permute-start | bytes 165896 | tf_op jit(solution)/shard_map/ppermute | solution.py:539
  15.6 1.3 %collective-permute-start.4 = (bf16[3,72,128]{2,1,0:T(8,128)(2,1)S(1)}, bf16[3,72,128]{2,1,0:T(8,128)(2,1)S(1)}, u32[]{:S(2)}, u32[]{:S(2)}) collective-permute-start(bf16[3,72,128]{2,1,0:T(8,128)(2,1)S(1)} %get-tuple-element.53), channel_id=1, source_target_pairs={{0,2},{1,3},{2,0},{3,1},{4,6},{5,7},{6,4},{7,5},{8,10},{9,11},{10,... | collective-permute-start | bytes 165896 | tf_op jit(solution)/shard_map/ppermute | solution.py:539
  16.9 0.2 collective-permute-start.5
  17.1 0.1 add_convert_fusion.2
  17.1 2.1 %collective-permute-done.6.far_ref = bf16[3,72,128]{2,1,0:T(8,128)(2,1)S(1)} collective-permute-done((bf16[3,72,128]{2,1,0:T(8,128)(2,1)S(1)}, bf16[3,72,128]{2,1,0:T(8,128)(2,1)S(1)}, u32[]{:S(2)}, u32[]{:S(2)}) %collective-permute-start.6) | collective-permute-done | bytes 55328 | tf_op jit(solution)/shard_map/ppermute | solution.py:539
  19.2 1.2 %collective-permute-done.4.near_ref = bf16[3,72,128]{2,1,0:T(8,128)(2,1)S(1)} collective-permute-done((bf16[3,72,128]{2,1,0:T(8,128)(2,1)S(1)}, bf16[3,72,128]{2,1,0:T(8,128)(2,1)S(1)}, u32[]{:S(2)}, u32[]{:S(2)}) %collective-permute-start.4) | collective-permute-done | bytes 55328 | tf_op jit(solution)/shard_map/ppermute | solution.py:539
  20.4 0.0 collective-permute-done.5.core_ref
  20.4 0.1 broadcast_in_dim.22.flags_ref
  20.5 7.9 %decode.1 = bf16[2,4,96,320]{3,2,1,0:T(8,128)(2,1)} custom-call(f32[3,384]{1,0:T(4,128)S(1)} %broadcast_in_dim.22.flags_ref, bf16[3,72,128]{2,1,0:T(8,128)(2,1)S(1)} %get-tuple-element.55.own_ref, bf16[3,72,128]{2,1,0:T(8,128)(2,1)S(1)} %collective-permute-done.4.near_ref, bf16[3,72,128]{2,1,0:T(8,128)(2,1)S(1)} %collective-permute-done.5.core_ref, ...), custom_call_target="tpu_custom_call" | custom-call | flops 5000000000 | bytes 8000000 | tf_op jit(solution)/shard_map/decode/pallas_call | solution.py:513
  (12 shorter events, 0.2 us)
Async XLA Ops:
  0.0 2.7 %copy-start.8 = (s32[16]{0:T(128)S(1)}, s32[16]{0:T(128)}, u32[]{:S(2)}) copy-start(s32[16]{0:T(128)} %constant.65.clone) | copy-start | bytes 196
  0.0 2.6 %copy-start.3 = (f32[384]{0:T(512)S(1)}, f32[384]{0:T(512)}, u32[]{:S(2)}) copy-start(f32[384]{0:T(512)} %param.20) | copy-start | bytes 4612
  0.0 2.6 %copy-start.4 = (f32[384]{0:T(512)S(1)}, f32[384]{0:T(512)}, u32[]{:S(2)}) copy-start(f32[384]{0:T(512)} %param.21) | copy-start | bytes 4612
  0.0 3.5 %copy-start.5 = (f32[192]{0:T(256)S(1)}, f32[192]{0:T(256)}, u32[]{:S(2)}) copy-start(f32[192]{0:T(256)} %param.24) | copy-start | bytes 2308
  0.0 3.5 %copy-start.6 = (f32[192]{0:T(256)S(1)}, f32[192]{0:T(256)}, u32[]{:S(2)}) copy-start(f32[192]{0:T(256)} %param.23) | copy-start | bytes 2308
  2.1 7.3 %copy-start.7 = (f32[96]{0:T(128)S(1)}, f32[96]{0:T(128)}, u32[]{:S(2)}) copy-start(f32[96]{0:T(128)} %param.26) | copy-start | bytes 1156
  2.1 7.3 %copy-start = (f32[5120]{0:T(1024)S(1)}, f32[5120]{0:T(1024)}, u32[]{:S(2)}) copy-start(f32[5120]{0:T(1024)} %param.16) | copy-start | bytes 61444
  2.1 7.3 %copy-start.1 = (f32[5120]{0:T(1024)S(1)}, f32[5120]{0:T(1024)}, u32[]{:S(2)}) copy-start(f32[5120]{0:T(1024)} %param.15) | copy-start | bytes 61444
  2.1 7.3 %copy-start.2 = (f32[64]{0:T(128)S(1)}, f32[64]{0:T(128)}, u32[]{:S(2)}) copy-start(f32[64]{0:T(128)} %param.18) | copy-start | bytes 772
  2.1 1.6 %collective-permute-start = (bf16[16,48,128]{2,1,0:T(8,128)(2,1)S(1)}, bf16[16,48,128]{2,1,0:T(8,128)(2,1)S(1)}, u32[]{:S(2)}, u32[]{:S(2)}) collective-permute-start(bf16[16,48,128]{2,1,0:T(8,128)(2,1)S(1)} %get-tuple-element.30), channel_id=1, source_target_pairs={{0,1},{1,0},{2,3},{3,2},{4,5},{5,4},{6,7},{7,6},{8,9},{9,8},{10,11... | collective-permute-start | bytes 589832 | tf_op jit(solution)/shard_map/ppermute | solution.py:539
  3.8 10.8 %collective-permute-start.1 = (bf16[6,48,128]{2,1,0:T(8,128)(2,1)S(1)}, bf16[6,48,128]{2,1,0:T(8,128)(2,1)S(1)}, u32[]{:S(2)}, u32[]{:S(2)}) collective-permute-start(bf16[6,48,128]{2,1,0:T(8,128)(2,1)S(1)} %get-tuple-element.49), channel_id=1, source_target_pairs={{0,8},{1,9},{2,10},{3,11},{4,12},{5,13},{6,14},{7,15},{8,0},{9,1},... | collective-permute-start | bytes 221192 | tf_op jit(solution)/shard_map/ppermute | solution.py:539
  7.8 6.8 %collective-permute-start.3 = (bf16[6,48,128]{2,1,0:T(8,128)(2,1)S(1)}, bf16[6,48,128]{2,1,0:T(8,128)(2,1)S(1)}, u32[]{:S(2)}, u32[]{:S(2)}) collective-permute-start(bf16[6,48,128]{2,1,0:T(8,128)(2,1)S(1)} %get-tuple-element.50), channel_id=1, source_target_pairs={{0,12},{1,13},{2,14},{3,15},{4,8},{5,9},{6,10},{7,11},{8,4},{9,5},... | collective-permute-start | bytes 221192 | tf_op jit(solution)/shard_map/ppermute | solution.py:539
  9.2 5.8 %collective-permute-start.2 = (bf16[6,48,128]{2,1,0:T(8,128)(2,1)S(1)}, bf16[6,48,128]{2,1,0:T(8,128)(2,1)S(1)}, u32[]{:S(2)}, u32[]{:S(2)}) collective-permute-start(bf16[6,48,128]{2,1,0:T(8,128)(2,1)S(1)} %get-tuple-element.51), channel_id=1, source_target_pairs={{0,4},{1,5},{2,6},{3,7},{4,0},{5,1},{6,2},{7,3},{8,12},{9,13},{10,... | collective-permute-start | bytes 221192 | tf_op jit(solution)/shard_map/ppermute | solution.py:539
  15.1 4.1 %collective-permute-start.6 = (bf16[3,72,128]{2,1,0:T(8,128)(2,1)S(1)}, bf16[3,72,128]{2,1,0:T(8,128)(2,1)S(1)}, u32[]{:S(2)}, u32[]{:S(2)}) collective-permute-start(bf16[3,72,128]{2,1,0:T(8,128)(2,1)S(1)} %get-tuple-element.52), channel_id=1, source_target_pairs={{0,3},{1,2},{2,1},{3,0},{4,7},{5,6},{6,5},{7,4},{8,11},{9,10},{10,... | collective-permute-start | bytes 165896 | tf_op jit(solution)/shard_map/ppermute | solution.py:539
  15.6 4.8 %collective-permute-start.4 = (bf16[3,72,128]{2,1,0:T(8,128)(2,1)S(1)}, bf16[3,72,128]{2,1,0:T(8,128)(2,1)S(1)}, u32[]{:S(2)}, u32[]{:S(2)}) collective-permute-start(bf16[3,72,128]{2,1,0:T(8,128)(2,1)S(1)} %get-tuple-element.53), channel_id=1, source_target_pairs={{0,2},{1,3},{2,0},{3,1},{4,6},{5,7},{6,4},{7,5},{8,10},{9,11},{10,... | collective-permute-start | bytes 165896 | tf_op jit(solution)/shard_map/ppermute | solution.py:539
  16.9 3.5 %collective-permute-start.5 = (bf16[3,72,128]{2,1,0:T(8,128)(2,1)S(1)}, bf16[3,72,128]{2,1,0:T(8,128)(2,1)S(1)}, u32[]{:S(2)}, u32[]{:S(2)}) collective-permute-start(bf16[3,72,128]{2,1,0:T(8,128)(2,1)S(1)} %get-tuple-element.54), channel_id=1, source_target_pairs={{0,1},{1,0},{2,3},{3,2},{4,5},{5,4},{6,7},{7,6},{8,9},{9,8},{10,11... | collective-permute-start | bytes 165896 | tf_op jit(solution)/shard_map/ppermute | solution.py:539

commit v5 on v4

--- a/solution.py
+++ b/solution.py
@@ -417,17 +417,20 @@
                     )
     del sub_one
 
-    def times_up(x):
-        dims = (((1,), (1,)), ((), ()))
-        return lax.dot_general(x, up_ref[...], dims, preferred_element_type=F32)
-
-    ua[...] = times_up(fa[...])
     extra_in = jnp.where(
         lax.broadcasted_iota(jnp.int32, (8, 1536), 0) < 6, fx[...], 0.0
     )
     extra_in = jnp.concatenate([extra_in, jnp.zeros((8, 1536), F32)], axis=0).astype(BF)
     fb[6 * TOK_W :] = extra_in
-    ub[...] = times_up(fb[...])
+    chunk = 3 * TOK_W
+    for n in range(0, 768, 256):
+        for first in (0, chunk):
+            for given, result in ((fa, ua), (fb, ub)):
+                rows = slice(first, first + chunk if first == 0 else given.shape[0])
+                result[rows, n : n + 256] = lax.dot_general(
+                    given[rows], up_ref[n : n + 256], (((1,), (1,)), ((), ())),
+                    preferred_element_type=F32,
+                )
     extra = ub[6 * TOK_W : 6 * TOK_W + 8]
     bias_up, gain_up = upv_ref[0:1], upv_ref[1:2] * 0.5
 
@@ -622,14 +625,14 @@
 
     def ready(parts):
         head_again, cin, up, cout = parts
-        return prepare(
+        return flags, prepare(
             head_again, mod_scale[None], mod_shift[None], head_bias[None],
             (((me // 2) * 2) ^ device_order(count))[:, None],
             cin, up, jnp.stack([up_bias, gain_up]), cout,
         )
 
     pieces, weights = gather_rows(own, give, weights, ready, me, count)
-    table, const, cin, up, upv, cout = weights
+    flags, (table, const, cin, up, upv, cout) = weights
     cinv = jnp.stack([conv_in_bias, gain_in])
     coutv = jnp.pad(out_bias, (0, 32))[None]
     out = decode(feats, flags, pieces, table, const, cin, cinv, up, upv, cout, coutv)

time: 28.5 us -> 28.4 us (level)
  no operation moved by 1% of the time
where the time goes in v5:
time: 28.4 us; the launch traced here: 28.3 us
  Pallas kernels  15.7 us (55%)
  starting transfers between devices  8.05 us (28%)
  waiting for transfers between devices  3.79 us (13%)
  local copies, waits for them, and re-layouts  0.33 us (1%)
    ppermute x7, starting transfers between devices, exchange(): return lax.ppermute(block, 'seq', [(i, i ^ mask) for i in range(count)])  8.05 us
    pallas_call x1, Pallas kernels, decode(): pl.pallas_call(functools.partial(decode_kernel, float(group)), in_specs=[...  7.84 us
    pallas_call x1, Pallas kernels, prepare(): pl.pallas_call(prepare_kernel, in_specs=[hbm, vmem, vmem, vmem, vmem, hbm...  5.14 us
    ppermute x7, waiting for transfers between devices, exchange(): return lax.ppermute(block, 'seq', [(i, i ^ mask) for i in range(count)])  3.79 us
    pallas_call x1, Pallas kernels, project(): pl.pallas_call(project_give_kernel, in_specs=[hbm, hbm, hbm], out_specs=[...  2.05 us
    pallas_call x1, Pallas kernels, project(): pl.pallas_call(project_own_kernel, in_specs=[vmem, vmem, vmem], out_specs...  0.7 us
  transfers between devices with their start and end apart: 7, of which 4 were waited for; matrix products, arithmetic and copies ran while one was open for 1% of the time, Pallas kernels for 21%

profile of v5, /device:TPU:0, one launch (start us, length us, event | category | flops | bytes accessed | tf_op | source)
XLA Modules:
  0.0 28.3 jit_solution(2196659411013215346)
XLA Ops:
  0.0 0.0 copy-start.8
  0.0 0.0 copy-start.3
  0.0 0.0 copy-start.4
  0.0 0.0 copy-start.5
  0.0 0.0 copy-start.6
  0.0 2.0 %project_give.1 = (bf16[16,48,128]{2,1,0:T(8,128)(2,1)S(1)}, bf16[320,1280]{1,0:T(8,128)(2,1)S(1)}, bf16[144,320]{1,0:T(8,128)(2,1)S(1)}, f32[64,128]{1,0:T(8,128)S(1)}) custom-call(bf16[2,320,1280]{2,1,0:T(8,128)(2,1)} %hid_ref.1, f32[64,5120]{1,0:T(8,128)} %w_ref.2, f32[1,5120]{1,0:T(1,128)} %bitcast.14), custom_call_target="tpu_custom_call" | custom-call | tf_op jit(solution)/shard_map/project_give/pallas_call | solution.py:120
  2.1 0.0 copy-start
  2.1 0.0 copy-start.1
  2.1 0.0 copy-start.2
  2.1 0.5 %collective-permute-start = (bf16[16,48,128]{2,1,0:T(8,128)(2,1)S(1)}, bf16[16,48,128]{2,1,0:T(8,128)(2,1)S(1)}, u32[]{:S(2)}, u32[]{:S(2)}) collective-permute-start(bf16[16,48,128]{2,1,0:T(8,128)(2,1)S(1)} %get-tuple-element.31), channel_id=1, source_target_pairs={{0,1},{1,0},{2,3},{3,2},{4,5},{5,4},{6,7},{7,6},{8,9},{9,8},{10,11... | collective-permute-start | bytes 589832 | tf_op jit(solution)/shard_map/ppermute | solution.py:542
  2.6 0.0 copy-done.3
  2.6 0.0 copy-done.4
  2.6 0.0 copy-done.8
  2.7 0.1 copy.15.dev_ref
  2.8 0.7 %project_own.1 = bf16[16,48,128]{2,1,0:T(8,128)(2,1)S(1)} custom-call(bf16[320,1280]{1,0:T(8,128)(2,1)S(1)} %get-tuple-element.28.hid_ref, bf16[144,320]{1,0:T(8,128)(2,1)S(1)} %get-tuple-element.29.stack_ref, f32[64,128]{1,0:T(8,128)S(1)} %get-tuple-element.30.gsum_ref), custom_call_target="tpu_custom_call" | custom-call | flops 117964800 | bytes 1300000 | tf_op jit(solution)/shard_map/project_own/pallas_call | solution.py:140
  3.5 0.0 copy-done.5
  3.5 0.0 copy-done.6
  3.5 0.2 collective-permute-done
  3.7 0.1 add_convert_fusion
  3.8 4.0 %collective-permute-start.1 = (bf16[6,48,128]{2,1,0:T(8,128)(2,1)S(1)}, bf16[6,48,128]{2,1,0:T(8,128)(2,1)S(1)}, u32[]{:S(2)}, u32[]{:S(2)}) collective-permute-start(bf16[6,48,128]{2,1,0:T(8,128)(2,1)S(1)} %get-tuple-element.51), channel_id=1, source_target_pairs={{0,8},{1,9},{2,10},{3,11},{4,12},{5,13},{6,14},{7,15},{8,0},{9,1},... | collective-permute-start | bytes 221192 | tf_op jit(solution)/shard_map/ppermute | solution.py:542
  7.8 1.3 %collective-permute-start.3 = (bf16[6,48,128]{2,1,0:T(8,128)(2,1)S(1)}, bf16[6,48,128]{2,1,0:T(8,128)(2,1)S(1)}, u32[]{:S(2)}, u32[]{:S(2)}) collective-permute-start(bf16[6,48,128]{2,1,0:T(8,128)(2,1)S(1)} %get-tuple-element.52), channel_id=1, source_target_pairs={{0,12},{1,13},{2,14},{3,15},{4,8},{5,9},{6,10},{7,11},{8,4},{9,5},... | collective-permute-start | bytes 221192 | tf_op jit(solution)/shard_map/ppermute | solution.py:542
  9.2 0.2 collective-permute-start.2
  9.4 0.1 add_convert_fusion.2
  9.5 0.0 copy-done
  9.5 0.0 copy-done.1
  9.5 0.0 copy-done.2
  9.5 0.0 copy-start.7
  9.5 5.1 %prepare.1 = (f32[16,128]{1,0:T(8,128)S(1)}, f32[1,128]{1,0:T(1,128)S(1)}, bf16[2,256,1536]{2,1,0:T(8,128)(2,1)S(1)}, bf16[768,1536]{1,0:T(8,128)(2,1)S(1)}, f32...) custom-call(f32[64,5120]{1,0:T(8,128)} %w_ref.2, f32[1,5120]{1,0:T(1,128)S(1)} %bitcast.15, f32[1,5120]{1,0:T(1,128)S(1)} %bitcast.16, ...), custom_call_target="tpu_custom_call" | custom-call | flops 20000000 | bytes 10000000 | tf_op jit(solution)/shard_map/prepare/pallas_call | solution.py:251
  14.6 0.0 collective-permute-done.1
  14.7 0.0 collective-permute-done.3
  14.7 0.3 collective-permute-done.2
  15.0 0.1 broadcast_in_dim.23.flags_ref
  15.2 0.5 %collective-permute-start.6 = (bf16[3,72,128]{2,1,0:T(8,128)(2,1)S(1)}, bf16[3,72,128]{2,1,0:T(8,128)(2,1)S(1)}, u32[]{:S(2)}, u32[]{:S(2)}) collective-permute-start(bf16[3,72,128]{2,1,0:T(8,128)(2,1)S(1)} %get-tuple-element.54), channel_id=1, source_target_pairs={{0,3},{1,2},{2,1},{3,0},{4,7},{5,6},{6,5},{7,4},{8,11},{9,10},{10,... | collective-permute-start | bytes 165896 | tf_op jit(solution)/shard_map/ppermute | solution.py:542
  15.7 1.2 %collective-permute-start.4 = (bf16[3,72,128]{2,1,0:T(8,128)(2,1)S(1)}, bf16[3,72,128]{2,1,0:T(8,128)(2,1)S(1)}, u32[]{:S(2)}, u32[]{:S(2)}) collective-permute-start(bf16[3,72,128]{2,1,0:T(8,128)(2,1)S(1)} %get-tuple-element.55), channel_id=1, source_target_pairs={{0,2},{1,3},{2,0},{3,1},{4,6},{5,7},{6,4},{7,5},{8,10},{9,11},{10,... | collective-permute-start | bytes 165896 | tf_op jit(solution)/shard_map/ppermute | solution.py:542
  16.9 0.2 collective-permute-start.5
  17.1 0.0 copy-done.7
  17.1 2.1 %collective-permute-done.6.far_ref = bf16[3,72,128]{2,1,0:T(8,128)(2,1)S(1)} collective-permute-done((bf16[3,72,128]{2,1,0:T(8,128)(2,1)S(1)}, bf16[3,72,128]{2,1,0:T(8,128)(2,1)S(1)}, u32[]{:S(2)}, u32[]{:S(2)}) %collective-permute-start.6) | collective-permute-done | bytes 55328 | tf_op jit(solution)/shard_map/ppermute | solution.py:542
  19.2 1.2 %collective-permute-done.4.near_ref = bf16[3,72,128]{2,1,0:T(8,128)(2,1)S(1)} collective-permute-done((bf16[3,72,128]{2,1,0:T(8,128)(2,1)S(1)}, bf16[3,72,128]{2,1,0:T(8,128)(2,1)S(1)}, u32[]{:S(2)}, u32[]{:S(2)}) %collective-permute-start.4) | collective-permute-done | bytes 55328 | tf_op jit(solution)/shard_map/ppermute | solution.py:542
  20.4 0.0 collective-permute-done.5.core_ref
  20.4 7.8 %decode.1 = bf16[2,4,96,320]{3,2,1,0:T(8,128)(2,1)} custom-call(f32[3,384]{1,0:T(4,128)S(1)} %broadcast_in_dim.23.flags_ref, bf16[3,72,128]{2,1,0:T(8,128)(2,1)S(1)} %get-tuple-element.57.own_ref, bf16[3,72,128]{2,1,0:T(8,128)(2,1)S(1)} %collective-permute-done.4.near_ref, bf16[3,72,128]{2,1,0:T(8,128)(2,1)S(1)} %collective-permute-done.5.core_ref, ...), custom_call_target="tpu_custom_call" | custom-call | flops 5000000000 | bytes 8000000 | tf_op jit(solution)/shard_map/decode/pallas_call | solution.py:516
  (13 shorter events, 0.2 us)
Async XLA Ops:
  0.0 2.6 %copy-start.8 = (s32[16]{0:T(128)S(1)}, s32[16]{0:T(128)}, u32[]{:S(2)}) copy-start(s32[16]{0:T(128)} %constant.65.clone) | copy-start | bytes 196
  0.0 2.6 %copy-start.3 = (f32[384]{0:T(512)S(1)}, f32[384]{0:T(512)}, u32[]{:S(2)}) copy-start(f32[384]{0:T(512)} %param.20) | copy-start | bytes 4612
  0.0 2.6 %copy-start.4 = (f32[384]{0:T(512)S(1)}, f32[384]{0:T(512)}, u32[]{:S(2)}) copy-start(f32[384]{0:T(512)} %param.21) | copy-start | bytes 4612
  0.0 3.5 %copy-start.5 = (f32[192]{0:T(256)S(1)}, f32[192]{0:T(256)}, u32[]{:S(2)}) copy-start(f32[192]{0:T(256)} %param.24) | copy-start | bytes 2308
  0.0 3.5 %copy-start.6 = (f32[192]{0:T(256)S(1)}, f32[192]{0:T(256)}, u32[]{:S(2)}) copy-start(f32[192]{0:T(256)} %param.23) | copy-start | bytes 2308
  2.1 7.4 %copy-start = (f32[5120]{0:T(1024)S(1)}, f32[5120]{0:T(1024)}, u32[]{:S(2)}) copy-start(f32[5120]{0:T(1024)} %param.16) | copy-start | bytes 61444
  2.1 7.4 %copy-start.1 = (f32[5120]{0:T(1024)S(1)}, f32[5120]{0:T(1024)}, u32[]{:S(2)}) copy-start(f32[5120]{0:T(1024)} %param.15) | copy-start | bytes 61444
  2.1 7.4 %copy-start.2 = (f32[64]{0:T(128)S(1)}, f32[64]{0:T(128)}, u32[]{:S(2)}) copy-start(f32[64]{0:T(128)} %param.18) | copy-start | bytes 772
  2.1 1.6 %collective-permute-start = (bf16[16,48,128]{2,1,0:T(8,128)(2,1)S(1)}, bf16[16,48,128]{2,1,0:T(8,128)(2,1)S(1)}, u32[]{:S(2)}, u32[]{:S(2)}) collective-permute-start(bf16[16,48,128]{2,1,0:T(8,128)(2,1)S(1)} %get-tuple-element.31), channel_id=1, source_target_pairs={{0,1},{1,0},{2,3},{3,2},{4,5},{5,4},{6,7},{7,6},{8,9},{9,8},{10,11... | collective-permute-start | bytes 589832 | tf_op jit(solution)/shard_map/ppermute | solution.py:542
  3.8 10.9 %collective-permute-start.1 = (bf16[6,48,128]{2,1,0:T(8,128)(2,1)S(1)}, bf16[6,48,128]{2,1,0:T(8,128)(2,1)S(1)}, u32[]{:S(2)}, u32[]{:S(2)}) collective-permute-start(bf16[6,48,128]{2,1,0:T(8,128)(2,1)S(1)} %get-tuple-element.51), channel_id=1, source_target_pairs={{0,8},{1,9},{2,10},{3,11},{4,12},{5,13},{6,14},{7,15},{8,0},{9,1},... | collective-permute-start | bytes 221192 | tf_op jit(solution)/shard_map/ppermute | solution.py:542
  7.8 6.8 %collective-permute-start.3 = (bf16[6,48,128]{2,1,0:T(8,128)(2,1)S(1)}, bf16[6,48,128]{2,1,0:T(8,128)(2,1)S(1)}, u32[]{:S(2)}, u32[]{:S(2)}) collective-permute-start(bf16[6,48,128]{2,1,0:T(8,128)(2,1)S(1)} %get-tuple-element.52), channel_id=1, source_target_pairs={{0,12},{1,13},{2,14},{3,15},{4,8},{5,9},{6,10},{7,11},{8,4},{9,5},... | collective-permute-start | bytes 221192 | tf_op jit(solution)/shard_map/ppermute | solution.py:542
  9.2 5.8 %collective-permute-start.2 = (bf16[6,48,128]{2,1,0:T(8,128)(2,1)S(1)}, bf16[6,48,128]{2,1,0:T(8,128)(2,1)S(1)}, u32[]{:S(2)}, u32[]{:S(2)}) collective-permute-start(bf16[6,48,128]{2,1,0:T(8,128)(2,1)S(1)} %get-tuple-element.53), channel_id=1, source_target_pairs={{0,4},{1,5},{2,6},{3,7},{4,0},{5,1},{6,2},{7,3},{8,12},{9,13},{10,... | collective-permute-start | bytes 221192 | tf_op jit(solution)/shard_map/ppermute | solution.py:542
  9.5 7.6 %copy-start.7 = (f32[96]{0:T(128)S(1)}, f32[96]{0:T(128)}, u32[]{:S(2)}) copy-start(f32[96]{0:T(128)} %param.26) | copy-start | bytes 1156
  15.2 4.1 %collective-permute-start.6 = (bf16[3,72,128]{2,1,0:T(8,128)(2,1)S(1)}, bf16[3,72,128]{2,1,0:T(8,128)(2,1)S(1)}, u32[]{:S(2)}, u32[]{:S(2)}) collective-permute-start(bf16[3,72,128]{2,1,0:T(8,128)(2,1)S(1)} %get-tuple-element.54), channel_id=1, source_target_pairs={{0,3},{1,2},{2,1},{3,0},{4,7},{5,6},{6,5},{7,4},{8,11},{9,10},{10,... | collective-permute-start | bytes 165896 | tf_op jit(solution)/shard_map/ppermute | solution.py:542
  15.7 4.7 %collective-permute-start.4 = (bf16[3,72,128]{2,1,0:T(8,128)(2,1)S(1)}, bf16[3,72,128]{2,1,0:T(8,128)(2,1)S(1)}, u32[]{:S(2)}, u32[]{:S(2)}) collective-permute-start(bf16[3,72,128]{2,1,0:T(8,128)(2,1)S(1)} %get-tuple-element.55), channel_id=1, source_target_pairs={{0,2},{1,3},{2,0},{3,1},{4,6},{5,7},{6,4},{7,5},{8,10},{9,11},{10,... | collective-permute-start | bytes 165896 | tf_op jit(solution)/shard_map/ppermute | solution.py:542
  16.9 3.5 %collective-permute-start.5 = (bf16[3,72,128]{2,1,0:T(8,128)(2,1)S(1)}, bf16[3,72,128]{2,1,0:T(8,128)(2,1)S(1)}, u32[]{:S(2)}, u32[]{:S(2)}) collective-permute-start(bf16[3,72,128]{2,1,0:T(8,128)(2,1)S(1)} %get-tuple-element.56), channel_id=1, source_target_pairs={{0,1},{1,0},{2,3},{3,2},{4,5},{5,4},{6,7},{7,6},{8,9},{9,8},{10,11... | collective-permute-start | bytes 165896 | tf_op jit(solution)/shard_map/ppermute | solution.py:542

commit v6 on v5

--- a/solution.py
+++ b/solution.py
@@ -302,14 +302,14 @@
     pick = pick.astype(F32).astype(BF)
     lane40 = lanes(HALF)
     lane80, sub80 = lanes(TOK_W), lax.broadcasted_iota(jnp.int32, (TOK_W, 128), 0)
+    loaded = [r[...].astype(F32) for r in (own_ref, near_ref, core_ref, far_ref)]
     wide = []
     for j in range(3):
         mine, other = [
-            jnp.concatenate([a[j, HALF:], b[j, HALF:]], axis=0)
-            for a, b in ((own_ref, near_ref), (core_ref, far_ref))
+            jnp.concatenate([a[j, HALF:], b[j, HALF:]], axis=0) for a, b in (loaded[:2], loaded[2:])
         ]
         wide += [choose(0, mine, other), choose(0, other, mine)]
-    wide = jnp.concatenate(wide, axis=1)
+    wide = jnp.concatenate(wide, axis=1).astype(BF)
     stats = jnp.dot(pick, wide, preferred_element_type=F32)
     means = stats[0:count]
     off = means - jnp.sum(means, axis=0, keepdims=True) * (1.0 / count)
@@ -340,8 +340,7 @@
     first_lanes = jnp.concatenate([lane40, lane40], axis=1) % 128 < 64
     for j in range(3):
         mine, other = [
-            a[j, 0:HALF].astype(F32) + b[j, 0:HALF].astype(F32)
-            for a, b in ((own_ref, near_ref), (core_ref, far_ref))
+            a[j, 0:HALF] + b[j, 0:HALF] for a, b in (loaded[:2], loaded[2:])
         ]
         sums = [choose(0, mine, other), choose(0, other, mine)]
         for f in range(2):

time: 28.4 us -> 28.4 us (level)
  no operation moved by 1% of the time
where the time goes in v6:
time: 28.4 us; the launch traced here: 28.3 us
  Pallas kernels  15.7 us (55%)
  starting transfers between devices  8.05 us (28%)
  waiting for transfers between devices  3.79 us (13%)
  local copies, waits for them, and re-layouts  0.33 us (1%)
    ppermute x7, starting transfers between devices, exchange(): return lax.ppermute(block, 'seq', [(i, i ^ mask) for i in range(count)])  8.05 us
    pallas_call x1, Pallas kernels, decode(): pl.pallas_call(functools.partial(decode_kernel, float(group)), in_specs=[...  7.85 us
    pallas_call x1, Pallas kernels, prepare(): pl.pallas_call(prepare_kernel, in_specs=[hbm, vmem, vmem, vmem, vmem, hbm...  5.14 us
    ppermute x7, waiting for transfers between devices, exchange(): return lax.ppermute(block, 'seq', [(i, i ^ mask) for i in range(count)])  3.79 us
    pallas_call x1, Pallas kernels, project(): pl.pallas_call(project_give_kernel, in_specs=[hbm, hbm, hbm], out_specs=[...  2.05 us
    pallas_call x1, Pallas kernels, project(): pl.pallas_call(project_own_kernel, in_specs=[vmem, vmem, vmem], out_specs...  0.7 us
  transfers between devices with their start and end apart: 7, of which 4 were waited for; matrix products, arithmetic and copies ran while one was open for 1% of the time, Pallas kernels for 21%

profile of v6, /device:TPU:0, one launch (start us, length us, event | category | flops | bytes accessed | tf_op | source)
XLA Modules:
  0.0 28.3 jit_solution(4420830775561713389)
XLA Ops:
  0.0 0.0 copy-start.8
  0.0 0.0 copy-start.3
  0.0 0.0 copy-start.4
  0.0 0.0 copy-start.5
  0.0 0.0 copy-start.6
  0.0 2.0 %project_give.1 = (bf16[16,48,128]{2,1,0:T(8,128)(2,1)S(1)}, bf16[320,1280]{1,0:T(8,128)(2,1)S(1)}, bf16[144,320]{1,0:T(8,128)(2,1)S(1)}, f32[64,128]{1,0:T(8,128)S(1)}) custom-call(bf16[2,320,1280]{2,1,0:T(8,128)(2,1)} %hid_ref.1, f32[64,5120]{1,0:T(8,128)} %w_ref.2, f32[1,5120]{1,0:T(1,128)} %bitcast.14), custom_call_target="tpu_custom_call" | custom-call | tf_op jit(solution)/shard_map/project_give/pallas_call | solution.py:120
  2.1 0.0 copy-start
  2.1 0.0 copy-start.1
  2.1 0.0 copy-start.2
  2.1 0.5 %collective-permute-start = (bf16[16,48,128]{2,1,0:T(8,128)(2,1)S(1)}, bf16[16,48,128]{2,1,0:T(8,128)(2,1)S(1)}, u32[]{:S(2)}, u32[]{:S(2)}) collective-permute-start(bf16[16,48,128]{2,1,0:T(8,128)(2,1)S(1)} %get-tuple-element.31), channel_id=1, source_target_pairs={{0,1},{1,0},{2,3},{3,2},{4,5},{5,4},{6,7},{7,6},{8,9},{9,8},{10,11... | collective-permute-start | bytes 589832 | tf_op jit(solution)/shard_map/ppermute | solution.py:541
  2.6 0.0 copy-done.3
  2.6 0.0 copy-done.4
  2.6 0.0 copy-done.8
  2.7 0.1 copy.15.dev_ref
  2.8 0.7 %project_own.1 = bf16[16,48,128]{2,1,0:T(8,128)(2,1)S(1)} custom-call(bf16[320,1280]{1,0:T(8,128)(2,1)S(1)} %get-tuple-element.28.hid_ref, bf16[144,320]{1,0:T(8,128)(2,1)S(1)} %get-tuple-element.29.stack_ref, f32[64,128]{1,0:T(8,128)S(1)} %get-tuple-element.30.gsum_ref), custom_call_target="tpu_custom_call" | custom-call | flops 117964800 | bytes 1300000 | tf_op jit(solution)/shard_map/project_own/pallas_call | solution.py:140
  3.5 0.0 copy-done.5
  3.5 0.0 copy-done.6
  3.5 0.2 collective-permute-done
  3.7 0.1 add_convert_fusion
  3.8 4.0 %collective-permute-start.1 = (bf16[6,48,128]{2,1,0:T(8,128)(2,1)S(1)}, bf16[6,48,128]{2,1,0:T(8,128)(2,1)S(1)}, u32[]{:S(2)}, u32[]{:S(2)}) collective-permute-start(bf16[6,48,128]{2,1,0:T(8,128)(2,1)S(1)} %get-tuple-element.51), channel_id=1, source_target_pairs={{0,8},{1,9},{2,10},{3,11},{4,12},{5,13},{6,14},{7,15},{8,0},{9,1},... | collective-permute-start | bytes 221192 | tf_op jit(solution)/shard_map/ppermute | solution.py:541
  7.8 1.3 %collective-permute-start.3 = (bf16[6,48,128]{2,1,0:T(8,128)(2,1)S(1)}, bf16[6,48,128]{2,1,0:T(8,128)(2,1)S(1)}, u32[]{:S(2)}, u32[]{:S(2)}) collective-permute-start(bf16[6,48,128]{2,1,0:T(8,128)(2,1)S(1)} %get-tuple-element.52), channel_id=1, source_target_pairs={{0,12},{1,13},{2,14},{3,15},{4,8},{5,9},{6,10},{7,11},{8,4},{9,5},... | collective-permute-start | bytes 221192 | tf_op jit(solution)/shard_map/ppermute | solution.py:541
  9.2 0.2 collective-permute-start.2
  9.4 0.1 add_convert_fusion.2
  9.5 0.0 copy-done
  9.5 0.0 copy-done.1
  9.5 0.0 copy-done.2
  9.5 0.0 copy-start.7
  9.5 5.1 %prepare.1 = (f32[16,128]{1,0:T(8,128)S(1)}, f32[1,128]{1,0:T(1,128)S(1)}, bf16[2,256,1536]{2,1,0:T(8,128)(2,1)S(1)}, bf16[768,1536]{1,0:T(8,128)(2,1)S(1)}, f32...) custom-call(f32[64,5120]{1,0:T(8,128)} %w_ref.2, f32[1,5120]{1,0:T(1,128)S(1)} %bitcast.15, f32[1,5120]{1,0:T(1,128)S(1)} %bitcast.16, ...), custom_call_target="tpu_custom_call" | custom-call | flops 20000000 | bytes 10000000 | tf_op jit(solution)/shard_map/prepare/pallas_call | solution.py:251
  14.6 0.0 collective-permute-done.1
  14.7 0.0 collective-permute-done.3
  14.7 0.3 collective-permute-done.2
  15.0 0.1 broadcast_in_dim.23.flags_ref
  15.2 0.5 %collective-permute-start.6 = (bf16[3,72,128]{2,1,0:T(8,128)(2,1)S(1)}, bf16[3,72,128]{2,1,0:T(8,128)(2,1)S(1)}, u32[]{:S(2)}, u32[]{:S(2)}) collective-permute-start(bf16[3,72,128]{2,1,0:T(8,128)(2,1)S(1)} %get-tuple-element.54), channel_id=1, source_target_pairs={{0,3},{1,2},{2,1},{3,0},{4,7},{5,6},{6,5},{7,4},{8,11},{9,10},{10,... | collective-permute-start | bytes 165896 | tf_op jit(solution)/shard_map/ppermute | solution.py:541
  15.7 1.2 %collective-permute-start.4 = (bf16[3,72,128]{2,1,0:T(8,128)(2,1)S(1)}, bf16[3,72,128]{2,1,0:T(8,128)(2,1)S(1)}, u32[]{:S(2)}, u32[]{:S(2)}) collective-permute-start(bf16[3,72,128]{2,1,0:T(8,128)(2,1)S(1)} %get-tuple-element.55), channel_id=1, source_target_pairs={{0,2},{1,3},{2,0},{3,1},{4,6},{5,7},{6,4},{7,5},{8,10},{9,11},{10,... | collective-permute-start | bytes 165896 | tf_op jit(solution)/shard_map/ppermute | solution.py:541
  16.9 0.2 collective-permute-start.5
  17.1 0.0 copy-done.7
  17.1 2.1 %collective-permute-done.6.far_ref = bf16[3,72,128]{2,1,0:T(8,128)(2,1)S(1)} collective-permute-done((bf16[3,72,128]{2,1,0:T(8,128)(2,1)S(1)}, bf16[3,72,128]{2,1,0:T(8,128)(2,1)S(1)}, u32[]{:S(2)}, u32[]{:S(2)}) %collective-permute-start.6) | collective-permute-done | bytes 55328 | tf_op jit(solution)/shard_map/ppermute | solution.py:541
  19.2 1.2 %collective-permute-done.4.near_ref = bf16[3,72,128]{2,1,0:T(8,128)(2,1)S(1)} collective-permute-done((bf16[3,72,128]{2,1,0:T(8,128)(2,1)S(1)}, bf16[3,72,128]{2,1,0:T(8,128)(2,1)S(1)}, u32[]{:S(2)}, u32[]{:S(2)}) %collective-permute-start.4) | collective-permute-done | bytes 55328 | tf_op jit(solution)/shard_map/ppermute | solution.py:541
  20.4 0.0 collective-permute-done.5.core_ref
  20.4 7.9 %decode.1 = bf16[2,4,96,320]{3,2,1,0:T(8,128)(2,1)} custom-call(f32[3,384]{1,0:T(4,128)S(1)} %broadcast_in_dim.23.flags_ref, bf16[3,72,128]{2,1,0:T(8,128)(2,1)S(1)} %get-tuple-element.57.own_ref, bf16[3,72,128]{2,1,0:T(8,128)(2,1)S(1)} %collective-permute-done.4.near_ref, bf16[3,72,128]{2,1,0:T(8,128)(2,1)S(1)} %collective-permute-done.5.core_ref, ...), custom_call_target="tpu_custom_call" | custom-call | flops 5000000000 | bytes 8000000 | tf_op jit(solution)/shard_map/decode/pallas_call | solution.py:515
  (13 shorter events, 0.2 us)
Async XLA Ops:
  0.0 2.6 %copy-start.8 = (s32[16]{0:T(128)S(1)}, s32[16]{0:T(128)}, u32[]{:S(2)}) copy-start(s32[16]{0:T(128)} %constant.65.clone) | copy-start | bytes 196
  0.0 2.6 %copy-start.3 = (f32[384]{0:T(512)S(1)}, f32[384]{0:T(512)}, u32[]{:S(2)}) copy-start(f32[384]{0:T(512)} %param.20) | copy-start | bytes 4612
  0.0 2.6 %copy-start.4 = (f32[384]{0:T(512)S(1)}, f32[384]{0:T(512)}, u32[]{:S(2)}) copy-start(f32[384]{0:T(512)} %param.21) | copy-start | bytes 4612
  0.0 3.5 %copy-start.5 = (f32[192]{0:T(256)S(1)}, f32[192]{0:T(256)}, u32[]{:S(2)}) copy-start(f32[192]{0:T(256)} %param.24) | copy-start | bytes 2308
  0.0 3.5 %copy-start.6 = (f32[192]{0:T(256)S(1)}, f32[192]{0:T(256)}, u32[]{:S(2)}) copy-start(f32[192]{0:T(256)} %param.23) | copy-start | bytes 2308
  2.1 7.4 %copy-start = (f32[5120]{0:T(1024)S(1)}, f32[5120]{0:T(1024)}, u32[]{:S(2)}) copy-start(f32[5120]{0:T(1024)} %param.16) | copy-start | bytes 61444
  2.1 7.4 %copy-start.1 = (f32[5120]{0:T(1024)S(1)}, f32[5120]{0:T(1024)}, u32[]{:S(2)}) copy-start(f32[5120]{0:T(1024)} %param.15) | copy-start | bytes 61444
  2.1 7.4 %copy-start.2 = (f32[64]{0:T(128)S(1)}, f32[64]{0:T(128)}, u32[]{:S(2)}) copy-start(f32[64]{0:T(128)} %param.18) | copy-start | bytes 772
  2.1 1.6 %collective-permute-start = (bf16[16,48,128]{2,1,0:T(8,128)(2,1)S(1)}, bf16[16,48,128]{2,1,0:T(8,128)(2,1)S(1)}, u32[]{:S(2)}, u32[]{:S(2)}) collective-permute-start(bf16[16,48,128]{2,1,0:T(8,128)(2,1)S(1)} %get-tuple-element.31), channel_id=1, source_target_pairs={{0,1},{1,0},{2,3},{3,2},{4,5},{5,4},{6,7},{7,6},{8,9},{9,8},{10,11... | collective-permute-start | bytes 589832 | tf_op jit(solution)/shard_map/ppermute | solution.py:541
  3.8 10.9 %collective-permute-start.1 = (bf16[6,48,128]{2,1,0:T(8,128)(2,1)S(1)}, bf16[6,48,128]{2,1,0:T(8,128)(2,1)S(1)}, u32[]{:S(2)}, u32[]{:S(2)}) collective-permute-start(bf16[6,48,128]{2,1,0:T(8,128)(2,1)S(1)} %get-tuple-element.51), channel_id=1, source_target_pairs={{0,8},{1,9},{2,10},{3,11},{4,12},{5,13},{6,14},{7,15},{8,0},{9,1},... | collective-permute-start | bytes 221192 | tf_op jit(solution)/shard_map/ppermute | solution.py:541
  7.8 6.8 %collective-permute-start.3 = (bf16[6,48,128]{2,1,0:T(8,128)(2,1)S(1)}, bf16[6,48,128]{2,1,0:T(8,128)(2,1)S(1)}, u32[]{:S(2)}, u32[]{:S(2)}) collective-permute-start(bf16[6,48,128]{2,1,0:T(8,128)(2,1)S(1)} %get-tuple-element.52), channel_id=1, source_target_pairs={{0,12},{1,13},{2,14},{3,15},{4,8},{5,9},{6,10},{7,11},{8,4},{9,5},... | collective-permute-start | bytes 221192 | tf_op jit(solution)/shard_map/ppermute | solution.py:541
  9.2 5.8 %collective-permute-start.2 = (bf16[6,48,128]{2,1,0:T(8,128)(2,1)S(1)}, bf16[6,48,128]{2,1,0:T(8,128)(2,1)S(1)}, u32[]{:S(2)}, u32[]{:S(2)}) collective-permute-start(bf16[6,48,128]{2,1,0:T(8,128)(2,1)S(1)} %get-tuple-element.53), channel_id=1, source_target_pairs={{0,4},{1,5},{2,6},{3,7},{4,0},{5,1},{6,2},{7,3},{8,12},{9,13},{10,... | collective-permute-start | bytes 221192 | tf_op jit(solution)/shard_map/ppermute | solution.py:541
  9.5 7.6 %copy-start.7 = (f32[96]{0:T(128)S(1)}, f32[96]{0:T(128)}, u32[]{:S(2)}) copy-start(f32[96]{0:T(128)} %param.26) | copy-start | bytes 1156
  15.2 4.1 %collective-permute-start.6 = (bf16[3,72,128]{2,1,0:T(8,128)(2,1)S(1)}, bf16[3,72,128]{2,1,0:T(8,128)(2,1)S(1)}, u32[]{:S(2)}, u32[]{:S(2)}) collective-permute-start(bf16[3,72,128]{2,1,0:T(8,128)(2,1)S(1)} %get-tuple-element.54), channel_id=1, source_target_pairs={{0,3},{1,2},{2,1},{3,0},{4,7},{5,6},{6,5},{7,4},{8,11},{9,10},{10,... | collective-permute-start | bytes 165896 | tf_op jit(solution)/shard_map/ppermute | solution.py:541
  15.7 4.7 %collective-permute-start.4 = (bf16[3,72,128]{2,1,0:T(8,128)(2,1)S(1)}, bf16[3,72,128]{2,1,0:T(8,128)(2,1)S(1)}, u32[]{:S(2)}, u32[]{:S(2)}) collective-permute-start(bf16[3,72,128]{2,1,0:T(8,128)(2,1)S(1)} %get-tuple-element.55), channel_id=1, source_target_pairs={{0,2},{1,3},{2,0},{3,1},{4,6},{5,7},{6,4},{7,5},{8,10},{9,11},{10,... | collective-permute-start | bytes 165896 | tf_op jit(solution)/shard_map/ppermute | solution.py:541
  16.9 3.5 %collective-permute-start.5 = (bf16[3,72,128]{2,1,0:T(8,128)(2,1)S(1)}, bf16[3,72,128]{2,1,0:T(8,128)(2,1)S(1)}, u32[]{:S(2)}, u32[]{:S(2)}) collective-permute-start(bf16[3,72,128]{2,1,0:T(8,128)(2,1)S(1)} %get-tuple-element.56), channel_id=1, source_target_pairs={{0,1},{1,0},{2,3},{3,2},{4,5},{5,4},{6,7},{7,6},{8,9},{9,8},{10,11... | collective-permute-start | bytes 165896 | tf_op jit(solution)/shard_map/ppermute | solution.py:541

commit v7 on v6

--- a/solution.py
+++ b/solution.py
@@ -554,6 +554,49 @@
     return lax.dynamic_slice_in_dim(block, start, size, 0)
 
 
+def last_kernel(count, placing, unit, *refs):
+    block_ref, *received, out0, out1, out2, out3, held = refs
+    size = received[0].shape[0]
+    me = lax.axis_index("seq")
+
+    def window(step, extent):
+        return jnp.clip(me // step * step - 1, 0, count - extent)
+
+    old_size, old_unit = placing
+    new = window(unit, size)
+    old = window(old_unit, old_size) if old_unit else 0
+    nothing = jnp.zeros(held.shape[1:], BF)
+    held[0] = nothing
+    held[size + 1] = nothing
+    for i in range(size):
+        own = block_ref[new - old + i].astype(F32)
+        others = [item[i].astype(F32) for item in received]
+        total = own[:HALF]
+        for item in others:
+            total = total + item[:HALF]
+        held[i + 1] = jnp.concatenate(
+            [total, own[HALF:]] + [item[HALF:] for item in others], axis=0
+        ).astype(BF)
+    for mask, out in ((0, out0), (2, out1), (1, out2), (3, out3)):
+        first = (me ^ mask) - new
+        for j in range(3):
+            out[j] = held[first + j]
+
+
+def last_sums(block, received, count, placing, unit):
+    rows = block.shape[1] + len(received) * (received[0].shape[1] - HALF)
+    vmem = pl.BlockSpec(memory_space=pltpu.VMEM)
+    return pl.pallas_call(
+        functools.partial(last_kernel, count, placing, unit),
+        in_specs=[vmem] * (1 + len(received)),
+        out_specs=[vmem] * 4,
+        out_shape=[jax.ShapeDtypeStruct((3, rows, 128), BF)] * 4,
+        scratch_shapes=[pltpu.VMEM((received[0].shape[0] + 2, rows, 128), BF)],
+        compiler_params=pltpu.CompilerParams(vmem_limit_bytes=16 << 20),
+        name="last_sums",
+    )(block, *received)
+
+
 def steps_of(count):
     bit = count.bit_length() - 3
     steps = [[2 << bit, 1 << bit, 3 << bit]]
@@ -579,7 +622,9 @@
         return jnp.clip(base - 1, 0, count - size)
 
     start = jnp.int32(0)
-    for masks in steps_of(count):
+    steps = steps_of(count)
+    placing = (count, 0)
+    for number, masks in enumerate(steps):
         unit = min(masks)
         size = unit + 2
         base = (me // unit) * unit
@@ -588,14 +633,17 @@
             exchange(cut(block, window(base ^ mask, size) - start, size), mask, count)
             for mask in masks
         ]
-        block = merged(cut(block, new - start, size), received)
-        if len(masks) > 1:
+        if number == len(steps) - 1:
+            block = last_sums(block, received, count, placing, unit)
+        else:
+            block = merged(cut(block, new - start, size), received)
+        if number == 0:
             block, weights = lax.optimization_barrier((block, ready(weights)))
         start = new
-    padded = jnp.pad(block, ((1, 1), (0, 0), (0, 0)))
-    pieces = [cut(padded, me - start, 3)]
-    for mask in (2, 1, 3):
-        pieces.append(exchange(cut(padded, (me ^ mask) - start, 3), mask, count))
+        placing = (size, unit)
+    pieces = [block[0]] + [
+        exchange(piece, mask, count) for piece, mask in zip(block[1:], (2, 1, 3), strict=True)
+    ]
     return pieces, weights
 
 

time: 28.4 us -> 29 us (1.021)
  waiting for transfers between devices: 3.79 us -> 4.08 us
    ppermute x7, starting transfers between devices: 8.05 us -> 8.34 us  [exchange(): return lax.ppermute(block, 'seq', [(i, i ^ mask) for i in range(count)])]
  transfers between devices with their start and end apart: 7 -> 7, of which waited for: 4 -> 4; matrix products, arithmetic and copies ran while one was open for 1% -> 1% of each run, Pallas kernels for 21% -> 20%
where the time goes in v7:
time: 29 us; the launch traced here: 28.8 us
  Pallas kernels  15.8 us (54%)
  starting transfers between devices  8.34 us (29%)
  waiting for transfers between devices  4.08 us (14%)
    ppermute x7, starting transfers between devices, exchange(): return lax.ppermute(block, 'seq', [(i, i ^ mask) for i in range(count)])  8.34 us
    pallas_call x1, Pallas kernels, decode(): pl.pallas_call(functools.partial(decode_kernel, float(group)), in_specs=[...  7.87 us
    pallas_call x1, Pallas kernels, prepare(): pl.pallas_call(prepare_kernel, in_specs=[hbm, vmem, vmem, vmem, vmem, hbm...  5.14 us
    ppermute x7, waiting for transfers between devices, exchange(): return lax.ppermute(block, 'seq', [(i, i ^ mask) for i in range(count)])  4.08 us
    pallas_call x1, Pallas kernels, project(): pl.pallas_call(project_give_kernel, in_specs=[hbm, hbm, hbm], out_specs=[...  2.05 us
    pallas_call x1, Pallas kernels, project(): pl.pallas_call(project_own_kernel, in_specs=[vmem, vmem, vmem], out_specs...  0.7 us
  transfers between devices with their start and end apart: 7, of which 4 were waited for; matrix products, arithmetic and copies ran while one was open for 1% of the time, Pallas kernels for 20%

profile of v7, /device:TPU:0, one launch (start us, length us, event | category | flops | bytes accessed | tf_op | source)
XLA Modules:
  0.0 28.8 jit_solution(16192658141566968716)
XLA Ops:
  0.0 0.0 copy-start.8
  0.0 0.0 copy-start.3
  0.0 0.0 copy-start.4
  0.0 0.0 copy-start.5
  0.0 0.0 copy-start.6
  0.0 2.0 %project_give.1 = (bf16[16,48,128]{2,1,0:T(8,128)(2,1)S(1)}, bf16[320,1280]{1,0:T(8,128)(2,1)S(1)}, bf16[144,320]{1,0:T(8,128)(2,1)S(1)}, f32[64,128]{1,0:T(8,128)S(1)}) custom-call(bf16[2,320,1280]{2,1,0:T(8,128)(2,1)} %hid_ref.1, f32[64,5120]{1,0:T(8,128)} %w_ref.2, f32[1,5120]{1,0:T(1,128)} %bitcast.14), custom_call_target="tpu_custom_call" | custom-call | tf_op jit(solution)/shard_map/project_give/pallas_call | solution.py:120
  2.1 0.0 copy-start
  2.1 0.0 copy-start.1
  2.1 0.0 copy-start.2
  2.1 0.5 %collective-permute-start = (bf16[16,48,128]{2,1,0:T(8,128)(2,1)S(1)}, bf16[16,48,128]{2,1,0:T(8,128)(2,1)S(1)}, u32[]{:S(2)}, u32[]{:S(2)}) collective-permute-start(bf16[16,48,128]{2,1,0:T(8,128)(2,1)S(1)} %get-tuple-element.38), channel_id=1, source_target_pairs={{0,1},{1,0},{2,3},{3,2},{4,5},{5,4},{6,7},{7,6},{8,9},{9,8},{10,11... | collective-permute-start | bytes 589832 | tf_op jit(solution)/shard_map/ppermute | solution.py:541
  2.6 0.0 copy-done.3
  2.6 0.0 copy-done.4
  2.6 0.0 copy-done.8
  2.7 0.1 copy.15.dev_ref
  2.8 0.7 %project_own.1 = bf16[16,48,128]{2,1,0:T(8,128)(2,1)S(1)} custom-call(bf16[320,1280]{1,0:T(8,128)(2,1)S(1)} %get-tuple-element.35.hid_ref, bf16[144,320]{1,0:T(8,128)(2,1)S(1)} %get-tuple-element.36.stack_ref, f32[64,128]{1,0:T(8,128)S(1)} %get-tuple-element.37.gsum_ref), custom_call_target="tpu_custom_call" | custom-call | flops 117964800 | bytes 1300000 | tf_op jit(solution)/shard_map/project_own/pallas_call | solution.py:140
  3.5 0.0 copy-done.5
  3.5 0.0 copy-done.6
  3.5 0.2 collective-permute-done
  3.7 0.1 add_convert_fusion.refs_0_
  3.8 5.0 %collective-permute-start.3 = (bf16[6,48,128]{2,1,0:T(8,128)(2,1)S(1)}, bf16[6,48,128]{2,1,0:T(8,128)(2,1)S(1)}, u32[]{:S(2)}, u32[]{:S(2)}) collective-permute-start(bf16[6,48,128]{2,1,0:T(8,128)(2,1)S(1)} %get-tuple-element.65), channel_id=1, source_target_pairs={{0,12},{1,13},{2,14},{3,15},{4,8},{5,9},{6,10},{7,11},{8,4},{9,5},... | collective-permute-start | bytes 221192 | tf_op jit(solution)/shard_map/ppermute | solution.py:541
  8.8 0.0 collective-permute-start.2
  8.8 0.6 %collective-permute-start.1 = (bf16[6,48,128]{2,1,0:T(8,128)(2,1)S(1)}, bf16[6,48,128]{2,1,0:T(8,128)(2,1)S(1)}, u32[]{:S(2)}, u32[]{:S(2)}) collective-permute-start(bf16[6,48,128]{2,1,0:T(8,128)(2,1)S(1)} %get-tuple-element.67), channel_id=1, source_target_pairs={{0,8},{1,9},{2,10},{3,11},{4,12},{5,13},{6,14},{7,15},{8,0},{9,1},... | collective-permute-start | bytes 221192 | tf_op jit(solution)/shard_map/ppermute | solution.py:541
  9.5 0.1 add_convert_fusion.1
  9.5 0.0 copy-done
  9.5 0.0 copy-done.1
  9.6 0.0 copy-done.2
  9.6 0.0 copy-start.7
  9.6 5.1 %prepare.1 = (f32[16,128]{1,0:T(8,128)S(1)}, f32[1,128]{1,0:T(1,128)S(1)}, bf16[2,256,1536]{2,1,0:T(8,128)(2,1)S(1)}, bf16[768,1536]{1,0:T(8,128)(2,1)S(1)}, f32...) custom-call(f32[64,5120]{1,0:T(8,128)} %w_ref.2, f32[1,5120]{1,0:T(1,128)S(1)} %bitcast.15, f32[1,5120]{1,0:T(1,128)S(1)} %bitcast.16, ...), custom_call_target="tpu_custom_call" | custom-call | flops 20000000 | bytes 10000000 | tf_op jit(solution)/shard_map/prepare/pallas_call | solution.py:251
  14.7 0.0 collective-permute-done.3.refs_3_
  14.7 0.0 collective-permute-done.2.refs_2_
  14.7 0.9 %collective-permute-done.1.refs_1_ = bf16[6,48,128]{2,1,0:T(8,128)(2,1)S(1)} collective-permute-done((bf16[6,48,128]{2,1,0:T(8,128)(2,1)S(1)}, bf16[6,48,128]{2,1,0:T(8,128)(2,1)S(1)}, u32[]{:S(2)}, u32[]{:S(2)}) %collective-permute-start.1) | collective-permute-done | bytes 73760 | tf_op jit(solution)/shard_map/ppermute | solution.py:541
  15.7 0.1 last_sums.1
  15.7 0.1 broadcast_in_dim.23.flags_ref
  15.8 1.5 %collective-permute-start.4 = (bf16[3,72,128]{2,1,0:T(8,128)(2,1)S(1)}, bf16[3,72,128]{2,1,0:T(8,128)(2,1)S(1)}, u32[]{:S(2)}, u32[]{:S(2)}) collective-permute-start(bf16[3,72,128]{2,1,0:T(8,128)(2,1)S(1)} %get-tuple-element.56), channel_id=1, source_target_pairs={{0,2},{1,3},{2,0},{3,1},{4,6},{5,7},{6,4},{7,5},{8,10},{9,11},{10,... | collective-permute-start | bytes 165896 | tf_op jit(solution)/shard_map/ppermute | solution.py:541
  17.3 0.0 collective-permute-start.5
  17.3 0.6 %collective-permute-start.6 = (bf16[3,72,128]{2,1,0:T(8,128)(2,1)S(1)}, bf16[3,72,128]{2,1,0:T(8,128)(2,1)S(1)}, u32[]{:S(2)}, u32[]{:S(2)}) collective-permute-start(bf16[3,72,128]{2,1,0:T(8,128)(2,1)S(1)} %get-tuple-element.58), channel_id=1, source_target_pairs={{0,3},{1,2},{2,1},{3,0},{4,7},{5,6},{6,5},{7,4},{8,11},{9,10},{10,... | collective-permute-start | bytes 165896 | tf_op jit(solution)/shard_map/ppermute | solution.py:541
  18.0 0.0 copy-done.7
  18.0 2.0 %collective-permute-done.4.near_ref = bf16[3,72,128]{2,1,0:T(8,128)(2,1)S(1)} collective-permute-done((bf16[3,72,128]{2,1,0:T(8,128)(2,1)S(1)}, bf16[3,72,128]{2,1,0:T(8,128)(2,1)S(1)}, u32[]{:S(2)}, u32[]{:S(2)}) %collective-permute-start.4) | collective-permute-done | bytes 55328 | tf_op jit(solution)/shard_map/ppermute | solution.py:541
  20.0 0.0 collective-permute-done.5.core_ref
  20.0 0.9 %collective-permute-done.6.far_ref = bf16[3,72,128]{2,1,0:T(8,128)(2,1)S(1)} collective-permute-done((bf16[3,72,128]{2,1,0:T(8,128)(2,1)S(1)}, bf16[3,72,128]{2,1,0:T(8,128)(2,1)S(1)}, u32[]{:S(2)}, u32[]{:S(2)}) %collective-permute-start.6) | collective-permute-done | bytes 55328 | tf_op jit(solution)/shard_map/ppermute | solution.py:541
  20.9 7.9 %decode.1 = bf16[2,4,96,320]{3,2,1,0:T(8,128)(2,1)} custom-call(f32[3,384]{1,0:T(4,128)S(1)} %broadcast_in_dim.23.flags_ref, bf16[3,72,128]{2,1,0:T(8,128)(2,1)S(1)} %get-tuple-element.55.own_ref, bf16[3,72,128]{2,1,0:T(8,128)(2,1)S(1)} %collective-permute-done.4.near_ref, bf16[3,72,128]{2,1,0:T(8,128)(2,1)S(1)} %collective-permute-done.5.core_ref, ...), custom_call_target="tpu_custom_call" | custom-call | flops 5000000000 | bytes 8000000 | tf_op jit(solution)/shard_map/decode/pallas_call | solution.py:515
  (7 shorter events, 0.1 us)
Async XLA Ops:
  0.0 2.6 %copy-start.8 = (s32[16]{0:T(128)S(1)}, s32[16]{0:T(128)}, u32[]{:S(2)}) copy-start(s32[16]{0:T(128)} %constant.60.clone) | copy-start | bytes 196
  0.0 2.6 %copy-start.3 = (f32[384]{0:T(512)S(1)}, f32[384]{0:T(512)}, u32[]{:S(2)}) copy-start(f32[384]{0:T(512)} %param.20) | copy-start | bytes 4612
  0.0 2.6 %copy-start.4 = (f32[384]{0:T(512)S(1)}, f32[384]{0:T(512)}, u32[]{:S(2)}) copy-start(f32[384]{0:T(512)} %param.21) | copy-start | bytes 4612
  0.0 3.5 %copy-start.5 = (f32[192]{0:T(256)S(1)}, f32[192]{0:T(256)}, u32[]{:S(2)}) copy-start(f32[192]{0:T(256)} %param.24) | copy-start | bytes 2308
  0.0 3.5 %copy-start.6 = (f32[192]{0:T(256)S(1)}, f32[192]{0:T(256)}, u32[]{:S(2)}) copy-start(f32[192]{0:T(256)} %param.23) | copy-start | bytes 2308
  2.1 7.5 %copy-start = (f32[5120]{0:T(1024)S(1)}, f32[5120]{0:T(1024)}, u32[]{:S(2)}) copy-start(f32[5120]{0:T(1024)} %param.16) | copy-start | bytes 61444
  2.1 7.5 %copy-start.1 = (f32[5120]{0:T(1024)S(1)}, f32[5120]{0:T(1024)}, u32[]{:S(2)}) copy-start(f32[5120]{0:T(1024)} %param.15) | copy-start | bytes 61444
  2.1 7.5 %copy-start.2 = (f32[64]{0:T(128)S(1)}, f32[64]{0:T(128)}, u32[]{:S(2)}) copy-start(f32[64]{0:T(128)} %param.18) | copy-start | bytes 772
  2.1 1.6 %collective-permute-start = (bf16[16,48,128]{2,1,0:T(8,128)(2,1)S(1)}, bf16[16,48,128]{2,1,0:T(8,128)(2,1)S(1)}, u32[]{:S(2)}, u32[]{:S(2)}) collective-permute-start(bf16[16,48,128]{2,1,0:T(8,128)(2,1)S(1)} %get-tuple-element.38), channel_id=1, source_target_pairs={{0,1},{1,0},{2,3},{3,2},{4,5},{5,4},{6,7},{7,6},{8,9},{9,8},{10,11... | collective-permute-start | bytes 589832 | tf_op jit(solution)/shard_map/ppermute | solution.py:541
  3.8 10.9 %collective-permute-start.3 = (bf16[6,48,128]{2,1,0:T(8,128)(2,1)S(1)}, bf16[6,48,128]{2,1,0:T(8,128)(2,1)S(1)}, u32[]{:S(2)}, u32[]{:S(2)}) collective-permute-start(bf16[6,48,128]{2,1,0:T(8,128)(2,1)S(1)} %get-tuple-element.65), channel_id=1, source_target_pairs={{0,12},{1,13},{2,14},{3,15},{4,8},{5,9},{6,10},{7,11},{8,4},{9,5},... | collective-permute-start | bytes 221192 | tf_op jit(solution)/shard_map/ppermute | solution.py:541
  8.8 5.9 %collective-permute-start.2 = (bf16[6,48,128]{2,1,0:T(8,128)(2,1)S(1)}, bf16[6,48,128]{2,1,0:T(8,128)(2,1)S(1)}, u32[]{:S(2)}, u32[]{:S(2)}) collective-permute-start(bf16[6,48,128]{2,1,0:T(8,128)(2,1)S(1)} %get-tuple-element.66), channel_id=1, source_target_pairs={{0,4},{1,5},{2,6},{3,7},{4,0},{5,1},{6,2},{7,3},{8,12},{9,13},{10,... | collective-permute-start | bytes 221192 | tf_op jit(solution)/shard_map/ppermute | solution.py:541
  8.8 6.8 %collective-permute-start.1 = (bf16[6,48,128]{2,1,0:T(8,128)(2,1)S(1)}, bf16[6,48,128]{2,1,0:T(8,128)(2,1)S(1)}, u32[]{:S(2)}, u32[]{:S(2)}) collective-permute-start(bf16[6,48,128]{2,1,0:T(8,128)(2,1)S(1)} %get-tuple-element.67), channel_id=1, source_target_pairs={{0,8},{1,9},{2,10},{3,11},{4,12},{5,13},{6,14},{7,15},{8,0},{9,1},... | collective-permute-start | bytes 221192 | tf_op jit(solution)/shard_map/ppermute | solution.py:541
  9.6 8.4 %copy-start.7 = (f32[96]{0:T(128)S(1)}, f32[96]{0:T(128)}, u32[]{:S(2)}) copy-start(f32[96]{0:T(128)} %param.26) | copy-start | bytes 1156
  15.8 4.2 %collective-permute-start.4 = (bf16[3,72,128]{2,1,0:T(8,128)(2,1)S(1)}, bf16[3,72,128]{2,1,0:T(8,128)(2,1)S(1)}, u32[]{:S(2)}, u32[]{:S(2)}) collective-permute-start(bf16[3,72,128]{2,1,0:T(8,128)(2,1)S(1)} %get-tuple-element.56), channel_id=1, source_target_pairs={{0,2},{1,3},{2,0},{3,1},{4,6},{5,7},{6,4},{7,5},{8,10},{9,11},{10,... | collective-permute-start | bytes 165896 | tf_op jit(solution)/shard_map/ppermute | solution.py:541
  17.3 2.6 %collective-permute-start.5 = (bf16[3,72,128]{2,1,0:T(8,128)(2,1)S(1)}, bf16[3,72,128]{2,1,0:T(8,128)(2,1)S(1)}, u32[]{:S(2)}, u32[]{:S(2)}) collective-permute-start(bf16[3,72,128]{2,1,0:T(8,128)(2,1)S(1)} %get-tuple-element.57), channel_id=1, source_target_pairs={{0,1},{1,0},{2,3},{3,2},{4,5},{5,4},{6,7},{7,6},{8,9},{9,8},{10,11... | collective-permute-start | bytes 165896 | tf_op jit(solution)/shard_map/ppermute | solution.py:541
  17.3 3.6 %collective-permute-start.6 = (bf16[3,72,128]{2,1,0:T(8,128)(2,1)S(1)}, bf16[3,72,128]{2,1,0:T(8,128)(2,1)S(1)}, u32[]{:S(2)}, u32[]{:S(2)}) collective-permute-start(bf16[3,72,128]{2,1,0:T(8,128)(2,1)S(1)} %get-tuple-element.58), channel_id=1, source_target_pairs={{0,3},{1,2},{2,1},{3,0},{4,7},{5,6},{6,5},{7,4},{8,11},{9,10},{10,... | collective-permute-start | bytes 165896 | tf_op jit(solution)/shard_map/ppermute | solution.py:541
